TPU v7x, 32 devices: a whole 2x2x4 slice. The times are simulated.
32 devices in a mesh: dp: 8 (over z, y), tensor: 4 (over x, core).
Axes of the slice: x: 2, y: 2, z: 4, core: 2. Of those that a mesh axis runs over, the one named last changes fastest.
Arguments:
- inputs: bfloat16 [8192, 2048], P(('dp', 'tensor')), may hold values from -6 to 6
- segments: int32 [8, 1024], P('dp', 'tensor'), may hold values from 0 to 2, as said below
- cotangent: bfloat16 [8192, 2048], P(('dp', 'tensor')), may hold values from -6 to 6
- qkv_weight: float32 [3, 2048, 2048], P(None, 'dp', 'tensor'), may hold values from -0.125 to 0.125
- qkv_first: float32 [3, 2048, 2048], P(None, 'dp', 'tensor')
- qkv_second: float32 [3, 2048, 2048], P(None, 'dp', 'tensor'), may hold values from 434.176 to 1720.32
- dense_weight: float32 [2048, 2048], P('tensor', 'dp'), may hold values from -0.75 to 0.75
- dense_first: float32 [2048, 2048], P('tensor', 'dp')
- dense_second: float32 [2048, 2048], P('tensor', 'dp'), may hold values from 13.1072 to 52.4288
- expand_weight: float32 [2048, 8192], P('dp', 'tensor'), may hold values from -0.125 to 0.125
- expand_first: float32 [2048, 8192], P('dp', 'tensor')
- expand_second: float32 [2048, 8192], P('dp', 'tensor'), may hold values from 155.648 to 622.592
- shrink_weight: float32 [8192, 2048], P('tensor', 'dp'), may hold values from -0.0625 to 0.0625
- shrink_first: float32 [8192, 2048], P('tensor', 'dp')
- shrink_second: float32 [8192, 2048], P('tensor', 'dp'), may hold values from 172.032 to 688.128
- small_params: float32 [11, 2048], P(None, 'dp')
- small_first: float32 [11, 2048], P(None, 'dp')
- small_second: float32 [11, 2048], P(None, 'dp'), may hold values from 868.352 to 3440.64
Outputs:
- output: bfloat16 [8192, 2048], P(('dp', 'tensor'))
- input_grad: float32 [8192, 2048], P(('dp', 'tensor'))
- qkv_new: float32 [3, 2048, 2048], P(None, 'dp', 'tensor')
- qkv_first_new: float32 [3, 2048, 2048], P(None, 'dp', 'tensor')
- qkv_second_new: float32 [3, 2048, 2048], P(None, 'dp', 'tensor')
- dense_new: float32 [2048, 2048], P('tensor', 'dp')
- dense_first_new: float32 [2048, 2048], P('tensor', 'dp')
- dense_second_new: float32 [2048, 2048], P('tensor', 'dp')
- expand_new: float32 [2048, 8192], P('dp', 'tensor')
- expand_first_new: float32 [2048, 8192], P('dp', 'tensor')
- expand_second_new: float32 [2048, 8192], P('dp', 'tensor')
- shrink_new: float32 [8192, 2048], P('tensor', 'dp')
- shrink_first_new: float32 [8192, 2048], P('tensor', 'dp')
- shrink_second_new: float32 [8192, 2048], P('tensor', 'dp')
- small_new: float32 [11, 2048], P(None, 'dp')
- small_first_new: float32 [11, 2048], P(None, 'dp')
- small_second_new: float32 [11, 2048], P(None, 'dp')
Inputs may be any that keep to these rules, and one draw needn't show every extreme that they name: `segments`: each row holds three documents numbered 0, 1, 2 in order, each of 64 tokens or more; document 1 holds token 170 and token 768 of the row.
All inputs are finite; a program needn't handle non-finite values.
Results may differ from a plain program's by a relative error of at most 0.012.
The roundings to bfloat16 on the way count: a program that leaves them out, or rounds other values in their place, can miss the bound.
Values may be sent and summed in bfloat16 or wider, within the bound.
A program may use at most 192 MiB of HBM per device.

v0:
```python
import jax
import jax.numpy as jnp
from jax import lax
from jax.sharding import PartitionSpec as P

D = 2048
HD = 64
ROT = 32
FF = 8192
STEP = 10


norm_eps = 1e-05
beta_first = 0.9
beta_second = 0.95
adam_eps = 1e-08
weight_decay = 0.1
matrix_rate = 0.05
vector_rate = 1.0
masked_score = -1e30


def doc_positions(doc_ids):
    places = jnp.arange(doc_ids.shape[0], dtype=jnp.int32)
    before = jnp.concatenate([doc_ids[:1] - 1, doc_ids[:-1]])
    starts = jnp.where(doc_ids != before, places, jnp.zeros_like(places))
    first = lax.cummax(starts, axis=0)
    return (places - first).astype(jnp.float32)


def doc_angles(doc_ids):
    half = ROT // 2
    freqs = 10000.0 ** (-jnp.arange(half, dtype=jnp.float32) / half)
    return doc_positions(doc_ids)[:, None] * freqs[None, :]


def rotate(values, angle):
    half = ROT // 2
    cosine = jnp.cos(angle)[:, None, :]
    sine = jnp.sin(angle)[:, None, :]
    first = values[..., :half]
    second = values[..., half:ROT]
    return jnp.concatenate(
        [first * cosine - second * sine, second * cosine + first * sine, values[..., ROT:]], axis=-1
    )


def adam_update(weight, first, second, grad, rate, decay):
    first_new = beta_first * first + (1.0 - beta_first) * grad
    second_new = beta_second * second + (1.0 - beta_second) * grad * grad
    first_hat = first_new / (1.0 - beta_first**STEP)
    second_hat = second_new / (1.0 - beta_second**STEP)
    weight_new = weight - rate * (first_hat / (jnp.sqrt(second_hat) + adam_eps) + decay * weight)
    return (weight_new, first_new, second_new)


def gelu_value(pre_values):
    return jax.nn.gelu(pre_values, approximate=True)


def per_device(
    inputs,
    segments,
    cotangent,
    qkv_weight,
    qkv_first,
    qkv_second,
    dense_weight,
    dense_first,
    dense_second,
    expand_weight,
    expand_first,
    expand_second,
    shrink_weight,
    shrink_first,
    shrink_second,
    small_params,
    small_first,
    small_second,
):
    tensor_count = lax.axis_size("tensor")
    tensor_rank = lax.axis_index("tensor")
    own_tokens = inputs.shape[0]
    length = own_tokens * tensor_count
    head_width = qkv_weight.shape[2]
    local_heads = head_width // HD
    hidden_width = expand_weight.shape[1]
    block_rows = min(512, length)
    block_count = length // block_rows
    scale = HD ** (-0.5)
    low_type = jnp.bfloat16
    wide_type = jnp.float32
    qkv_low = qkv_weight.astype(low_type)
    dense_low = dense_weight.astype(low_type)
    expand_low = expand_weight.astype(low_type)
    shrink_low = shrink_weight.astype(low_type)
    small_low = small_params.astype(low_type)
    qkv_full, dense_full, expand_full, shrink_full, params_low = (
        lax.all_gather(qkv_low, "dp", axis=1, tiled=True),
        lax.all_gather(dense_low, "dp", axis=1, tiled=True),
        lax.all_gather(expand_low, "dp", axis=0, tiled=True),
        lax.all_gather(shrink_low, "dp", axis=1, tiled=True),
        lax.all_gather(small_low, "dp", axis=1, tiled=True),
    )
    params = params_low.astype(wide_type)
    rows_own = inputs.astype(wide_type)
    centered = rows_own - jnp.mean(rows_own, axis=-1, keepdims=True)
    inv_std = lax.rsqrt(jnp.mean(centered * centered, axis=-1, keepdims=True) + norm_eps)
    unit_rows = centered * inv_std
    normed_own = (unit_rows * params[0] + params[1]).astype(low_type)
    normed = lax.all_gather(normed_own, "tensor", axis=0, tiled=True)
    doc_ids = lax.all_gather(segments, "tensor", axis=1, tiled=True)[0]
    angle = doc_angles(doc_ids)
    qkv_bias = lax.dynamic_slice_in_dim(params[2:5], tensor_rank * head_width, head_width, 1)
    expand_bias = lax.dynamic_slice_in_dim(
        params[7:].reshape(FF), tensor_rank * hidden_width, hidden_width, 0
    )
    projected = (
        jnp.einsum("sd,jde->jse", normed, qkv_full, preferred_element_type=wide_type)
        + qkv_bias[:, None, :]
    )
    queries = rotate(projected[0].reshape(length, local_heads, HD), angle).astype(low_type)
    keys = rotate(projected[1].reshape(length, local_heads, HD), angle).astype(low_type)
    values = projected[2].reshape(length, local_heads, HD).astype(low_type)
    key_places = jnp.arange(length, dtype=jnp.int32)

    def block_scores(start):
        query_block = lax.dynamic_slice_in_dim(queries, start, block_rows, 0)
        query_docs = lax.dynamic_slice_in_dim(doc_ids, start, block_rows, 0)
        query_places = start + jnp.arange(block_rows, dtype=jnp.int32)
        allowed = (query_docs[:, None] == doc_ids[None, :]) & (
            key_places[None, :] <= query_places[:, None]
        )
        scores = (
            jnp.einsum("qhd,khd->hqk", query_block, keys, preferred_element_type=wide_type) * scale
        )
        return (query_block, jnp.where(allowed[None], scores, masked_score), allowed)

    def forward_block(start):
        query_block, scores, allowed = block_scores(start)
        peak = jnp.max(scores, axis=-1, keepdims=True)
        expo = jnp.exp(scores - peak)
        total = jnp.sum(expo, axis=-1, keepdims=True)
        weights = (expo / total).astype(low_type)
        result = jnp.einsum("hqk,khd->qhd", weights, values, preferred_element_type=wide_type)
        return (result, peak[..., 0] + jnp.log(total[..., 0]))

    starts = jnp.arange(block_count, dtype=jnp.int32) * block_rows
    attended_blocks, log_totals = lax.map(forward_block, starts)
    attended = attended_blocks.reshape(length, head_width).astype(low_type)
    hidden_pre = jnp.dot(normed, expand_full, preferred_element_type=wide_type) + expand_bias
    hidden_act = gelu_value(hidden_pre).astype(low_type)
    branch = lax.psum_scatter(
        jnp.dot(attended, dense_full, preferred_element_type=wide_type)
        + jnp.dot(hidden_act, shrink_full, preferred_element_type=wide_type),
        "tensor",
        scatter_dimension=0,
        tiled=True,
    )
    output = (rows_own + branch + params[5] + params[6]).astype(low_type)
    qkv_back, dense_back, expand_back, shrink_back = (
        lax.all_gather(qkv_low, "dp", axis=1, tiled=True),
        lax.all_gather(dense_low, "dp", axis=1, tiled=True),
        lax.all_gather(expand_low, "dp", axis=0, tiled=True),
        lax.all_gather(shrink_low, "dp", axis=1, tiled=True),
    )
    back_rows = lax.all_gather(cotangent, "tensor", axis=0, tiled=True)
    back_own = cotangent.astype(wide_type)
    bias_back = jnp.sum(back_own, axis=0)
    attended_back = (
        jnp.einsum("sd,kd->sk", back_rows, dense_back, preferred_element_type=wide_type)
        .astype(low_type)
        .reshape(length, local_heads, HD)
    )
    act_back = jnp.einsum("sd,fd->sf", back_rows, shrink_back, preferred_element_type=wide_type)
    gelu_pull = jax.vjp(gelu_value, hidden_pre)[1]
    pre_back = gelu_pull(act_back)[0].astype(low_type)

    def backward_block(carry, start):
        key_sum, value_sum = carry
        query_block, scores, allowed = block_scores(start)
        lse_block = lax.dynamic_index_in_dim(log_totals, start // block_rows, 0, keepdims=False)
        probs = jnp.where(allowed[None], jnp.exp(scores - lse_block[..., None]), 0.0)
        back_block = lax.dynamic_slice_in_dim(attended_back, start, block_rows, 0)
        value_sum = value_sum + jnp.einsum(
            "hqk,qhd->khd", probs.astype(low_type), back_block, preferred_element_type=wide_type
        )
        prob_back = jnp.einsum("qhd,khd->hqk", back_block, values, preferred_element_type=wide_type)
        inner = jnp.sum(probs * prob_back, axis=-1, keepdims=True)
        score_back = (probs * (prob_back - inner)).astype(low_type)
        query_back = scale * jnp.einsum(
            "hqk,khd->qhd", score_back, keys, preferred_element_type=wide_type
        )
        key_sum = key_sum + scale * jnp.einsum(
            "hqk,qhd->khd", score_back, query_block, preferred_element_type=wide_type
        )
        return ((key_sum, value_sum), query_back)

    zero_heads = jnp.zeros((length, local_heads, HD), wide_type)
    (key_back, value_back), query_blocks = lax.scan(
        backward_block, (zero_heads, zero_heads), starts
    )
    query_back = query_blocks.reshape(length, local_heads, HD)
    proj_back = jnp.stack(
        [
            rotate(query_back, -angle).reshape(length, head_width),
            rotate(key_back, -angle).reshape(length, head_width),
            value_back.reshape(length, head_width),
        ]
    ).astype(low_type)
    qkv_bias_grad = jnp.sum(proj_back, axis=1, dtype=wide_type)
    expand_bias_grad = jnp.sum(pre_back, axis=0, dtype=wide_type)
    normed_back = lax.psum_scatter(
        jnp.einsum("jse,jde->sd", proj_back, qkv_back, preferred_element_type=wide_type)
        + jnp.einsum("sf,df->sd", pre_back, expand_back, preferred_element_type=wide_type),
        "tensor",
        scatter_dimension=0,
        tiled=True,
    )
    unit_back = normed_back * params[0]
    input_grad = back_own + inv_std * (
        unit_back
        - jnp.mean(unit_back, axis=-1, keepdims=True)
        - unit_rows * jnp.mean(unit_back * unit_rows, axis=-1, keepdims=True)
    )
    gain_grad = jnp.sum(normed_back * unit_rows, axis=0)
    shift_grad = jnp.sum(normed_back, axis=0)
    qkv_rows = lax.dynamic_update_slice_in_dim(
        jnp.zeros((3, D), wide_type), qkv_bias_grad, tensor_rank * head_width, 1
    )
    expand_rows = lax.dynamic_update_slice_in_dim(
        jnp.zeros((FF,), wide_type), expand_bias_grad, tensor_rank * hidden_width, 0
    ).reshape(FF // D, D)
    params_grad = jnp.concatenate(
        [
            gain_grad[None],
            shift_grad[None],
            qkv_rows,
            bias_back[None],
            bias_back[None],
            expand_rows,
        ],
        axis=0,
    )
    qkv_grad = jnp.einsum("sd,jse->jde", normed, proj_back, preferred_element_type=wide_type)
    expand_grad = jnp.einsum("sd,sf->df", normed, pre_back, preferred_element_type=wide_type)
    dense_grad = jnp.einsum("sk,sd->kd", attended, back_rows, preferred_element_type=wide_type)
    shrink_grad = jnp.einsum("sf,sd->fd", hidden_act, back_rows, preferred_element_type=wide_type)
    qkv_sum, dense_sum, expand_sum, shrink_sum, params_part = (
        lax.psum_scatter(qkv_grad, "dp", scatter_dimension=1, tiled=True),
        lax.psum_scatter(dense_grad, "dp", scatter_dimension=1, tiled=True),
        lax.psum_scatter(expand_grad, "dp", scatter_dimension=0, tiled=True),
        lax.psum_scatter(shrink_grad, "dp", scatter_dimension=1, tiled=True),
        lax.psum_scatter(params_grad, "dp", scatter_dimension=1, tiled=True),
    )
    params_sum = lax.psum(params_part, "tensor")
    qkv_new = adam_update(qkv_weight, qkv_first, qkv_second, qkv_sum, matrix_rate, weight_decay)
    dense_new = adam_update(
        dense_weight, dense_first, dense_second, dense_sum, matrix_rate, weight_decay
    )
    expand_new = adam_update(
        expand_weight, expand_first, expand_second, expand_sum, matrix_rate, weight_decay
    )
    shrink_new = adam_update(
        shrink_weight, shrink_first, shrink_second, shrink_sum, matrix_rate, weight_decay
    )
    small_new = adam_update(small_params, small_first, small_second, params_sum, vector_rate, 0.0)
    return (
        output,
        input_grad,
        qkv_new[0],
        qkv_new[1],
        qkv_new[2],
        dense_new[0],
        dense_new[1],
        dense_new[2],
        expand_new[0],
        expand_new[1],
        expand_new[2],
        shrink_new[0],
        shrink_new[1],
        shrink_new[2],
        small_new[0],
        small_new[1],
        small_new[2],
    )


def solution(mesh):
    in_specs = (
        P(("dp", "tensor"), None),
        P("dp", "tensor"),
        P(("dp", "tensor"), None),
        P(None, "dp", "tensor"),
        P(None, "dp", "tensor"),
        P(None, "dp", "tensor"),
        P("tensor", "dp"),
        P("tensor", "dp"),
        P("tensor", "dp"),
        P("dp", "tensor"),
        P("dp", "tensor"),
        P("dp", "tensor"),
        P("tensor", "dp"),
        P("tensor", "dp"),
        P("tensor", "dp"),
        P(None, "dp"),
        P(None, "dp"),
        P(None, "dp"),
    )
    out_specs = (
        P(("dp", "tensor"), None),
        P(("dp", "tensor"), None),
        P(None, "dp", "tensor"),
        P(None, "dp", "tensor"),
        P(None, "dp", "tensor"),
        P("tensor", "dp"),
        P("tensor", "dp"),
        P("tensor", "dp"),
        P("dp", "tensor"),
        P("dp", "tensor"),
        P("dp", "tensor"),
        P("tensor", "dp"),
        P("tensor", "dp"),
        P("tensor", "dp"),
        P(None, "dp"),
        P(None, "dp"),
        P(None, "dp"),
    )
    return jax.shard_map(
        per_device, mesh=mesh, in_specs=in_specs, out_specs=out_specs, check_vma=False
    )
```

profile of v0, /device:TPU:0, one launch (start us, length us, event | category | flops | bytes accessed | tf_op | source)
XLA Modules:
  0.0 1721.1 jit_solution(1825285594585759738)
XLA Ops:
  8.1 32.3 %all_gather.29 = bf16[11,2048]{1,0:T(8,128)(2,1)S(1)} all-gather(bf16[11,256]{1,0:T(8,128)(2,1)S(1)} %convert_element_type.81), channel_id=1, replica_groups=mesh['dp'=8,'tensor'=4] {'dp'}, dimensions={1}, use_global_device_ids=true | all-gather | bytes 50688 | tf_op jit(solution)/shard_map/all_gather | solution.py:103
  60.9 21.9 %all-gather.7.cloned.1.call-done = bf16[1024,2048]{1,0:T(8,128)(2,1)} async-done(((bf16[256,2048]{1,0:T(8,128)(2,1)}), bf16[1024,2048]{1,0:T(8,128)(2,1)}) %all-gather.7.cloned.1.call-update) | async-done | bytes 4194320 | tf_op jit(solution)/shard_map/all_gather | solution.py:111
  82.9 102.6 %all-gather.9.cloned.1.call-done = bf16[3,2048,512]{1,2,0:T(8,128)(2,1)} async-done(((bf16[3,256,512]{1,2,0:T(8,128)(2,1)}), bf16[3,2048,512]{1,2,0:T(8,128)(2,1)}) %all-gather.9.cloned.1.call-update) | async-done | bytes 6291472 | tf_op jit(solution)/shard_map/all_gather | solution.py:99
  197.0 35.5 %while.30 = (s32[]{:T(128)}, bf16[2,512,8,64]{1,3,2,0:T(8,128)(2,1)}, f32[2,8,512]{2,1,0:T(8,128)S(1)}, s32[2]{0:T(128)S(1)}, s32[1024]{0:T(1024)S(1)}, /*index=...) while((s32[]{:T(128)}, ...), condition=%wide.region_7.8_spmd.clone, body=%wide.region_4.7_spmd.clone.sunk | while | flops 1125642752 | bytes 56244916 | solution.py:149
  244.6 102.9 %all-gather.13.cloned.1.call-done = bf16[2048,2048]{1,0:T(8,128)(2,1)} async-done(((bf16[256,2048]{1,0:T(8,128)(2,1)}), bf16[2048,2048]{1,0:T(8,128)(2,1)}) %all-gather.13.cloned.1.call-update) | async-done | bytes 8388624 | tf_op jit(solution)/shard_map/all_gather | solution.py:101
  347.6 12.6 fusion.77
  363.4 12.8 fusion.67
  376.3 61.5 %reduce-scatter.14.cloned.1.call-done = f32[512,256]{1,0:T(8,128)} async-done(((f32[512,2048]{1,0:T(8,128)}), f32[512,256]{1,0:T(8,128)}) %reduce-scatter.14.cloned.1.call-update) | async-done | bytes 524304 | tf_op jit(solution)/shard_map/reduce_scatter | solution.py:251
  440.4 284.0 %reduce-scatter.18.cloned.1.call-done = f32[2048,256]{1,0:T(8,128)} async-done(((f32[2048,2048]{1,0:T(8,128)}), f32[2048,256]{1,0:T(8,128)}) %reduce-scatter.18.cloned.1.call-update) | async-done | bytes 2097168 | tf_op jit(solution)/shard_map/reduce_scatter | solution.py:253
  732.6 44.5 %all-gather.11.cloned.1.call-done = bf16[512,2048]{1,0:T(8,128)(2,1)} async-done(((bf16[512,256]{1,0:T(8,128)(2,1)}), bf16[512,2048]{1,0:T(8,128)(2,1)}) %all-gather.11.cloned.1.call-update) | async-done | bytes 2097168 | tf_op jit(solution)/shard_map/all_gather | solution.py:100
  783.4 161.6 %while.31 = (s32[]{:T(128)}, f32[1024,8,64]{0,2,1:T(8,128)S(1)}, f32[1024,8,64]{0,2,1:T(8,128)}, f32[2,512,8,64]{1,0,3,2:T(2,128)}, s32[2]{0:T(128)S(1)}, /*inde...) while((s32[]{:T(128)}, f32[1024,8,64]{0,2,1:T(8,128)S(1)}, ...), condition=%wide.region_11.12_spmd.clone, body=%wide.region_9.11_spmd.clone.sunk | while | flops 2730750464 | bytes 187791856 | solution.py:200
  799.1 13.9 multiply_reduce_fusion.3
  829.8 19.7 %dynamic_update_slice.33 = f32[2,512,8,64]{1,0,3,2:T(2,128)} dynamic-update-slice(f32[2,512,8,64]{1,0,3,2:T(2,128)} %get-tuple-element.624, f32[1,512,8,64]{1,0,3,2:T(1,128)} %copy.79, s32[]{:T(128)} %get-tuple-element.621, s32[]{:T(128)} %constant.173.clone.1..sunk.1, s32[]{:T(128)} %constant.173.clone.1..sunk.1, s32[]{:T(128)} %constant.173.clone.1..sunk.1) | dynamic-update-slice | bytes 2097156 | tf_op jit(solution)/shard_map/while/body/jit(dynamic_update_index_in_dim)/dynamic_update_slice | solution.py:149
  879.3 14.0 multiply_reduce_fusion.3
  910.0 19.6 %dynamic_update_slice.33 = f32[2,512,8,64]{1,0,3,2:T(2,128)} dynamic-update-slice(f32[2,512,8,64]{1,0,3,2:T(2,128)} %get-tuple-element.624, f32[1,512,8,64]{1,0,3,2:T(1,128)} %copy.79, s32[]{:T(128)} %get-tuple-element.621, s32[]{:T(128)} %constant.173.clone.1..sunk.1, s32[]{:T(128)} %constant.173.clone.1..sunk.1, s32[]{:T(128)} %constant.173.clone.1..sunk.1) | dynamic-update-slice | bytes 2097156 | tf_op jit(solution)/shard_map/while/body/jit(dynamic_update_index_in_dim)/dynamic_update_slice | solution.py:149
  959.4 18.9 %convert_reduce_fusion = (f32[2048]{0:T(1024)S(1)}, bf16[1024,2048]{1,0:T(8,128)(2,1)S(1)}) fusion(f32[1024,2048]{1,0:T(8,128)} %copy-done.39, f32[2048]{0:T(1024)S(1)} %copy-done.36, bf16[1024,2048]{1,0:T(8,128)(2,1)} %all-gather.17.cloned.1.call-done, bf16[2048,2048]{1,0:T(8,128)(2,1)} %all-gather.15.cloned.1.call-done), kind=kOutput, calls=%fused_computation.51 | convolution fusion | flops 8638167040 | bytes 25182208 | tf_op jit(solution)/shard_map/sd,fd->sf/dot_general | solution.py:175
  978.4 12.8 fusion.78
  1001.9 16.5 fusion.68
  1040.3 31.7 %reduce-scatter.10.cloned.1.call-done = f32[256,2048]{1,0:T(8,128)} async-done(((f32[1024,2048]{1,0:T(8,128)}), f32[256,2048]{1,0:T(8,128)}) %reduce-scatter.10.cloned.1.call-update) | async-done | bytes 2097168 | tf_op jit(solution)/shard_map/reduce_scatter | solution.py:213
  1074.7 71.6 %reduce-scatter.8.cloned.1.call-done = f32[256,2048]{1,0:T(8,128)} async-done(((f32[1024,2048]{1,0:T(8,128)}), f32[256,2048]{1,0:T(8,128)}) %reduce-scatter.8.cloned.1.call-update) | async-done | bytes 2097168 | tf_op jit(solution)/shard_map/reduce_scatter | solution.py:153
  1153.7 15.2 fusion.80
  1174.0 183.7 %reduce-scatter.12.cloned.1.call-done = f32[3,256,512]{1,2,0:T(8,128)} async-done(((f32[3,2048,512]{1,2,0:T(8,128)}), f32[3,256,512]{1,2,0:T(8,128)}) %reduce-scatter.12.cloned.1.call-update) | async-done | bytes 1572880 | tf_op jit(solution)/shard_map/reduce_scatter | solution.py:250
  1371.7 50.1 %reduce-scatter.20.cloned.1.call-done = f32[11,256]{1,0:T(8,128)} async-done(((f32[11,2048]{1,0:T(8,128)}), f32[11,256]{1,0:T(8,128)}) %reduce-scatter.20.cloned.1.call-update) | async-done | bytes 11280 | tf_op jit(solution)/shard_map/reduce_scatter | solution.py:254
  1433.1 274.3 %reduce-scatter.16.cloned.1.call-done = f32[256,2048]{1,0:T(8,128)} async-done(((f32[2048,2048]{1,0:T(8,128)}), f32[256,2048]{1,0:T(8,128)}) %reduce-scatter.16.cloned.1.call-update) | async-done | bytes 2097168 | tf_op jit(solution)/shard_map/reduce_scatter | solution.py:252
  (232 shorter events, 275.8 us)
Async XLA Ops:
  7.2 75.7 %all-gather.7.cloned.1.call-start = ((), (), s32[]{:S(2)}) async-start(), calls=%async_computation.7 | async-start | bytes 5242880 | tf_op jit(solution)/shard_map/all_gather | solution.py:111
  47.3 138.1 %all-gather.9.cloned.1.call-start = ((), (), s32[]{:S(2)}) async-start(), calls=%async_computation.8 | async-start | bytes 7077888 | tf_op jit(solution)/shard_map/all_gather | solution.py:99
  49.0 187.8 %all-gather.17.cloned.1.call-start = ((), (), s32[]{:S(2)}) async-start(), calls=%async_computation.13 | async-start | bytes 5242880 | tf_op jit(solution)/shard_map/all_gather | solution.py:167
  49.7 297.8 %all-gather.13.cloned.1.call-start = ((), (), s32[]{:S(2)}) async-start(), calls=%async_computation.10 | async-start | bytes 9437184 | tf_op jit(solution)/shard_map/all_gather | solution.py:101
  52.5 385.2 %reduce-scatter.14.cloned.1.call-start = ((), (), s32[]{:S(2)}) async-start(), calls=%async_computation.16 | async-start | bytes 4718592 | tf_op jit(solution)/shard_map/reduce_scatter | solution.py:251
  243.8 480.7 %reduce-scatter.18.cloned.1.call-start = ((), (), s32[]{:S(2)}) async-start(), calls=%async_computation.18 | async-start | bytes 18874368 | tf_op jit(solution)/shard_map/reduce_scatter | solution.py:253
  244.6 115.6 %copy-start.35 = (f32[2048]{0:T(1024)}, f32[2048]{0:T(1024)S(1)}, u32[]{:S(2)}) copy-start(f32[2048]{0:T(1024)S(1)} %dynamic_slice.48) | copy-start | bytes 24580
  376.2 61.6 %copy-start.20 = (f32[512,256]{1,0:T(8,128)S(1)}, f32[512,256]{1,0:T(8,128)}, u32[]{:S(2)}) copy-start(f32[512,256]{1,0:T(8,128)} %param.29) | copy-start | bytes 1572868
  376.2 61.6 %copy-start.21 = (f32[512,256]{1,0:T(8,128)S(1)}, f32[512,256]{1,0:T(8,128)}, u32[]{:S(2)}) copy-start(f32[512,256]{1,0:T(8,128)} %param.30) | copy-start | bytes 1572868
  376.2 401.0 %all-gather.11.cloned.1.call-start = ((), (), s32[]{:S(2)}) async-start(), calls=%async_computation.9 | async-start | bytes 2359296 | tf_op jit(solution)/shard_map/all_gather | solution.py:100
  440.3 519.1 %all-gather.15.cloned.1.call-start = ((), (), s32[]{:S(2)}) async-start(), calls=%async_computation.11 | async-start | bytes 9437184 | tf_op jit(solution)/shard_map/all_gather | solution.py:102
  732.6 339.3 %reduce-scatter.10.cloned.1.call-start = ((), (), s32[]{:S(2)}) async-start(), calls=%async_computation.14 | async-start | bytes 10485760 | tf_op jit(solution)/shard_map/reduce_scatter | solution.py:213
  1001.9 144.4 %reduce-scatter.8.cloned.1.call-start = ((), (), s32[]{:S(2)}) async-start(), calls=%async_computation.12 | async-start | bytes 10485760 | tf_op jit(solution)/shard_map/reduce_scatter | solution.py:153
  1024.3 333.3 %reduce-scatter.12.cloned.1.call-start = ((), (), s32[]{:S(2)}) async-start(), calls=%async_computation.15 | async-start | bytes 14155776 | tf_op jit(solution)/shard_map/reduce_scatter | solution.py:250
  1037.7 108.7 %copy-start.27 = (f32[1,2048]{1,0:T(1,128)S(1)}, f32[1,2048]{1,0:T(1,128)}, u32[]{:S(2)}) copy-start(f32[1,2048]{1,0:T(1,128)} %get-tuple-element.420) | copy-start | bytes 24580
  1037.7 108.6 %copy-start.28 = (f32[1,2048]{1,0:T(1,128)S(1)}, f32[1,2048]{1,0:T(1,128)}, u32[]{:S(2)}) copy-start(f32[1,2048]{1,0:T(1,128)} %get-tuple-element.421) | copy-start | bytes 24580
  1037.7 384.1 %reduce-scatter.20.cloned.1.call-start = ((), (), s32[]{:S(2)}) async-start(), calls=%async_computation.19 | async-start | bytes 147456 | tf_op jit(solution)/shard_map/reduce_scatter | solution.py:254
  1071.9 74.4 %copy-start.9 = (f32[256,2048]{1,0:T(8,128)S(1)}, f32[256,2048]{1,0:T(8,128)}, u32[]{:S(2)}) copy-start(f32[256,2048]{1,0:T(8,128)} %reduce-scatter.10.cloned.1.call-done) | copy-start | bytes 6291460
  1153.7 553.7 %reduce-scatter.16.cloned.1.call-start = ((), (), s32[]{:S(2)}) async-start(), calls=%async_computation.17 | async-start | bytes 18874368 | tf_op jit(solution)/shard_map/reduce_scatter | solution.py:252
  1168.9 188.7 %copy-start.7 = (f32[3,256,512]{1,2,0:T(8,128)S(1)}, f32[3,256,512]{1,2,0:T(8,128)}, u32[]{:S(2)}) copy-start(f32[3,256,512]{1,2,0:T(8,128)} %copy-done.6) | copy-start | bytes 4718596
  1365.5 66.9 %copy-start.26 = (f32[11,256]{1,0:T(8,128)S(1)}, f32[11,256]{1,0:T(8,128)}, u32[]{:S(2)}) copy-start(f32[11,256]{1,0:T(8,128)} %param.37) | copy-start | bytes 33796
  1365.5 66.9 %copy-start.33 = (f32[11,256]{1,0:T(8,128)S(1)}, f32[11,256]{1,0:T(8,128)}, u32[]{:S(2)}) copy-start(f32[11,256]{1,0:T(8,128)} %param.38) | copy-start | bytes 33796
  1365.5 66.9 %copy-start.34 = (f32[11,256]{1,0:T(8,128)S(1)}, f32[11,256]{1,0:T(8,128)}, u32[]{:S(2)}) copy-start(f32[11,256]{1,0:T(8,128)} %param.39) | copy-start | bytes 33796
  1365.5 341.9 %copy-start.8 = (f32[256,2048]{1,0:T(8,128)S(1)}, f32[256,2048]{1,0:T(8,128)}, u32[]{:S(2)}) copy-start(f32[256,2048]{1,0:T(8,128)} %param.31) | copy-start | bytes 6291460
  (33 other events, 442.1 us)
Sparse Core Ops, SparseCore 0:
  47.5 35.3 all-gather.6
  85.5 99.9 all-gather.8
  187.0 32.6 all-gather.16
  222.3 125.2 all-gather.12
  351.1 86.6 reduce-scatter.13
  441.9 282.5 reduce-scatter.17
  727.1 50.0 all-gather.10
  779.8 123.5 all-gather.14
  1002.0 69.8 reduce-scatter.9
  1074.5 71.7 reduce-scatter.7
  1149.9 207.6 reduce-scatter.11
  1361.4 60.3 reduce-scatter.19
  1425.6 281.8 reduce-scatter.15
where the time goes:
time: 1730 us; the launch traced here: 1720 us
  waiting for transfers between devices  1230 us (71%)
  matrix products  241 us (14%)
  local copies, waits for them, and re-layouts  86.6 us (5%)
  other arithmetic  86.5 us (5%)
  blocking collectives  48.2 us (3%)
    reduce_scatter x1, waiting for transfers between devices, per_device(): lax.psum_scatter(shrink_grad, 'dp', scatter_dimension=1, tiled=True)  284 us
    reduce_scatter x1, waiting for transfers between devices, per_device(): lax.psum_scatter(expand_grad, 'dp', scatter_dimension=0, tiled=True)  274 us
    reduce_scatter x1, waiting for transfers between devices, per_device(): lax.psum_scatter(qkv_grad, 'dp', scatter_dimension=1, tiled=True)  184 us
    all_gather x1, waiting for transfers between devices, per_device(): lax.all_gather(expand_low, 'dp', axis=0, tiled=True)  103 us
    all_gather x1, waiting for transfers between devices, per_device(): lax.all_gather(qkv_low, 'dp', axis=1, tiled=True)  103 us
    reduce_scatter x1, waiting for transfers between devices, per_device(): lax.psum_scatter(jnp.dot(attended, dense_full, preferred_element_type=wid...  71.6 us
    reduce_scatter x1, waiting for transfers between devices, per_device(): lax.psum_scatter(dense_grad, 'dp', scatter_dimension=1, tiled=True)  61.5 us
    reduce_scatter x1, waiting for transfers between devices, per_device(): lax.psum_scatter(params_grad, 'dp', scatter_dimension=1, tiled=True)  50.1 us
  transfers between devices with their start and end apart: 13, of which 11 were waited for; matrix products, arithmetic and copies ran while one was open for 20% of the time, Pallas kernels for 0%

commit v1 on v0

v1 whole, which is shorter than its diff:
```python
import functools
import jax
import jax.numpy as jnp
from jax import lax
from jax.experimental import pallas as pl
from jax.experimental.pallas import tpu as pltpu
from jax.sharding import PartitionSpec as P

D = 2048
HD = 64
ROT = 32
FF = 8192
STEP = 10

norm_eps = 1e-05
beta_first = 0.9
beta_second = 0.95
adam_eps = 1e-08
weight_decay = 0.1
matrix_rate = 0.05
vector_rate = 1.0
masked_score = -1e30

SUB_BIT = 1
ROW_BIT = 0

bf16 = jnp.bfloat16
f32 = jnp.float32


def exchange(values, axis, bit):
    count = lax.axis_size(axis)
    return lax.ppermute(values, axis, [(i, i ^ (1 << bit)) for i in range(count)])


def place_order(count):
    bits = count.bit_length() - 1
    order = []
    for p in range(count):
        high = (p >> 1) & ((1 << (bits - 2)) - 1)
        order.append(((p & 1) << SUB_BIT) | (high << 2) | ((p >> (bits - 1)) << ROW_BIT))
    return order


def adam_update(weight, first, second, grad, rate, decay):
    first_new = beta_first * first + (1.0 - beta_first) * grad
    second_new = beta_second * second + (1.0 - beta_second) * grad * grad
    first_hat = first_new / (1.0 - beta_first**STEP)
    second_hat = second_new / (1.0 - beta_second**STEP)
    weight_new = weight - rate * (first_hat / (jnp.sqrt(second_hat) + adam_eps) + decay * weight)
    return (weight_new, first_new, second_new)


def gelu_value(pre_values):
    return jax.nn.gelu(pre_values, approximate=True)


def vmem_params(mib):
    return pltpu.CompilerParams(vmem_limit_bytes=mib * 2**20)


def place_of(block, count):
    bits = count.bit_length() - 1
    return ((block >> SUB_BIT) & 1) | ((block >> 2) << 1) | (((block >> ROW_BIT) & 1) << (bits - 1))


def move_blocks(count, source, load, store):
    width = D // count
    if width % 128 == 0:
        for j in range(count):
            start = pl.multiple_of(source(j) * width, width)
            store(pl.ds(j * width, width), load(pl.ds(start, width)))
        return
    for unit in range(count // 2):
        parts = []
        for half in range(2):
            block = source(2 * unit + half)
            value = load(pl.ds(pl.multiple_of((block >> 1) * 128, 128), 128))
            parts.append(pltpu.roll(value, ((block & 1) ^ half) * 64, 1))
        lane = lax.broadcasted_iota(jnp.int32, parts[0].shape, 1)
        store(pl.ds(unit * 128, 128), jnp.where(lane < 64, parts[0], parts[1]))


def norm_kernel(order, me_ref, x_ref, dy_ref, g_ref, b_ref, n_ref, ns_ref, dyr_ref, dys_ref, dysum_ref, tmp):
    me = me_ref[0]
    count = len(order)
    rows = x_ref[...].astype(f32)
    mean = jnp.mean(rows, axis=-1, keepdims=True)
    centered = rows - mean
    inv = lax.rsqrt(jnp.mean(centered * centered, axis=-1, keepdims=True) + norm_eps)
    tmp[...] = centered * inv * g_ref[...] + b_ref[...]
    dysum_ref[...] = jnp.sum(dy_ref[...].astype(f32), axis=0, keepdims=True)

    def store_to(ref):
        def store(lanes, value):
            ref[:, lanes] = value.astype(bf16)

        return store

    for flip, n_out, dy_out in ((0, n_ref, dyr_ref), (1, ns_ref, dys_ref)):
        source = lambda j: me ^ order[j ^ flip]
        move_blocks(count, source, lambda lanes: tmp[:, lanes], store_to(n_out))
        move_blocks(count, source, lambda lanes: dy_ref[:, lanes].astype(f32), store_to(dy_out))


def smem_spec():
    return pl.BlockSpec(memory_space=pltpu.SMEM)


def norm_call(order, me, x, dy, gain, shift):
    shape = jax.ShapeDtypeStruct(x.shape, bf16)
    vm = pl.BlockSpec(memory_space=pltpu.VMEM)
    return pl.pallas_call(
        functools.partial(norm_kernel, order),
        out_shape=[shape, shape, shape, shape, jax.ShapeDtypeStruct((1, D), f32)],
        in_specs=[smem_spec(), vm, vm, vm, vm],
        out_specs=[vm] * 5,
        scratch_shapes=[pltpu.VMEM(x.shape, f32)],
        compiler_params=vmem_params(32),
        name="norm",
    )(me, x, dy, gain, shift)


def assemble(order, me, keep_ref, recv_ref, tmp):
    count = len(order)

    def store(lanes, value):
        tmp[:, lanes] = value

    def add(lanes, value):
        tmp[:, lanes] += value

    move_blocks(count, lambda j: place_of(j ^ me, count), lambda lanes: keep_ref[:, lanes].astype(f32), store)
    move_blocks(count, lambda j: place_of(j ^ me, count) ^ 1, lambda lanes: recv_ref[:, lanes].astype(f32), add)


def out_kernel(order, me_ref, x_ref, keep_ref, recv_ref, b_ref, o_ref, tmp):
    assemble(order, me_ref[0], keep_ref, recv_ref, tmp)
    o_ref[...] = (x_ref[...].astype(f32) + tmp[...] + b_ref[0:1] + b_ref[1:2]).astype(bf16)


def out_call(order, me, x, keep, recv, biases):
    vm = pl.BlockSpec(memory_space=pltpu.VMEM)
    return pl.pallas_call(
        functools.partial(out_kernel, order),
        out_shape=jax.ShapeDtypeStruct(x.shape, bf16),
        in_specs=[smem_spec(), vm, vm, vm, vm],
        out_specs=vm,
        scratch_shapes=[pltpu.VMEM(x.shape, f32)],
        compiler_params=vmem_params(32),
        name="block_output",
    )(me, x, keep, recv, biases)


def norm_back_kernel(order, me_ref, x_ref, dy_ref, keep_ref, recv_ref, g_ref, o_ref, sums_ref, tmp):
    assemble(order, me_ref[0], keep_ref, recv_ref, tmp)
    rows = x_ref[...].astype(f32)
    centered = rows - jnp.mean(rows, axis=-1, keepdims=True)
    inv = lax.rsqrt(jnp.mean(centered * centered, axis=-1, keepdims=True) + norm_eps)
    unit = centered * inv
    back = tmp[...]
    sums_ref[0:1] = jnp.sum(back * unit, axis=0, keepdims=True)
    sums_ref[1:2] = jnp.sum(back, axis=0, keepdims=True)
    e = back * g_ref[...]
    o_ref[...] = dy_ref[...].astype(f32) + inv * (
        e - jnp.mean(e, axis=-1, keepdims=True) - unit * jnp.mean(e * unit, axis=-1, keepdims=True)
    )


def norm_back_call(order, me, x, dy, keep, recv, gain):
    vm = pl.BlockSpec(memory_space=pltpu.VMEM)
    return pl.pallas_call(
        functools.partial(norm_back_kernel, order),
        out_shape=[jax.ShapeDtypeStruct(x.shape, f32), jax.ShapeDtypeStruct((2, D), f32)],
        in_specs=[smem_spec()] + [vm] * 5,
        out_specs=[vm, vm],
        scratch_shapes=[pltpu.VMEM(x.shape, f32)],
        compiler_params=vmem_params(40),
        name="norm_back",
    )(me, x, dy, keep, recv, gain)


def swap_rotary(values):
    lane = lax.broadcasted_iota(jnp.int32, values.shape, 1)
    half = ROT // 2
    return jnp.where(
        lane % ROT < half, pltpu.roll(values, 128 - half, 1), pltpu.roll(values, half, 1)
    )


def rel_block(me_t, block, bits):
    rel = me_t ^ block
    return tuple((rel >> b) & 1 for b in range(bits))


def dot_nn(a, b):
    return lax.dot_general(a, b, (((1,), (0,)), ((), ())), preferred_element_type=f32)


def dot_nt(a, b):
    return lax.dot_general(a, b, (((1,), (1,)), ((), ())), preferred_element_type=f32)


def mask_bias(bias, dcol_ref, drow_ref, qb, rows):
    kend = (qb + 1) * rows
    shape = (kend, rows)
    key = lax.broadcasted_iota(jnp.int32, shape, 0)
    query = lax.broadcasted_iota(jnp.int32, shape, 1) + qb * rows
    same = dcol_ref[0, :kend, :] == drow_ref[0, 0:1, qb * rows : kend]
    bias[:kend, :] = jnp.where(same & (key <= query), 0.0, masked_score)


def attend_kernel(
    tbits, width, me_ref, proj_ref, cos_ref, sin_ref, dcol_ref, drow_ref, o_ref, qkv_ref, lse_ref, bias
):
    me_t = me_ref[1]
    rows = proj_ref.shape[-2]
    blocks = 1 << tbits
    scale = HD ** (-0.5)
    pairs = width // 128
    for b in range(blocks):
        rel = rel_block(me_t, b, tbits)
        place = slice(b * rows, (b + 1) * rows)
        cosine = cos_ref[0, place, :]
        sine = sin_ref[0, place, :]
        for j in range(2 * pairs):
            lanes = slice(j * 128, (j + 1) * 128)
            part = proj_ref[rel + (0, slice(None), lanes)]
            qkv_ref[0, place, lanes] = (part * cosine + swap_rotary(part) * sine).astype(bf16)
        qkv_ref[0, place, 2 * width :] = proj_ref[rel + (0, slice(None), slice(2 * width, None))].astype(bf16)
    lane = lax.broadcasted_iota(jnp.int32, (rows, 128), 1)
    zero = jnp.zeros((rows, 128), bf16)
    for qb in range(blocks):
        kend = (qb + 1) * rows
        place = slice(qb * rows, kend)
        rel = rel_block(me_t, qb, tbits)
        mask_bias(bias, dcol_ref, drow_ref, qb, rows)

        def pair_body(pair, carry):
            base = pl.multiple_of(pair * 128, 128)
            q = qkv_ref[0, place, pl.ds(base, 128)] * jnp.asarray(scale, bf16)
            k = qkv_ref[0, :kend, pl.ds(base + width, 128)]
            v = qkv_ref[0, :kend, pl.ds(base + 2 * width, 128)]
            vt = v.T
            outs = []
            for h in range(2):
                mine = (lane < HD) if h == 0 else (lane >= HD)
                s = dot_nt(k, jnp.where(mine, q, zero)) + bias[:kend, :]
                peak = jnp.max(s, axis=0, keepdims=True)
                expo = jnp.exp(s - peak)
                total = jnp.sum(expo, axis=0, keepdims=True)
                weights = (expo * (1.0 / total)).astype(bf16)
                outs.append(dot_nn(vt[h * HD : (h + 1) * HD, :], weights))
                lse_ref[0, pl.ds(pair * 2 + h, 1), place] = peak + jnp.log(total)
            both = jnp.concatenate(outs, axis=0)
            o_ref[rel + (0, slice(None), pl.ds(base, 128))] = both.T.astype(bf16)
            return carry

        lax.fori_loop(0, pairs, pair_body, 0)


def attend_call(me, proj, cosine, sine, doc_col, doc_row):
    tbits = proj.ndim - 3
    seqs = proj.shape[tbits]
    rows = proj.shape[-2]
    width = proj.shape[-1] // 3
    length = rows << tbits
    lead = (2,) * tbits
    seq3 = lambda s: (s, 0, 0)
    rel_map = lambda s: (0,) * tbits + (s, 0, 0)
    heads = width // HD
    return pl.pallas_call(
        functools.partial(attend_kernel, tbits, width),
        grid=(seqs,),
        out_shape=[
            jax.ShapeDtypeStruct(lead + (seqs, rows, width), bf16),
            jax.ShapeDtypeStruct((seqs, length, 3 * width), bf16),
            jax.ShapeDtypeStruct((seqs, heads, length), f32),
        ],
        in_specs=[
            smem_spec(),
            pl.BlockSpec(lead + (1, rows, 3 * width), rel_map),
            pl.BlockSpec((1, length, 128), seq3),
            pl.BlockSpec((1, length, 128), seq3),
            pl.BlockSpec((1, length, 1), seq3),
            pl.BlockSpec((1, 1, length), seq3),
        ],
        out_specs=[
            pl.BlockSpec(lead + (1, rows, width), rel_map),
            pl.BlockSpec((1, length, 3 * width), seq3),
            pl.BlockSpec((1, heads, length), seq3),
        ],
        scratch_shapes=[pltpu.VMEM((length, rows), f32)],
        compiler_params=vmem_params(50),
        name="attend",
    )(me, proj, cosine, sine, doc_col, doc_row)


def attend_back_kernel(
    tbits, width, me_ref, qkv_ref, do_ref, lse_ref, cos_ref, sin_ref, dcol_ref, drow_ref, o_ref, sum_ref, bias, dk, dv
):
    me_t = me_ref[1]
    rows = do_ref.shape[-2]
    blocks = 1 << tbits
    scale = HD ** (-0.5)
    pairs = width // 128
    lane = lax.broadcasted_iota(jnp.int32, (rows, 128), 1)
    zero = jnp.zeros((rows, 128), bf16)
    dk[...] = jnp.zeros_like(dk)
    dv[...] = jnp.zeros_like(dv)
    sum_ref[...] = jnp.zeros_like(sum_ref)
    for qb in range(blocks):
        kend = (qb + 1) * rows
        place = slice(qb * rows, kend)
        rel = rel_block(me_t, qb, tbits)
        mask_bias(bias, dcol_ref, drow_ref, qb, rows)

        def pair_body(pair, carry):
            base = pl.multiple_of(pair * 128, 128)
            lanes = pl.ds(base, 128)
            q = qkv_ref[0, place, lanes]
            k = qkv_ref[0, :kend, pl.ds(base + width, 128)]
            v = qkv_ref[0, :kend, pl.ds(base + 2 * width, 128)]
            kt = k.T
            do = do_ref[rel + (0, slice(None), lanes)]
            outs = []
            for h in range(2):
                mine = (lane < HD) if h == 0 else (lane >= HD)
                qm = jnp.where(mine, q, zero) * jnp.asarray(scale, bf16)
                dom = jnp.where(mine, do, zero)
                s = dot_nt(k, qm) + bias[:kend, :]
                probs = jnp.exp(s - lse_ref[0, pl.ds(pair * 2 + h, 1), place])
                dprobs = dot_nt(v, dom)
                inner = jnp.sum(probs * dprobs, axis=0, keepdims=True)
                ds = (probs * (dprobs - inner)).astype(bf16)
                dv[:kend, lanes] += dot_nn(probs.astype(bf16), dom)
                dk[:kend, lanes] += dot_nn(ds, qm)
                outs.append(dot_nn(kt[h * HD : (h + 1) * HD, :], ds))
            dq = jnp.concatenate(outs, axis=0).T * scale
            dq = dq * cos_ref[0, place, :] - swap_rotary(dq) * sin_ref[0, place, :]
            dq = dq.astype(bf16)
            o_ref[rel + (0, slice(None), lanes)] = dq
            sum_ref[0, :, lanes] += jnp.sum(dq.astype(f32), axis=0, keepdims=True)
            return carry

        lax.fori_loop(0, pairs, pair_body, 0)
    for b in range(blocks):
        rel = rel_block(me_t, b, tbits)
        place = slice(b * rows, (b + 1) * rows)
        cosine = cos_ref[0, place, :]
        sine = sin_ref[0, place, :]
        for j in range(pairs):
            lanes = slice(j * 128, (j + 1) * 128)
            part = dk[place, lanes]
            part = (part * cosine - swap_rotary(part) * sine).astype(bf16)
            kl = slice(width + j * 128, width + (j + 1) * 128)
            o_ref[rel + (0, slice(None), kl)] = part
            sum_ref[0, :, kl] += jnp.sum(part.astype(f32), axis=0, keepdims=True)
            part = dv[place, lanes].astype(bf16)
            vl = slice(2 * width + j * 128, 2 * width + (j + 1) * 128)
            o_ref[rel + (0, slice(None), vl)] = part
            sum_ref[0, :, vl] += jnp.sum(part.astype(f32), axis=0, keepdims=True)


def attend_back_call(me, qkv, do, lse, cosine, sine, doc_col, doc_row):
    tbits = do.ndim - 3
    seqs = do.shape[tbits]
    rows = do.shape[-2]
    width = do.shape[-1]
    length = rows << tbits
    lead = (2,) * tbits
    seq3 = lambda s: (s, 0, 0)
    rel_map = lambda s: (0,) * tbits + (s, 0, 0)
    heads = width // HD
    return pl.pallas_call(
        functools.partial(attend_back_kernel, tbits, width),
        grid=(seqs,),
        out_shape=[
            jax.ShapeDtypeStruct(lead + (seqs, rows, 3 * width), bf16),
            jax.ShapeDtypeStruct((seqs, 1, 3 * width), f32),
        ],
        in_specs=[
            smem_spec(),
            pl.BlockSpec((1, length, 3 * width), seq3),
            pl.BlockSpec(lead + (1, rows, width), rel_map),
            pl.BlockSpec((1, heads, length), seq3),
            pl.BlockSpec((1, length, 128), seq3),
            pl.BlockSpec((1, length, 128), seq3),
            pl.BlockSpec((1, length, 1), seq3),
            pl.BlockSpec((1, 1, length), seq3),
        ],
        out_specs=[
            pl.BlockSpec(lead + (1, rows, 3 * width), rel_map),
            pl.BlockSpec((1, 1, 3 * width), seq3),
        ],
        scratch_shapes=[
            pltpu.VMEM((length, rows), f32),
            pltpu.VMEM((length, width), f32),
            pltpu.VMEM((length, width), f32),
        ],
        compiler_params=vmem_params(50),
        name="attend_back",
    )(me, qkv, do, lse, cosine, sine, doc_col, doc_row)


def rotary_tables(doc_ids):
    length = doc_ids.shape[1]
    places = jnp.arange(length, dtype=jnp.int32)[None, :]
    before = jnp.concatenate([doc_ids[:, :1] - 1, doc_ids[:, :-1]], axis=1)
    starts = jnp.where(doc_ids != before, places, 0)
    first = lax.cummax(starts, axis=1)
    pos = (places - first).astype(f32)
    half = ROT // 2
    freqs = 10000.0 ** (-jnp.arange(half, dtype=f32) / half)
    angle = pos[:, :, None] * freqs
    cosine = jnp.cos(angle)
    sine = jnp.sin(angle)
    rest = doc_ids.shape + (HD - ROT,)
    cosine = jnp.concatenate([cosine, cosine, jnp.ones(rest, f32)], axis=-1)
    sine = jnp.concatenate([-sine, sine, jnp.zeros(rest, f32)], axis=-1)
    return jnp.concatenate([cosine, cosine], axis=-1), jnp.concatenate([sine, sine], axis=-1)


def per_device(
    inputs,
    segments,
    cotangent,
    qkv_weight,
    qkv_first,
    qkv_second,
    dense_weight,
    dense_first,
    dense_second,
    expand_weight,
    expand_first,
    expand_second,
    shrink_weight,
    shrink_first,
    shrink_second,
    small_params,
    small_first,
    small_second,
):
    dp = lax.axis_size("dp")
    tensor_count = lax.axis_size("tensor")
    dbits = dp.bit_length() - 1
    tbits = tensor_count.bit_length() - 1
    d_me = lax.axis_index("dp")
    t_me = lax.axis_index("tensor")
    sub = (d_me >> SUB_BIT) & 1
    order = place_order(dp)
    high_bits = list(range(2, dbits))
    gather_bits = high_bits + [ROW_BIT]
    rows = inputs.shape[0]
    me = jnp.stack([d_me, t_me]).astype(jnp.int32)

    stack = small_params.astype(bf16)[None]
    for bit in [SUB_BIT] + gather_bits:
        stack = jnp.concatenate([stack, exchange(stack, "dp", bit)], axis=0)
    block_of = jnp.asarray(order, jnp.int32) ^ d_me
    hit = jnp.arange(dp, dtype=jnp.int32)[:, None] == block_of[None, :]
    params = jnp.sum(
        jnp.where(hit[:, :, None, None], stack.astype(f32)[None], 0.0), axis=1
    )
    params = jnp.transpose(params, (1, 0, 2)).reshape(small_params.shape[0], D)

    ids = segments
    ids = jnp.concatenate([ids, exchange(ids, "dp", SUB_BIT)], axis=0)
    for bit in range(tbits):
        other = exchange(ids, "tensor", bit)
        flag = ((t_me >> bit) & 1) == 0
        ids = jnp.concatenate([jnp.where(flag, ids, other), jnp.where(flag, other, ids)], axis=1)
    cosine, sine = rotary_tables(ids)
    doc_col = ids[:, :, None]
    doc_row = ids[:, None, :]

    normed_own, normed_swap, back_own, back_swap, back_sum = norm_call(
        order, me, inputs, cotangent, params[0:1], params[1:2]
    )

    def gather_tokens(own, swapped):
        pieces = [own, exchange(swapped, "dp", SUB_BIT)]
        for bit in reversed(range(tbits)):
            pieces = pieces + [exchange(piece, "tensor", bit) for piece in pieces]
        return jnp.concatenate(pieces, axis=0)

    def gather_weight(low, split_axis, gather_axis):
        half = low.shape[split_axis] // 2
        keep = lax.dynamic_slice_in_dim(low, sub * half, half, split_axis)
        send = lax.dynamic_slice_in_dim(low, (1 - sub) * half, half, split_axis)
        pieces = [keep, exchange(send, "dp", SUB_BIT)]
        for bit in gather_bits:
            pieces = pieces + [exchange(piece, "dp", bit) for piece in pieces]
        return jnp.concatenate(pieces, axis=gather_axis)

    qkv_full = gather_weight(qkv_weight.astype(bf16), 2, 1)
    width = qkv_full.shape[2]
    qkv_wide = jnp.transpose(qkv_full, (1, 0, 2)).reshape(D, 3 * width)
    normed = gather_tokens(normed_own, normed_swap)
    expand_full = gather_weight(expand_weight.astype(bf16), 1, 0)
    hidden = expand_full.shape[1]
    back_rows = gather_tokens(back_own, back_swap)
    dense_full = gather_weight(dense_weight.astype(bf16), 0, 1)
    shrink_full = gather_weight(shrink_weight.astype(bf16), 0, 1)
    tokens = normed.shape[0]

    head_start = t_me * (2 * width) + sub * width
    hidden_start = t_me * (2 * hidden) + sub * hidden
    qkv_bias = lax.dynamic_slice_in_dim(params[2:5], head_start, width, 1).reshape(3 * width)
    expand_bias = lax.dynamic_slice_in_dim(params[7:].reshape(FF), hidden_start, hidden, 0)

    lead = (2,) * tbits
    proj = jnp.dot(normed, qkv_wide, preferred_element_type=f32) + qkv_bias
    attended, qkv_low, lse = attend_call(
        me, proj.reshape(lead + (2, rows, 3 * width)), cosine, sine, doc_col, doc_row
    )
    attended = attended.reshape(tokens, width)
    hidden_pre = jnp.dot(normed, expand_full, preferred_element_type=f32) + expand_bias
    hidden_act = gelu_value(hidden_pre).astype(bf16)

    def scatter_tokens(partial):
        half = tokens // 2
        recv = exchange(partial(half, tokens).astype(bf16), "tensor", 0)
        part = (partial(0, half) + recv.astype(f32)).astype(bf16)
        for bit in range(1, tbits):
            half = half // 2
            recv = exchange(part[half:], "tensor", bit)
            part = (part[:half].astype(f32) + recv.astype(f32)).astype(bf16)
        return part[:rows], exchange(part[rows:], "dp", SUB_BIT)

    def branch(start, stop):
        return jnp.dot(attended[start:stop], dense_full, preferred_element_type=f32) + jnp.dot(
            hidden_act[start:stop], shrink_full, preferred_element_type=f32
        )

    keep, recv = scatter_tokens(branch)
    output = out_call(order, me, inputs, keep, recv, params[5:7])

    def scatter_weight(partial, split_axis, gather_axis):
        recv = exchange(partial(1).astype(bf16), "dp", ROW_BIT)
        part = (partial(0) + recv.astype(f32)).astype(bf16)
        for bit in reversed(high_bits):
            half = part.shape[gather_axis] // 2
            recv = exchange(lax.slice_in_dim(part, half, 2 * half, axis=gather_axis), "dp", bit)
            part = (lax.slice_in_dim(part, 0, half, axis=gather_axis).astype(f32) + recv.astype(f32)).astype(bf16)
        half = part.shape[gather_axis] // 2
        recv = exchange(lax.slice_in_dim(part, half, 2 * half, axis=gather_axis), "dp", SUB_BIT)
        keep = lax.slice_in_dim(part, 0, half, axis=gather_axis)
        flag = sub == 0
        return jnp.concatenate(
            [jnp.where(flag, keep, recv), jnp.where(flag, recv, keep)], axis=split_axis
        ).astype(f32)

    halves = [slice(0, D // 2), slice(D // 2, D)]
    shrink_sum = scatter_weight(
        lambda i: jnp.einsum("sf,sd->fd", hidden_act, back_rows[:, halves[i]], preferred_element_type=f32), 0, 1
    )
    dense_sum = scatter_weight(
        lambda i: jnp.einsum("sk,sd->kd", attended, back_rows[:, halves[i]], preferred_element_type=f32), 0, 1
    )

    attended_back = jnp.einsum("sd,kd->sk", back_rows, dense_full, preferred_element_type=f32).astype(bf16)
    act_back = jnp.einsum("sd,fd->sf", back_rows, shrink_full, preferred_element_type=f32)
    pre_back = jax.vjp(gelu_value, hidden_pre)[1](act_back)[0].astype(bf16)
    expand_bias_grad = jnp.sum(pre_back, axis=0, dtype=f32)
    proj_back, qkv_bias_grad = attend_back_call(
        me, qkv_low, attended_back.reshape(lead + (2, rows, width)), lse, cosine, sine, doc_col, doc_row
    )
    proj_back = proj_back.reshape(tokens, 3 * width)
    qkv_bias_grad = jnp.sum(qkv_bias_grad, axis=(0, 1)).reshape(3, width)

    expand_sum = scatter_weight(
        lambda i: jnp.einsum("sd,sf->df", normed[:, halves[i]], pre_back, preferred_element_type=f32), 1, 0
    )

    def normed_back(start, stop):
        return jnp.einsum("se,de->sd", proj_back[start:stop], qkv_wide, preferred_element_type=f32) + jnp.einsum(
            "sf,df->sd", pre_back[start:stop], expand_full, preferred_element_type=f32
        )

    keep, recv = scatter_tokens(normed_back)
    input_grad, gain_shift = norm_back_call(order, me, inputs, cotangent, keep, recv, params[0:1])
    qkv_sum = scatter_weight(
        lambda i: jnp.einsum(
            "sd,se->de", normed[:, halves[i]], proj_back, preferred_element_type=f32
        ).reshape(D // 2, 3, width),
        2,
        0,
    )
    qkv_sum = jnp.transpose(qkv_sum, (1, 0, 2))

    qkv_rows = lax.dynamic_update_slice_in_dim(jnp.zeros((3, D), f32), qkv_bias_grad, head_start, 1)
    expand_rows = lax.dynamic_update_slice_in_dim(
        jnp.zeros((FF,), f32), expand_bias_grad, hidden_start, 0
    ).reshape(FF // D, D)
    params_grad = jnp.concatenate([gain_shift, qkv_rows, back_sum, back_sum, expand_rows], axis=0)
    part = params_grad
    for bit in reversed(range(dbits)):
        half = part.shape[1] // 2
        mine = (d_me >> bit) & 1
        send = lax.dynamic_slice_in_dim(part, (1 - mine) * half, half, 1)
        part = lax.dynamic_slice_in_dim(part, mine * half, half, 1) + exchange(send, "dp", bit)
    for bit in range(tbits):
        part = part + exchange(part, "tensor", bit)

    qkv_new = adam_update(qkv_weight, qkv_first, qkv_second, qkv_sum, matrix_rate, weight_decay)
    dense_new = adam_update(dense_weight, dense_first, dense_second, dense_sum, matrix_rate, weight_decay)
    expand_new = adam_update(expand_weight, expand_first, expand_second, expand_sum, matrix_rate, weight_decay)
    shrink_new = adam_update(shrink_weight, shrink_first, shrink_second, shrink_sum, matrix_rate, weight_decay)
    small_new = adam_update(small_params, small_first, small_second, part, vector_rate, 0.0)
    return (output, input_grad) + qkv_new + dense_new + expand_new + shrink_new + small_new


def solution(mesh):
    token_spec = P(("dp", "tensor"), None)
    qkv_spec = P(None, "dp", "tensor")
    row_spec = P("tensor", "dp")
    column_spec = P("dp", "tensor")
    small_spec = P(None, "dp")
    weight_specs = (qkv_spec,) * 3 + (row_spec,) * 3 + (column_spec,) * 3 + (row_spec,) * 3 + (small_spec,) * 3
    return jax.shard_map(
        per_device,
        mesh=mesh,
        in_specs=(token_spec, P("dp", "tensor"), token_spec) + weight_specs,
        out_specs=(token_spec, token_spec) + weight_specs,
        check_vma=False,
    )
```

time: 1730 us -> 828 us (0.48)
  waiting for transfers between devices: 1230 us -> 362 us
  matrix products: 241 us -> 148 us
  starting transfers between devices: 0.54 us -> 68.7 us
  Pallas kernels: 0 us -> 66.3 us
  blocking collectives: 48.2 us -> 0 us
  other arithmetic: 86.5 us -> 60.8 us
  local copies, waits for them, and re-layouts: 86.6 us -> 110 us
    reduce_scatter x7 -> x0, waiting for transfers between devices: 957 us -> none  [the longest x1 284 us: per_device(): lax.psum_scatter(shrink_grad, 'dp', scatter_dimension=1, tiled=True)]
    ppermute x0 -> x71, waiting for transfers between devices: none -> 362 us  [exchange(): return lax.ppermute(values, axis, [(i, i ^ 1 << bit) for i in range(count)])]
    all_gather x6 -> x0, waiting for transfers between devices: 272 us -> none  [the longest x1 103 us: per_device(): lax.all_gather(expand_low, 'dp', axis=0, tiled=True)]
    dot_general x26 -> x20, matrix products: 241 us -> 148 us  [the longest x1 22.6 us: per_device(): jnp.einsum('sd,fd->sf', back_rows, shrink_full, preferred_element_type=f32)]
    ppermute x0 -> x71, starting transfers between devices: none -> 68.7 us  [exchange(): return lax.ppermute(values, axis, [(i, i ^ 1 << bit) for i in range(count)])]
    pallas_call x0 -> x5, Pallas kernels: none -> 66.3 us  [the longest x1 29.6 us: attend_back_call(): pl.pallas_call(functools.partial(attend_back_kernel, tbits, width), grid=...]
    unnamed x85 -> x184, local copies, waits for them, and re-layouts: 22.2 us -> 76.1 us
    dynamic_update_slice x6 -> x2, local copies, waits for them, and re-layouts: 44.1 us -> 0.56 us  [the longest x1 0.56 us: per_device(): lax.dynamic_update_slice_in_dim(jnp.zeros((FF,), f32), expand_bias_grad,...]
  transfers between devices with their start and end apart: 13 -> 71, of which waited for: 11 -> 29; matrix products, arithmetic and copies ran while one was open for 20% -> 31% of each run, Pallas kernels for 0% -> 5%
where the time goes in v1:
time: 828 us; the launch traced here: 818 us
  waiting for transfers between devices  362 us (44%)
  matrix products  148 us (18%)
  local copies, waits for them, and re-layouts  110 us (13%)
  starting transfers between devices  68.7 us (8%)
  Pallas kernels  66.3 us (8%)
  other arithmetic  60.8 us (7%)
    ppermute x71, waiting for transfers between devices, exchange(): return lax.ppermute(values, axis, [(i, i ^ 1 << bit) for i in range(count)])  362 us
    unnamed x184, local copies, waits for them, and re-layouts  76.1 us
    ppermute x71, starting transfers between devices, exchange(): return lax.ppermute(values, axis, [(i, i ^ 1 << bit) for i in range(count)])  68.7 us
    pallas_call x1, Pallas kernels, attend_back_call(): pl.pallas_call(functools.partial(attend_back_kernel, tbits, width), grid=...  29.6 us
    pallas_call x1, Pallas kernels, attend_call(): pl.pallas_call(functools.partial(attend_kernel, tbits, width), grid=(seqs...  28.4 us
    convert_element_type x2, other arithmetic, scatter_tokens(): part = (partial(0, half) + recv.astype(f32)).astype(bf16)  23.2 us
    dot_general x1, matrix products, per_device(): jnp.einsum('sd,fd->sf', back_rows, shrink_full, preferred_element_type=f32)  22.6 us
    dot_general x2, matrix products, normed_back(): jnp.einsum('sf,df->sd', pre_back[start:stop], expand_full, preferred_elem...  17.7 us
  transfers between devices with their start and end apart: 71, of which 29 were waited for; matrix products, arithmetic and copies ran while one was open for 31% of the time, Pallas kernels for 5%

profile of v1, /device:TPU:0, one launch (start us, length us, event | category | flops | bytes accessed | tf_op | source)
XLA Modules:
  0.0 818.5 jit_solution(17813118774173750883)
XLA Ops:
  20.1 8.7 %collective-permute-done.17 = s32[1,256]{1,0:T(1,128)S(1)} collective-permute-done((s32[1,256]{1,0:T(1,128)S(1)}, s32[1,256]{1,0:T(1,128)S(1)}, u32[]{:S(2)}, u32[]{:S(2)}) %collective-permute-start.17) | collective-permute-done | bytes 1056 | tf_op jit(solution)/shard_map/ppermute | solution.py:33
  80.7 29.5 %collective-permute-done.28 = bf16[256,1024]{1,0:T(8,128)(2,1)} collective-permute-done((bf16[256,1024]{1,0:T(8,128)(2,1)}, bf16[256,1024]{1,0:T(8,128)(2,1)}, u32[]{:S(2)}, u32[]{:S(2)}) %collective-permute-start.28) | collective-permute-done | bytes 524320 | tf_op jit(solution)/shard_map/ppermute | solution.py:33
  116.1 16.6 %collective-permute-done.35 = bf16[1024,256]{1,0:T(8,128)(2,1)} collective-permute-done((bf16[1024,256]{1,0:T(8,128)(2,1)}, bf16[1024,256]{1,0:T(8,128)(2,1)}, u32[]{:S(2)}, u32[]{:S(2)}) %collective-permute-start.35) | collective-permute-done | bytes 524320 | tf_op jit(solution)/shard_map/ppermute | solution.py:33
  136.7 15.6 %collective-permute-done.12 = bf16[3,256,256]{1,2,0:T(8,128)(2,1)S(1)} collective-permute-done((bf16[3,256,256]{1,2,0:T(8,128)(2,1)}, bf16[3,256,256]{1,2,0:T(8,128)(2,1)S(1)}, u32[]{:S(2)}, u32[]{:S(2)}) %collective-permute-start.12) | collective-permute-done | bytes 393248 | tf_op jit(solution)/shard_map/ppermute | solution.py:33
  169.9 8.7 %collective-permute-done.32 = bf16[256,1024]{1,0:T(8,128)(2,1)S(1)} collective-permute-done((bf16[256,1024]{1,0:T(8,128)(2,1)}, bf16[256,1024]{1,0:T(8,128)(2,1)S(1)}, u32[]{:S(2)}, u32[]{:S(2)}) %collective-permute-start.32) | collective-permute-done | bytes 524320 | tf_op jit(solution)/shard_map/ppermute | solution.py:33
  181.9 7.9 collective-permute-done.38
  204.8 13.9 %collective-permute-done.44 = bf16[256,2048]{1,0:T(8,128)(2,1)S(1)} collective-permute-done((bf16[256,2048]{1,0:T(8,128)(2,1)S(1)}, bf16[256,2048]{1,0:T(8,128)(2,1)S(1)}, u32[]{:S(2)}, u32[]{:S(2)}) %collective-permute-start.44) | collective-permute-done | bytes 1048608 | tf_op jit(solution)/shard_map/ppermute | solution.py:33
  223.1 9.9 %collective-permute-done.40 = bf16[1024,256]{1,0:T(8,128)(2,1)S(1)} collective-permute-done((bf16[1024,256]{1,0:T(8,128)(2,1)S(1)}, bf16[1024,256]{1,0:T(8,128)(2,1)S(1)}, u32[]{:S(2)}, u32[]{:S(2)}) %collective-permute-start.40) | collective-permute-done | bytes 524320 | tf_op jit(solution)/shard_map/ppermute | solution.py:33
  242.0 13.1 %collective-permute-done.46 = bf16[256,2048]{1,0:T(8,128)(2,1)S(1)} collective-permute-done((bf16[256,2048]{1,0:T(8,128)(2,1)S(1)}, bf16[256,2048]{1,0:T(8,128)(2,1)S(1)}, u32[]{:S(2)}, u32[]{:S(2)}) %collective-permute-start.46) | collective-permute-done | bytes 1048608 | tf_op jit(solution)/shard_map/ppermute | solution.py:33
  258.9 13.5 %fusion.87 = f32[2048,1024]{1,0:T(8,128)} fusion(bf16[2048,2048]{1,0:T(8,128)(2,1)} %constant_dynamic-update-slice_fusion, bf16[2048,1024]{1,0:T(8,128)(2,1)S(1)} %constant_dynamic-update-slice_fusion.24), kind=kOutput, calls=%fused_computation.197 | convolution fusion | flops 8589934592 | bytes 20971520 | tf_op jit(solution)/shard_map/dot_general | solution.py:518
  272.4 22.6 %convert_reduce_fusion = (f32[1024]{0:T(1024)S(1)}, bf16[2048,1024]{1,0:T(8,128)(2,1)}, bf16[2048,1024]{1,0:T(8,128)(2,1)}) fusion(f32[2048,1024]{1,0:T(8,128)} %fusion.87, f32[1024]{0:T(1024)S(1)} %dynamic_slice.55, bf16[2048,2048]{1,0:T(8,128)(2,1)S(1)} %constant_dynamic-update-slice_fusion.40, bf16[1024,2048]{1,0:T(8,128)(2,1)} %constant_dynamic-update-slice_fusion.32), kind=kOutput, calls=%fused_computation.9 | convolution fusion | flops 8642362368 | bytes 29368320 | tf_op jit(solution)/shard_map/sd,fd->sf/dot_general | solution.py:563
  295.0 10.8 %fusion.29 = f32[1024,2048]{1,0:T(8,128)} fusion(bf16[2048,1024]{1,0:T(8,128)(2,1)} %copy-done.43, bf16[2048,1024]{1,0:T(8,128)(2,1)} %get-tuple-element.147), kind=kOutput, calls=%fused_computation.49 | convolution fusion | flops 4294967296 | bytes 14680064 | tf_op jit(solution)/shard_map/sf,df->sd/dot_general | solution.py:577
  305.9 8.5 %fusion.37 = bf16[1024,1024]{0,1:T(8,128)(2,1)} fusion(bf16[2048,1024]{1,0:T(8,128)(2,1)S(1)} %copy-done.56, bf16[2048,2048]{1,0:T(8,128)(2,1)} %constant_dynamic-update-slice_fusion), kind=kOutput, calls=%fused_computation.61 | convolution fusion | flops 4296015872 | bytes 10485760 | tf_op jit(solution)/shard_map/sd,sf->df/dot_general | solution.py:573
  314.4 8.6 %broadcast_add_fusion = f32[2048,768]{1,0:T(8,128)} fusion(f32[768]{0:T(1024)S(1)} %add.222, bf16[2048,2048]{1,0:T(8,128)(2,1)S(1)} %copy-done.40, bf16[2048,768]{0,1:T(8,128)(2,1)S(1)} %bitcast.113), kind=kOutput, calls=%fused_computation.40 | convolution fusion | flops 6444023808 | bytes 17828864 | tf_op jit(solution)/shard_map/dot_general | solution.py:513
  323.0 28.4 %attend.1 = (bf16[2,2,2,256,256]{4,3,2,1,0:T(8,128)(2,1)S(1)}, bf16[2,1024,768]{2,1,0:T(8,128)(2,1)}, f32[2,4,1024]{2,1,0:T(4,128)S(1)}) custom-call(s32[2]{0:T(128)S(1)} %pad_add_fusion.3.me_ref, f32[2,2,2,256,768]{4,3,2,1,0:T(8,128)} %bitcast.97, f32[2,1024,128]{2,1,0:T(8,128)S(1)} %concatenate.95.cos_ref, f32[2,1024,128]{2,1,0:T(8,128)S(1)} %concatenate.96.sin_ref, ...), custom_call_target="tpu_custom_call" | custom-call | tf_op jit(solution)/shard_map/attend/pallas_call | solution.py:272
  409.2 82.8 %collective-permute-done.23 = bf16[256,256]{1,0:T(8,128)(2,1)S(1)} collective-permute-done((bf16[256,256]{1,0:T(8,128)(2,1)S(1)}, bf16[256,256]{1,0:T(8,128)(2,1)S(1)}, u32[]{:S(2)}, u32[]{:S(2)}) %collective-permute-start.23) | collective-permute-done | bytes 131104 | tf_op jit(solution)/shard_map/ppermute | solution.py:33
  505.4 29.6 %attend_back.1 = (bf16[2,2,2,256,768]{4,3,2,1,0:T(8,128)(2,1)}, f32[2,1,768]{2,1,0:T(1,128)S(1)}) custom-call(s32[2]{0:T(128)S(1)} %pad_add_fusion.3.me_ref, bf16[2,1024,768]{2,1,0:T(8,128)(2,1)} %get-tuple-element.32.qkv_ref, bf16[2,2,2,256,256]{4,3,2,1,0:T(8,128)(2,1)S(1)} %bitcast.89, f32[2,4,1024]{2,1,0:T(4,128)S(1)} %get-tuple-element.35.lse_ref, ...), custom_call_target="tpu_custom_call" | custom-call | tf_op jit(solution)/shard_map/attend_back/pallas_call | solution.py:375
  590.5 56.8 %collective-permute-done.64 = bf16[1024,512]{1,0:T(8,128)(2,1)S(1)} collective-permute-done((bf16[1024,512]{1,0:T(8,128)(2,1)S(1)}, bf16[1024,512]{1,0:T(8,128)(2,1)S(1)}, u32[]{:S(2)}, u32[]{:S(2)}) %collective-permute-start.64) | collective-permute-done | bytes 1048608 | tf_op jit(solution)/shard_map/ppermute | solution.py:33
  648.6 20.7 %collective-permute-done.61 = bf16[512,1024]{0,1:T(8,128)(2,1)S(1)} collective-permute-done((bf16[512,1024]{0,1:T(8,128)(2,1)S(1)}, bf16[512,1024]{0,1:T(8,128)(2,1)S(1)}, u32[]{:S(2)}, u32[]{:S(2)}) %collective-permute-start.61) | collective-permute-done | bytes 1048608 | tf_op jit(solution)/shard_map/ppermute | solution.py:33
  670.5 11.6 %add_convert_fusion = bf16[1024,2048]{1,0:T(8,128)(2,1)} fusion(bf16[1024,2048]{1,0:T(8,128)(2,1)} %collective-permute-done.51, f32[1024,2048]{1,0:T(8,128)} %fusion.88, f32[1024,2048]{1,0:T(8,128)} %fusion.31), kind=kLoop, calls=%fused_computation.10 | loop fusion | flops 8388608 | bytes 25165824 | tf_op jit(solution)/shard_map/convert_element_type | solution.py:524
  700.8 11.6 %add_convert_fusion.2 = bf16[1024,2048]{1,0:T(8,128)(2,1)} fusion(bf16[1024,2048]{1,0:T(8,128)(2,1)} %collective-permute-done.41, f32[1024,2048]{1,0:T(8,128)} %fusion.86, f32[1024,2048]{1,0:T(8,128)} %fusion.35), kind=kLoop, calls=%fused_computation.12 | loop fusion | flops 8388608 | bytes 25165824 | tf_op jit(solution)/shard_map/convert_element_type | solution.py:524
  716.2 18.1 %collective-permute-done.52 = bf16[512,2048]{1,0:T(8,128)(2,1)} collective-permute-done((bf16[512,2048]{1,0:T(8,128)(2,1)}, bf16[512,2048]{1,0:T(8,128)(2,1)}, u32[]{:S(2)}, u32[]{:S(2)}) %collective-permute-start.52) | collective-permute-done | bytes 2097184 | tf_op jit(solution)/shard_map/ppermute | solution.py:33
  745.1 18.6 %collective-permute-done.53.recv_ref = bf16[256,2048]{1,0:T(8,128)(2,1)S(1)} collective-permute-done((bf16[256,2048]{1,0:T(8,128)(2,1)S(1)}, bf16[256,2048]{1,0:T(8,128)(2,1)S(1)}, u32[]{:S(2)}, u32[]{:S(2)}) %collective-permute-start.53) | collective-permute-done | bytes 1048608 | tf_op jit(solution)/shard_map/ppermute | solution.py:33
  769.5 8.0 collective-permute-done.42
  (428 shorter events, 341.9 us)
Async XLA Ops:
  3.9 70.8 %collective-permute-start.11 = (bf16[3,256,256]{1,2,0:T(8,128)(2,1)}, bf16[3,256,256]{1,2,0:T(8,128)(2,1)}, u32[]{:S(2)}, u32[]{:S(2)}) collective-permute-start(bf16[3,256,256]{1,2,0:T(8,128)(2,1)} %get-tuple-element.163), channel_id=1, source_target_pairs={{0,16},{4,20},{8,24},{12,28},{16,0},{20,4},{24,8},{28,12},{1,17},{... | collective-permute-start | bytes 1179656 | tf_op jit(solution)/shard_map/ppermute | solution.py:33
  7.9 66.8 %collective-permute-start.13 = (bf16[3,256,256]{1,2,0:T(8,128)(2,1)}, bf16[3,256,256]{1,2,0:T(8,128)(2,1)}, u32[]{:S(2)}, u32[]{:S(2)}) collective-permute-start(bf16[3,256,256]{1,2,0:T(8,128)(2,1)} %get-tuple-element.163), channel_id=1, source_target_pairs={{0,4},{4,0},{8,12},{12,8},{16,20},{20,16},{24,28},{28,24},{1,5},{5... | collective-permute-start | bytes 1179656 | tf_op jit(solution)/shard_map/ppermute | solution.py:33
  11.1 62.0 %collective-permute-start.10 = (bf16[3,256,256]{1,2,0:T(8,128)(2,1)}, bf16[3,256,256]{1,2,0:T(8,128)(2,1)}, u32[]{:S(2)}, u32[]{:S(2)}) collective-permute-start(bf16[3,256,256]{1,2,0:T(8,128)(2,1)} %get-tuple-element.185), channel_id=1, source_target_pairs={{0,8},{4,12},{8,0},{12,4},{16,24},{20,28},{24,16},{28,20},{1,9},{5... | collective-permute-start | bytes 1179656 | tf_op jit(solution)/shard_map/ppermute | solution.py:33
  63.2 47.0 %collective-permute-start.28 = (bf16[256,1024]{1,0:T(8,128)(2,1)}, bf16[256,1024]{1,0:T(8,128)(2,1)}, u32[]{:S(2)}, u32[]{:S(2)}) collective-permute-start(bf16[256,1024]{1,0:T(8,128)(2,1)} %get-tuple-element.165), channel_id=1, source_target_pairs={{0,16},{4,20},{8,24},{12,28},{16,0},{20,4},{24,8},{28,12},{1,17},{... | collective-permute-start | bytes 1572872 | tf_op jit(solution)/shard_map/ppermute | solution.py:33
  74.7 58.0 %collective-permute-start.35 = (bf16[1024,256]{1,0:T(8,128)(2,1)}, bf16[1024,256]{1,0:T(8,128)(2,1)}, u32[]{:S(2)}, u32[]{:S(2)}) collective-permute-start(bf16[1024,256]{1,0:T(8,128)(2,1)} %get-tuple-element.167), channel_id=1, source_target_pairs={{0,16},{4,20},{8,24},{12,28},{16,0},{20,4},{24,8},{28,12},{1,17},{... | collective-permute-start | bytes 1572872 | tf_op jit(solution)/shard_map/ppermute | solution.py:33
  80.4 74.4 %collective-permute-start.37 = (bf16[1024,256]{1,0:T(8,128)(2,1)}, bf16[1024,256]{1,0:T(8,128)(2,1)S(1)}, u32[]{:S(2)}, u32[]{:S(2)}) collective-permute-start(bf16[1024,256]{1,0:T(8,128)(2,1)} %get-tuple-element.167), channel_id=1, source_target_pairs={{0,4},{4,0},{8,12},{12,8},{16,20},{20,16},{24,28},{28,24},{1,5},{5... | collective-permute-start | bytes 1572872 | tf_op jit(solution)/shard_map/ppermute | solution.py:33
  110.2 42.0 %collective-permute-start.12 = (bf16[3,256,256]{1,2,0:T(8,128)(2,1)}, bf16[3,256,256]{1,2,0:T(8,128)(2,1)S(1)}, u32[]{:S(2)}, u32[]{:S(2)}) collective-permute-start(bf16[3,256,256]{1,2,0:T(8,128)(2,1)} %collective-permute-done.10), channel_id=1, source_target_pairs={{0,16},{4,20},{8,24},{12,28},{16,0},{20,4},{24,8},{28,12},{1,17},{... | collective-permute-start | bytes 1179656 | tf_op jit(solution)/shard_map/ppermute | solution.py:33
  114.1 43.2 %collective-permute-start.14 = (bf16[3,256,256]{1,2,0:T(8,128)(2,1)}, bf16[3,256,256]{1,2,0:T(8,128)(2,1)S(1)}, u32[]{:S(2)}, u32[]{:S(2)}) collective-permute-start(bf16[3,256,256]{1,2,0:T(8,128)(2,1)} %collective-permute-done.10), channel_id=1, source_target_pairs={{0,4},{4,0},{8,12},{12,8},{16,20},{20,16},{24,28},{28,24},{1,5},{5... | collective-permute-start | bytes 1179656 | tf_op jit(solution)/shard_map/ppermute | solution.py:33
  115.8 41.4 %collective-permute-start.15 = (bf16[3,256,256]{1,2,0:T(8,128)(2,1)}, bf16[3,256,256]{1,2,0:T(8,128)(2,1)S(1)}, u32[]{:S(2)}, u32[]{:S(2)}) collective-permute-start(bf16[3,256,256]{1,2,0:T(8,128)(2,1)} %collective-permute-done.11), channel_id=1, source_target_pairs={{0,4},{4,0},{8,12},{12,8},{16,20},{20,16},{24,28},{28,24},{1,5},{5... | collective-permute-start | bytes 1179656 | tf_op jit(solution)/shard_map/ppermute | solution.py:33
  395.5 172.4 %collective-permute-start.63 = (bf16[1024,1024]{1,0:T(8,128)(2,1)}, bf16[1024,1024]{1,0:T(8,128)(2,1)}, u32[]{:S(2)}, u32[]{:S(2)}) collective-permute-start(bf16[1024,1024]{1,0:T(8,128)(2,1)} %fusion.40), channel_id=1, source_target_pairs={{0,4},{4,0},{8,12},{12,8},{16,20},{20,16},{24,28},{28,24},{1,5},{5... | collective-permute-start | bytes 6291464 | tf_op jit(solution)/shard_map/ppermute | solution.py:33
  396.7 180.6 %collective-permute-start.60 = (bf16[1024,1024]{0,1:T(8,128)(2,1)}, bf16[1024,1024]{0,1:T(8,128)(2,1)}, u32[]{:S(2)}, u32[]{:S(2)}) collective-permute-start(bf16[1024,1024]{0,1:T(8,128)(2,1)} %fusion.37), channel_id=1, source_target_pairs={{0,4},{4,0},{8,12},{12,8},{16,20},{20,16},{24,28},{28,24},{1,5},{5... | collective-permute-start | bytes 6291464 | tf_op jit(solution)/shard_map/ppermute | solution.py:33
  397.6 94.5 %collective-permute-start.23 = (bf16[256,256]{1,0:T(8,128)(2,1)S(1)}, bf16[256,256]{1,0:T(8,128)(2,1)S(1)}, u32[]{:S(2)}, u32[]{:S(2)}) collective-permute-start(bf16[256,256]{1,0:T(8,128)(2,1)S(1)} %get-tuple-element.161), channel_id=1, source_target_pairs={{0,4},{4,0},{8,12},{12,8},{16,20},{20,16},{24,28},{28,24},{1,5},{5... | collective-permute-start | bytes 393224 | tf_op jit(solution)/shard_map/ppermute | solution.py:33
  404.1 90.8 %collective-permute-start.24 = (bf16[256,256]{1,0:T(8,128)(2,1)}, bf16[256,256]{1,0:T(8,128)(2,1)S(1)}, u32[]{:S(2)}, u32[]{:S(2)}) collective-permute-start(bf16[256,256]{1,0:T(8,128)(2,1)} %collective-permute-done.20), channel_id=1, source_target_pairs={{0,4},{4,0},{8,12},{12,8},{16,20},{20,16},{24,28},{28,24},{1,5},{5... | collective-permute-start | bytes 393224 | tf_op jit(solution)/shard_map/ppermute | solution.py:33
  407.5 89.8 %collective-permute-start.25 = (bf16[256,256]{1,0:T(8,128)(2,1)}, bf16[256,256]{1,0:T(8,128)(2,1)S(1)}, u32[]{:S(2)}, u32[]{:S(2)}) collective-permute-start(bf16[256,256]{1,0:T(8,128)(2,1)} %collective-permute-done.21), channel_id=1, source_target_pairs={{0,4},{4,0},{8,12},{12,8},{16,20},{20,16},{24,28},{28,24},{1,5},{5... | collective-permute-start | bytes 393224 | tf_op jit(solution)/shard_map/ppermute | solution.py:33
  545.0 125.5 %collective-permute-start.51 = (bf16[1024,2048]{1,0:T(8,128)(2,1)}, bf16[1024,2048]{1,0:T(8,128)(2,1)}, u32[]{:S(2)}, u32[]{:S(2)}) collective-permute-start(bf16[1024,2048]{1,0:T(8,128)(2,1)} %add_convert_fusion.1), channel_id=1, source_target_pairs={{0,1},{1,0},{2,3},{3,2},{4,5},{5,4},{6,7},{7,6},{8,9},{9,8},{10,11... | collective-permute-start | bytes 12582920 | tf_op jit(solution)/shard_map/ppermute | solution.py:33
  557.8 129.3 %collective-permute-start.54 = (bf16[1024,3,256]{0,2,1:T(8,128)(2,1)}, bf16[1024,3,256]{0,2,1:T(8,128)(2,1)}, u32[]{:S(2)}, u32[]{:S(2)}) collective-permute-start(bf16[1024,3,256]{0,2,1:T(8,128)(2,1)} %fusion.45), channel_id=1, source_target_pairs={{0,4},{4,0},{8,12},{12,8},{16,20},{20,16},{24,28},{28,24},{1,5},{5... | collective-permute-start | bytes 4718600 | tf_op jit(solution)/shard_map/ppermute | solution.py:33
  562.2 138.6 %collective-permute-start.41 = (bf16[1024,2048]{1,0:T(8,128)(2,1)}, bf16[1024,2048]{1,0:T(8,128)(2,1)}, u32[]{:S(2)}, u32[]{:S(2)}) collective-permute-start(bf16[1024,2048]{1,0:T(8,128)(2,1)} %add_convert_fusion.3), channel_id=1, source_target_pairs={{0,1},{1,0},{2,3},{3,2},{4,5},{5,4},{6,7},{7,6},{8,9},{9,8},{10,11... | collective-permute-start | bytes 12582920 | tf_op jit(solution)/shard_map/ppermute | solution.py:33
  575.4 71.9 %collective-permute-start.64 = (bf16[1024,512]{1,0:T(8,128)(2,1)S(1)}, bf16[1024,512]{1,0:T(8,128)(2,1)S(1)}, u32[]{:S(2)}, u32[]{:S(2)}) collective-permute-start(bf16[1024,512]{1,0:T(8,128)(2,1)S(1)} %slice.256), channel_id=1, source_target_pairs={{0,16},{4,20},{8,24},{12,28},{16,0},{20,4},{24,8},{28,12},{1,17},{... | collective-permute-start | bytes 3145736 | tf_op jit(solution)/shard_map/ppermute | solution.py:33
  583.5 85.7 %collective-permute-start.61 = (bf16[512,1024]{0,1:T(8,128)(2,1)S(1)}, bf16[512,1024]{0,1:T(8,128)(2,1)S(1)}, u32[]{:S(2)}, u32[]{:S(2)}) collective-permute-start(bf16[512,1024]{0,1:T(8,128)(2,1)S(1)} %slice.252), channel_id=1, source_target_pairs={{0,16},{4,20},{8,24},{12,28},{16,0},{20,4},{24,8},{28,12},{1,17},{... | collective-permute-start | bytes 3145736 | tf_op jit(solution)/shard_map/ppermute | solution.py:33
  648.6 48.0 %collective-permute-start.65 = (bf16[1024,256]{1,0:T(8,128)(2,1)}, bf16[1024,256]{1,0:T(8,128)(2,1)}, u32[]{:S(2)}, u32[]{:S(2)}) collective-permute-start(bf16[1024,256]{1,0:T(8,128)(2,1)} %slice.258), channel_id=1, source_target_pairs={{0,8},{4,12},{8,0},{12,4},{16,24},{20,28},{24,16},{28,20},{1,9},{5... | collective-permute-start | bytes 1572872 | tf_op jit(solution)/shard_map/ppermute | solution.py:33
  685.4 48.9 %collective-permute-start.52 = (bf16[512,2048]{1,0:T(8,128)(2,1)}, bf16[512,2048]{1,0:T(8,128)(2,1)}, u32[]{:S(2)}, u32[]{:S(2)}) collective-permute-start(bf16[512,2048]{1,0:T(8,128)(2,1)} %slice.236), channel_id=1, source_target_pairs={{0,2},{1,3},{2,0},{3,1},{4,6},{5,7},{6,4},{7,5},{8,10},{9,11},{10,... | collective-permute-start | bytes 6291464 | tf_op jit(solution)/shard_map/ppermute | solution.py:33
  694.4 48.4 %collective-permute-start.55 = (bf16[512,3,256]{0,2,1:T(8,128)(2,1)}, bf16[512,3,256]{0,2,1:T(8,128)(2,1)}, u32[]{:S(2)}, u32[]{:S(2)}) collective-permute-start(bf16[512,3,256]{0,2,1:T(8,128)(2,1)} %slice.242), channel_id=1, source_target_pairs={{0,16},{4,20},{8,24},{12,28},{16,0},{20,4},{24,8},{28,12},{1,17},{... | collective-permute-start | bytes 2359304 | tf_op jit(solution)/shard_map/ppermute | solution.py:33
  715.7 61.8 %collective-permute-start.42 = (bf16[512,2048]{1,0:T(8,128)(2,1)}, bf16[512,2048]{1,0:T(8,128)(2,1)S(1)}, u32[]{:S(2)}, u32[]{:S(2)}) collective-permute-start(bf16[512,2048]{1,0:T(8,128)(2,1)} %slice.229), channel_id=1, source_target_pairs={{0,2},{1,3},{2,0},{3,1},{4,6},{5,7},{6,4},{7,5},{8,10},{9,11},{10,... | collective-permute-start | bytes 6291464 | tf_op jit(solution)/shard_map/ppermute | solution.py:33
  745.1 52.9 %collective-permute-start.56 = (bf16[256,3,256]{0,2,1:T(8,128)(2,1)}, bf16[256,3,256]{0,2,1:T(8,128)(2,1)}, u32[]{:S(2)}, u32[]{:S(2)}) collective-permute-start(bf16[256,3,256]{0,2,1:T(8,128)(2,1)} %slice.244), channel_id=1, source_target_pairs={{0,8},{4,12},{8,0},{12,4},{16,24},{20,28},{24,16},{28,20},{1,9},{5... | collective-permute-start | bytes 1179656 | tf_op jit(solution)/shard_map/ppermute | solution.py:33
  (112 other events, 2063.4 us)

commit v2 on v1

v2 whole, which is shorter than its diff:
```python
import functools
import jax
import jax.numpy as jnp
from jax import lax
from jax.experimental import pallas as pl
from jax.experimental.pallas import tpu as pltpu
from jax.sharding import PartitionSpec as P

D = 2048
HD = 64
ROT = 32
FF = 8192
STEP = 10

norm_eps = 1e-05
beta_first = 0.9
beta_second = 0.95
adam_eps = 1e-08
weight_decay = 0.1
matrix_rate = 0.05
vector_rate = 1.0
masked_score = -1e30

SUB_BIT = 1
ROW_BIT = 0

bf16 = jnp.bfloat16
f32 = jnp.float32


def exchange(values, axis, bit):
    count = lax.axis_size(axis)
    return lax.ppermute(values, axis, [(i, i ^ (1 << bit)) for i in range(count)])


def place_order(count):
    bits = count.bit_length() - 1
    order = []
    for p in range(count):
        high = (p >> 1) & ((1 << (bits - 2)) - 1)
        order.append(((p & 1) << SUB_BIT) | (high << 2) | ((p >> (bits - 1)) << ROW_BIT))
    return order


def adam_update(weight, first, second, grad, rate, decay):
    first_new = beta_first * first + (1.0 - beta_first) * grad
    second_new = beta_second * second + (1.0 - beta_second) * grad * grad
    first_hat = first_new / (1.0 - beta_first**STEP)
    second_hat = second_new / (1.0 - beta_second**STEP)
    weight_new = weight - rate * (first_hat / (jnp.sqrt(second_hat) + adam_eps) + decay * weight)
    return (weight_new, first_new, second_new)


def after(values, *others):
    return lax.optimization_barrier((values,) + others)[0]


def gelu_value(pre_values):
    return jax.nn.gelu(pre_values, approximate=True)


def vmem_params(mib):
    return pltpu.CompilerParams(vmem_limit_bytes=mib * 2**20)


def place_of(block, count):
    bits = count.bit_length() - 1
    return ((block >> SUB_BIT) & 1) | ((block >> 2) << 1) | (((block >> ROW_BIT) & 1) << (bits - 1))


def move_blocks(count, source, load, store):
    width = D // count
    if width % 128 == 0:
        for j in range(count):
            start = pl.multiple_of(source(j) * width, width)
            store(pl.ds(j * width, width), load(pl.ds(start, width)))
        return
    for unit in range(count // 2):
        parts = []
        for half in range(2):
            block = source(2 * unit + half)
            value = load(pl.ds(pl.multiple_of((block >> 1) * 128, 128), 128))
            parts.append(pltpu.roll(value, ((block & 1) ^ half) * 64, 1))
        lane = lax.broadcasted_iota(jnp.int32, parts[0].shape, 1)
        store(pl.ds(unit * 128, 128), jnp.where(lane < 64, parts[0], parts[1]))


def smem_spec():
    return pl.BlockSpec(memory_space=pltpu.SMEM)


def assemble(order, me, keep_ref, recv_ref, tmp):
    count = len(order)

    def store(lanes, value):
        tmp[:, lanes] = value

    def add(lanes, value):
        tmp[:, lanes] += value

    move_blocks(count, lambda j: place_of(j ^ me, count), lambda lanes: keep_ref[:, lanes].astype(f32), store)
    move_blocks(count, lambda j: place_of(j ^ me, count) ^ 1, lambda lanes: recv_ref[:, lanes].astype(f32), add)


def out_kernel(order, me_ref, x_ref, keep_ref, recv_ref, b_ref, o_ref, tmp):
    assemble(order, me_ref[0], keep_ref, recv_ref, tmp)
    o_ref[...] = (x_ref[...].astype(f32) + tmp[...] + b_ref[0:1] + b_ref[1:2]).astype(bf16)


def out_call(order, me, x, keep, recv, biases):
    vm = pl.BlockSpec(memory_space=pltpu.VMEM)
    return pl.pallas_call(
        functools.partial(out_kernel, order),
        out_shape=jax.ShapeDtypeStruct(x.shape, bf16),
        in_specs=[smem_spec(), vm, vm, vm, vm],
        out_specs=vm,
        scratch_shapes=[pltpu.VMEM(x.shape, f32)],
        compiler_params=vmem_params(32),
        name="block_output",
    )(me, x, keep, recv, biases)


def norm_back_kernel(order, me_ref, x_ref, dy_ref, keep_ref, recv_ref, g_ref, o_ref, sums_ref, tmp):
    assemble(order, me_ref[0], keep_ref, recv_ref, tmp)
    rows = x_ref[...].astype(f32)
    centered = rows - jnp.mean(rows, axis=-1, keepdims=True)
    inv = lax.rsqrt(jnp.mean(centered * centered, axis=-1, keepdims=True) + norm_eps)
    unit = centered * inv
    back = tmp[...]
    sums_ref[0:1] = jnp.sum(back * unit, axis=0, keepdims=True)
    sums_ref[1:2] = jnp.sum(back, axis=0, keepdims=True)
    e = back * g_ref[...]
    o_ref[...] = dy_ref[...].astype(f32) + inv * (
        e - jnp.mean(e, axis=-1, keepdims=True) - unit * jnp.mean(e * unit, axis=-1, keepdims=True)
    )


def norm_back_call(order, me, x, dy, keep, recv, gain):
    vm = pl.BlockSpec(memory_space=pltpu.VMEM)
    return pl.pallas_call(
        functools.partial(norm_back_kernel, order),
        out_shape=[jax.ShapeDtypeStruct(x.shape, f32), jax.ShapeDtypeStruct((2, D), f32)],
        in_specs=[smem_spec()] + [vm] * 5,
        out_specs=[vm, vm],
        scratch_shapes=[pltpu.VMEM(x.shape, f32)],
        compiler_params=vmem_params(40),
        name="norm_back",
    )(me, x, dy, keep, recv, gain)


def swap_rotary(values):
    lane = lax.broadcasted_iota(jnp.int32, values.shape, 1)
    half = ROT // 2
    return jnp.where(
        lane % ROT < half, pltpu.roll(values, 128 - half, 1), pltpu.roll(values, half, 1)
    )


def dot_nn(a, b):
    return lax.dot_general(a, b, (((1,), (0,)), ((), ())), preferred_element_type=f32)


def dot_nt(a, b):
    return lax.dot_general(a, b, (((1,), (1,)), ((), ())), preferred_element_type=f32)


def dot_tn(a, b):
    return lax.dot_general(a, b, (((0,), (0,)), ((), ())), preferred_element_type=f32)


def rel_index(rel, seq, tbits):
    index = seq
    for b in range(tbits):
        index = index | (((rel >> b) & 1) << (tbits - b))
    return index


def mask_bias(bias, start_row, qb, rows):
    kend = (qb + 1) * rows
    key = lax.broadcasted_iota(jnp.int32, (kend, rows), 0)
    query = lax.broadcasted_iota(jnp.int32, (kend, rows), 1) + qb * rows
    bias[:kend, :] = jnp.where((key >= start_row) & (key <= query), 0.0, masked_score)


def attend_rows(qkv, lse, bias, o, seq, qb, width, out_rows):
    rows = bias.shape[1]
    kend = (qb + 1) * rows
    place = slice(qb * rows, kend)
    lane = lax.broadcasted_iota(jnp.int32, (rows, 128), 1)
    zero = jnp.zeros((rows, 128), bf16)

    def pair_body(pair, carry):
        base = pl.multiple_of(pair * 128, 128)
        q = qkv[seq, place, pl.ds(base, 128)] * jnp.asarray(HD ** (-0.5), bf16)
        k = qkv[seq, :kend, pl.ds(base + width, 128)]
        v = qkv[seq, :kend, pl.ds(base + 2 * width, 128)]
        vt = v.T
        outs = []
        for h in range(2):
            mine = (lane < HD) if h == 0 else (lane >= HD)
            s = dot_nt(k, jnp.where(mine, q, zero)) + bias[:kend, :]
            peak = jnp.max(s, axis=0, keepdims=True)
            expo = jnp.exp(s - peak)
            total = jnp.sum(expo, axis=0, keepdims=True)
            weights = (expo * (1.0 / total)).astype(bf16)
            outs.append(dot_nn(vt[h * HD : (h + 1) * HD, :], weights))
            lse[seq, pl.ds(pair * 2 + h, 1), place] = peak + jnp.log(total)
        o[out_rows, pl.ds(base, 128)] = jnp.concatenate(outs, axis=0).T.astype(bf16)
        return carry

    lax.fori_loop(0, width // 128, pair_body, 0)


def attend_back_rows(qkv, lse, bias, do, cosb, sinb, dk, dv, dp, sums, seq, qb, width, out_rows):
    rows = bias.shape[1]
    kend = (qb + 1) * rows
    place = slice(qb * rows, kend)
    scale = HD ** (-0.5)
    lane = lax.broadcasted_iota(jnp.int32, (rows, 128), 1)
    zero = jnp.zeros((rows, 128), bf16)

    def pair_body(pair, carry):
        base = pl.multiple_of(pair * 128, 128)
        lanes = pl.ds(base, 128)
        q = qkv[seq, place, lanes]
        k = qkv[seq, :kend, pl.ds(base + width, 128)]
        v = qkv[seq, :kend, pl.ds(base + 2 * width, 128)]
        kt = k.T
        dout = do[out_rows, lanes]
        outs = []
        for h in range(2):
            mine = (lane < HD) if h == 0 else (lane >= HD)
            qm = jnp.where(mine, q, zero) * jnp.asarray(scale, bf16)
            dom = jnp.where(mine, dout, zero)
            s = dot_nt(k, qm) + bias[:kend, :]
            probs = jnp.exp(s - lse[seq, pl.ds(pair * 2 + h, 1), place])
            dprobs = dot_nt(v, dom)
            inner = jnp.sum(probs * dprobs, axis=0, keepdims=True)
            ds = (probs * (dprobs - inner)).astype(bf16)
            dv[:kend, lanes] += dot_nn(probs.astype(bf16), dom)
            dk[:kend, lanes] += dot_nn(ds, qm)
            outs.append(dot_nn(kt[h * HD : (h + 1) * HD, :], ds))
        dq = jnp.concatenate(outs, axis=0).T * scale
        dq = dq * cosb[seq, place, :] - swap_rotary(dq) * sinb[seq, place, :]
        dq = dq.astype(bf16)
        dp[out_rows, lanes] = dq
        sums[0:1, lanes] += jnp.sum(dq.astype(f32), axis=0, keepdims=True)
        return carry

    lax.fori_loop(0, width // 128, pair_body, 0)


def attend_back_keys(cosb, sinb, dk, dv, dp, sums, seq, b, width, out_rows):
    rows = out_rows.size
    place = slice(b * rows, (b + 1) * rows)
    cosine = cosb[seq, place, :]
    sine = sinb[seq, place, :]
    for j in range(width // 128):
        lanes = slice(j * 128, (j + 1) * 128)
        part = dk[place, lanes]
        part = (part * cosine - swap_rotary(part) * sine).astype(bf16)
        kl = slice(width + j * 128, width + (j + 1) * 128)
        dp[out_rows, kl] = part
        sums[0:1, kl] += jnp.sum(part.astype(f32), axis=0, keepdims=True)
        part = dv[place, lanes].astype(bf16)
        vl = slice(2 * width + j * 128, 2 * width + (j + 1) * 128)
        dp[out_rows, vl] = part
        sums[0:1, vl] += jnp.sum(part.astype(f32), axis=0, keepdims=True)


class Links:
    def __init__(self, send_sems, recv_sems, local_sems):
        self.send_sems, self.recv_sems, self.local_sems = send_sems, recv_sems, local_sems
        self.sent, self.count, self.locals = [], 0, 0

    def send(self, src, dst, axis, bit):
        partner = lax.axis_index(axis) ^ (1 << bit)
        i = self.count
        self.count += 1
        copy = pltpu.make_async_remote_copy(
            src_ref=src,
            dst_ref=dst,
            send_sem=self.send_sems.at[i],
            recv_sem=self.recv_sems.at[i],
            device_id={axis: partner},
            device_id_type=pl.DeviceIdType.MESH,
        )
        copy.start()
        self.sent.append(copy)
        return copy

    def local(self, src, dst):
        copy = pltpu.make_async_copy(src, dst, self.local_sems.at[self.locals])
        self.locals += 1
        copy.start()
        return copy

    def finish(self):
        for copy in self.sent:
            copy.wait_send()


def greet(dbits, tbits):
    barrier = pltpu.get_barrier_semaphore()
    partners = [("dp", b) for b in range(dbits)] + [("tensor", b) for b in range(tbits)]
    for axis, bit in partners:
        pl.semaphore_signal(
            barrier,
            inc=1,
            device_id={axis: lax.axis_index(axis) ^ (1 << bit)},
            device_id_type=pl.DeviceIdType.MESH,
        )
    pl.semaphore_wait(barrier, len(partners))


class Gathered:
    def __init__(self, links, slot, count, bits):
        self.links, self.slot, self.bits = links, slot, bits
        self.arrived = {0: None}
        self.steps = []
        size = 1
        for step, bit in enumerate(bits):
            self.steps.append((bit, size))
            size *= 2

    def push(self, p, first=0):
        for step in range(max(first, 1), len(self.steps)):
            bit, size = self.steps[step]
            if p < size:
                self.arrived[p + size] = self.links.send(self.slot(p), self.slot(p + size), "dp", bit)

    def start(self, outgoing):
        self.arrived[1] = self.links.send(outgoing, self.slot(1), "dp", self.bits[0])

    def take(self, p):
        self.arrived[p].wait_recv()
        self.push(p)


class GatheredPairs(Gathered):
    def __init__(self, links, slot, count, bits, own, received):
        super().__init__(links, slot, count, bits)
        self.own, self.received = own, received

    def push(self, p, first=0):
        if p % 2 == 0 and (p > 0 or first > 0):
            unit = p // 2
            for step in range(1, len(self.steps)):
                bit, size = self.steps[step]
                if p < size:
                    other = unit + size // 2
                    self.arrived[2 * other] = self.links.send(self.slot(unit), self.slot(other), "dp", bit)

    def start(self, outgoing):
        self.arrived[1] = self.links.send(outgoing, self.received, "dp", self.bits[0])

    def take(self, p):
        if p == 1:
            self.arrived[1].wait_recv()
            both = [self.own[...].astype(f32), self.received[...].astype(f32)]
            self.slot(0)[...] = jnp.concatenate(both, axis=1).astype(bf16)
            self.push(0, 1)
        elif p % 2 == 0:
            self.arrived[p].wait_recv()
            self.push(p)


def cast_store(dst, src):
    dst[...] = src[...].astype(bf16)


def gather_kernel(
    cfg,
    x_ref, dy_ref, ids_ref, small_ref, freq_ref, qkv_ref, w1_ref, wo_ref, w2_ref,
    n_out, dy_out, wq_out, w1_out, wo_out, w2_out, h_out, gp_out, o_out, dp_out, params_out, dysum_out, sums_out,
    n, dyb, wq, w1, wo, w2, sq, s1, so, s2, sta, stb, stc, std, tmp, nsw, pbuf, idb, cosb, sinb, startb,
    qkvb, lse, bias, o, do, dk, dv, dp, hst, gst, send_sems, recv_sems, local_sems, *pieces
):
    dbits, tbits = cfg
    order = place_order(1 << dbits)
    count = len(order)
    me = lax.axis_index("dp")
    me_t = lax.axis_index("tensor")
    sub = (me >> SUB_BIT) & 1
    rows = x_ref.shape[0]
    width = wo.shape[0]
    hidden = w2.shape[0]
    blk = D // count
    seqs = 2
    blocks = 1 << tbits
    length = rows * blocks
    links = Links(send_sems, recv_sems, local_sems)
    bits = [SUB_BIT] + list(range(2, dbits)) + [ROW_BIT]

    own_q = pl.ds(pl.multiple_of(sub * width, width), width)
    other_q = pl.ds(pl.multiple_of((1 - sub) * width, width), width)
    own_h = pl.ds(pl.multiple_of(sub * hidden, hidden), hidden)
    other_h = pl.ds(pl.multiple_of((1 - sub) * hidden, hidden), hidden)
    loads_q = []
    for j in range(3):
        lanes = pl.ds(j * width, width)
        loads_q.append(links.local(qkv_ref.at[j, :, other_q], std.at[:, lanes]))
        loads_q.append(links.local(qkv_ref.at[j, :, own_q], stc.at[:, lanes]))
    loads_2 = [links.local(w2_ref.at[other_h, :], stb), links.local(w2_ref.at[own_h, :], sta)]

    def row_slot(ref):
        return lambda p: ref.at[pl.ds(p * blk, blk), :]

    def column_gather(ref, own, received):
        unit = max(blk, 128)
        slot = lambda p: ref.at[:, pl.ds(p * unit, unit)]
        if unit == blk:
            return Gathered(links, slot, count, bits), slot(0)
        return GatheredPairs(links, slot, count, bits, own, received), own

    gq = Gathered(links, row_slot(wq), count, bits)
    g1 = Gathered(links, row_slot(w1), count, bits)
    go, wo_own = column_gather(wo, *pieces[0:2])
    g2, w2_own = column_gather(w2, *pieces[2:4])

    pbuf[0] = small_ref[...]
    idb[0] = ids_ref[...]
    greet(dbits, tbits)
    size = 1

    def ring(buf, size, axis, bit):
        return links.send(buf.at[pl.ds(0, size)], buf.at[pl.ds(size, size)], axis, bit)

    hop_p = ring(pbuf, 1, "dp", bits[0])
    hop_i = ring(idb, 1, "dp", SUB_BIT)

    for copy in loads_q:
        copy.wait()
    cast_store(sq, std.at[:, pl.ds(0, 3 * width)])
    gq.start(sq)
    wq[0:blk, :] = stc[:, : 3 * width].astype(bf16)
    gq.push(0)
    loads_1 = [links.local(w1_ref.at[:, other_h], std), links.local(w1_ref.at[:, own_h], stc)]

    x = x_ref[...].astype(f32)
    mean = jnp.mean(x, axis=-1, keepdims=True)
    x = x - mean
    inv = lax.rsqrt(jnp.mean(x * x, axis=-1, keepdims=True) + norm_eps)
    tmp[...] = x * inv

    ihops = [("tensor", bit) for bit in reversed(range(tbits))]
    isize = 2
    for step, bit in enumerate(bits[1:]):
        hop_p.wait_recv()
        size *= 2
        hop_p = ring(pbuf, size, "dp", bit)
        if step < len(ihops):
            hop_i.wait_recv()
            hop_i = ring(idb, isize, *ihops[step])
            isize *= 2
    hop_p.wait_recv()

    for a in range(0, count, max(1, 128 // blk)):
        part = [pbuf[place_of((a + k) ^ me, count)].astype(f32) for k in range(max(1, 128 // blk))]
        lanes = pl.ds(a * blk, max(blk, 128))
        params_out[:, lanes] = part[0] if len(part) == 1 else jnp.concatenate(part, axis=1)

    tmp[...] = tmp[...] * params_out[0:1, :] + params_out[1:2, :]

    def store_to(ref, count_rows):
        def store(lanes, value):
            ref[0:count_rows, lanes] = value.astype(bf16)

        return store

    load_tmp = lambda lanes: tmp[:, lanes]
    move_blocks(count, lambda j: me ^ order[j ^ 1], load_tmp, store_to(nsw, rows))
    tok = lambda ref, i: ref.at[pl.ds(i * rows, rows), :]
    n_in = {1: links.send(nsw, tok(n, 1), "dp", SUB_BIT)}
    move_blocks(count, lambda j: me ^ order[j], load_tmp, store_to(n, rows))

    def push_tokens(ref, arrived, i):
        for step, bit in enumerate(reversed(range(tbits))):
            size = 2 << step
            if i < size:
                arrived[i + size] = links.send(tok(ref, i), tok(ref, i + size), "tensor", bit)

    push_tokens(n, n_in, 0)

    def take_tokens(ref, arrived, i):
        arrived[i].wait_recv()
        push_tokens(ref, arrived, i)

    gq.take(1)
    for copy in loads_1:
        copy.wait()
    cast_store(s1, std)
    g1.start(s1)
    w1[0:blk, :] = stc[...].astype(bf16)
    g1.push(0)

    for copy in loads_2:
        copy.wait()
    cast_store(s2, stb)
    w2_own[...] = sta[...].astype(bf16)
    own_k = pl.ds(pl.multiple_of(sub * width, width), width)
    other_k = pl.ds(pl.multiple_of((1 - sub) * width, width), width)
    loads_o = [
        links.local(wo_ref.at[other_k, :], stb.at[pl.ds(0, width), :]),
        links.local(wo_ref.at[own_k, :], sta.at[pl.ds(0, width), :]),
    ]
    take_tokens(n, n_in, 1)
    g1.take(1)

    load_dy = lambda lanes: dy_ref[:, lanes].astype(f32)
    move_blocks(count, lambda j: me ^ order[j], load_dy, store_to(dyb, rows))
    n_in[1].wait_send()
    links.sent = [copy for copy in links.sent if copy is not n_in[1]]
    move_blocks(count, lambda j: me ^ order[j ^ 1], load_dy, store_to(nsw, rows))
    for copy in loads_o:
        copy.wait()
    so[...] = stb[0:width, :].astype(bf16)
    wo_own[...] = sta[0:width, :].astype(bf16)
    dy_in = {1: links.send(nsw, tok(dyb, 1), "dp", SUB_BIT)}
    go.start(so)
    g2.start(s2)
    push_tokens(dyb, dy_in, 0)
    go.push(0)

    for step in range(len(bits) - 1, len(ihops)):
        hop_i.wait_recv()
        hop_i = ring(idb, isize, *ihops[step])
        isize *= 2
    hop_i.wait_recv()
    half = ROT // 2
    for seq in range(seqs):
        row = jnp.concatenate(
            [idb[rel_index(me_t ^ b, seq, tbits)][0:1, :] for b in range(blocks)], axis=1
        ).astype(f32)
        first = jnp.sum(jnp.where(row < 1.0, 1.0, 0.0), axis=1, keepdims=True)
        second = jnp.sum(jnp.where(row < 2.0, 1.0, 0.0), axis=1, keepdims=True)
        begin = jnp.where(row < 1.0, 0.0, jnp.where(row < 2.0, first, second))
        place = lax.broadcasted_iota(jnp.int32, (1, length), 1).astype(f32)
        startb[seq, 0:1, :] = begin.astype(jnp.int32)
        angle = freq_ref[:, 0:1] * (place - begin)
        cosine, sine = jnp.cos(angle), jnp.sin(angle)
        rest = (HD - ROT, length)
        cosine = jnp.concatenate([cosine, cosine, jnp.ones(rest, f32)], axis=0)
        sine = jnp.concatenate([-sine, sine, jnp.zeros(rest, f32)], axis=0)
        cosb[seq] = jnp.concatenate([cosine, cosine], axis=0).T
        sinb[seq] = jnp.concatenate([sine, sine], axis=0).T

    dysum_out[...] = jnp.sum(dy_ref[...].astype(f32), axis=0, keepdims=True)

    head_start = me_t * (2 * width) + sub * width
    hidden_start = me_t * (2 * hidden) + sub * hidden
    lanes = pl.ds(pl.multiple_of(head_start, width), width)
    qkv_bias = [params_out[2 + j : 3 + j, lanes] for j in range(3)]
    row = 7 + hidden_start // D
    hidden_bias = params_out[pl.ds(row, 1), pl.ds(pl.multiple_of(hidden_start % D, hidden), hidden)]

    for p in range(2, count):
        gq.take(p)
    pairs = width // 128
    for c in range(blocks):
        for i in (2 * c, 2 * c + 1):
            if i > 1:
                take_tokens(n, n_in, i)
        rel = sum(((c >> (tbits - 1 - b)) & 1) << b for b in range(tbits))
        block = me_t ^ rel
        place = pl.ds(pl.multiple_of(block * rows, rows), rows)
        part = dot_nn(n[2 * c * rows : (2 * c + 2) * rows, :], wq[...])
        for seq in range(seqs):
            seq_rows = slice(seq * rows, (seq + 1) * rows)
            cosine, sine = cosb[seq, place, :], sinb[seq, place, :]
            for j in range(3 * pairs):
                kind, pair = j // pairs, j % pairs
                value = part[seq_rows, j * 128 : (j + 1) * 128] + qkv_bias[kind][:, pair * 128 : (pair + 1) * 128]
                if kind < 2:
                    value = value * cosine + swap_rotary(value) * sine
                qkvb[seq, place, j * 128 : (j + 1) * 128] = value.astype(bf16)
    stores = [links.local(n, n_out), links.local(wq, wq_out)]

    mid = count // 2

    def seq_rows_of(seq, b):
        return pl.ds(pl.multiple_of(rel_index(me_t ^ b, seq, tbits) * rows, rows), rows)

    def attend(seq):
        for qb in range(blocks):
            mask_bias(bias, startb[seq, 0:1, qb * rows : (qb + 1) * rows], qb, rows)
            attend_rows(qkvb, lse, bias, o, seq, qb, width, seq_rows_of(seq, qb))

    def attend_back(seq):
        dk[...] = jnp.zeros_like(dk)
        dv[...] = jnp.zeros_like(dv)
        for qb in range(blocks):
            mask_bias(bias, startb[seq, 0:1, qb * rows : (qb + 1) * rows], qb, rows)
            attend_back_rows(
                qkvb, lse, bias, do, cosb, sinb, dk, dv, dp, sums_out, seq, qb, width, seq_rows_of(seq, qb)
            )
        for b in range(blocks):
            attend_back_keys(cosb, sinb, dk, dv, dp, sums_out, seq, b, width, seq_rows_of(seq, b))

    sums_out[...] = jnp.zeros_like(sums_out)
    go.take(1)
    g2.push(0)
    g2.take(1)
    g1.take(2)
    attend(0)
    take_tokens(dyb, dy_in, 1)
    for p in range(3, mid):
        g1.take(p)
    attend(1)
    stores.append(links.local(o, o_out))
    for p in range(mid, count):
        g1.take(p)
    stores.append(links.local(w1, w1_out))

    kept = {}
    tile = hst.shape[2]
    for c in range(blocks):
        place = pl.ds(2 * c * rows, 2 * rows)
        for t in range(hidden // tile):
            lanes = pl.ds(t * tile, tile)
            slot = (c * (hidden // tile) + t) % 2
            for copy in kept.pop(slot, ()):
                copy.wait()
            v = dot_nn(n[place, :], w1[:, lanes]) + hidden_bias[:, t * tile : (t + 1) * tile]
            root = 0.7978845608028654
            square = v * v
            th = jnp.tanh(root * (v + 0.044715 * v * square))
            hst[slot] = (0.5 * v * (1.0 + th)).astype(bf16)
            gst[slot] = (
                0.5 * (1.0 + th) + 0.5 * v * (1.0 - th * th) * (root * (1.0 + (3 * 0.044715) * square))
            ).astype(bf16)
            kept[slot] = (
                links.local(hst.at[slot], h_out.at[place, lanes]),
                links.local(gst.at[slot], gp_out.at[place, lanes]),
            )
    for copies in kept.values():
        stores.extend(copies)

    for p in range(2, count):
        go.take(p)
    stores.append(links.local(wo, wo_out))
    for c in range(blocks):
        for i in (2 * c, 2 * c + 1):
            if i > 1:
                take_tokens(dyb, dy_in, i)
        place = slice(2 * c * rows, (2 * c + 2) * rows)
        do[place, :] = dot_nt(dyb[place, :], wo[...]).astype(bf16)
    stores.append(links.local(dyb, dy_out))
    g2.take(2)
    attend_back(0)
    for p in range(3, mid):
        g2.take(p)
    attend_back(1)
    stores.append(links.local(dp, dp_out))
    for p in range(mid, count):
        g2.take(p)
    stores.append(links.local(w2, w2_out))
    for copy in stores:
        copy.wait()
    links.finish()


def gather_call(dbits, tbits, x, dy, ids, small, qkv_weight, expand_weight, dense_weight, shrink_weight):
    count = 1 << dbits
    blk = D // count
    rows = x.shape[0]
    width = qkv_weight.shape[2] // 2
    hidden = expand_weight.shape[1] // 2
    tokens = rows * (2 << tbits)
    length = rows << tbits
    heads = width // HD
    half = ROT // 2
    freqs = (10000.0 ** (-jnp.arange(half, dtype=f32) / half))[:, None] * jnp.ones((1, 128), f32)
    any_spec = pl.BlockSpec(memory_space=pl.ANY)
    vm = pl.BlockSpec(memory_space=pltpu.VMEM)
    shape = lambda s, t=bf16: jax.ShapeDtypeStruct(s, t)
    vmem = lambda s, t=bf16: pltpu.VMEM(s, t)
    weights = 4 * (2 * count - 1) + 2 * 32 + 16
    scratch = [
        vmem((tokens, D)),
        vmem((tokens, D)),
        vmem((D, 3 * width)),
        vmem((D, hidden)),
        vmem((width, D)),
        vmem((hidden, D)),
        vmem((blk, 3 * width)),
        vmem((blk, hidden)),
        vmem((width, blk)),
        vmem((hidden, blk)),
        vmem((hidden, blk), f32),
        vmem((hidden, blk), f32),
        vmem((blk, hidden), f32),
        vmem((blk, hidden), f32),
        vmem((rows, D), f32),
        vmem((rows, D)),
        vmem((count, small.shape[0], blk)),
        vmem((2 << tbits, 8, rows), jnp.int32),
        vmem((2, length, 128), f32),
        vmem((2, length, 128), f32),
        vmem((2, 8, length), jnp.int32),
        vmem((2, length, 3 * width)),
        vmem((2, heads, length), f32),
        vmem((length, rows), f32),
        vmem((tokens, width)),
        vmem((tokens, width)),
        vmem((length, width), f32),
        vmem((length, width), f32),
        vmem((tokens, 3 * width)),
        vmem((2, 2 * rows, min(hidden, 512))),
        vmem((2, 2 * rows, min(hidden, 512))),
        pltpu.SemaphoreType.DMA((weights,)),
        pltpu.SemaphoreType.DMA((weights,)),
        pltpu.SemaphoreType.DMA((40,)),
    ]
    pieces = (vmem((width, blk)), vmem((hidden, blk)))
    scratch += [pieces[0]] * 2 + [pieces[1]] * 2 if blk % 128 else [vmem((16, 128))] * 4
    return pl.pallas_call(
        functools.partial(gather_kernel, (dbits, tbits)),
        out_shape=[
            shape((tokens, D)),
            shape((tokens, D)),
            shape((D, 3 * width)),
            shape((D, hidden)),
            shape((width, D)),
            shape((hidden, D)),
            shape((tokens, hidden)),
            shape((tokens, hidden)),
            shape((tokens, width)),
            shape((tokens, 3 * width)),
            shape((small.shape[0], D), f32),
            shape((1, D), f32),
            shape((8, 3 * width), f32),
        ],
        in_specs=[vm] * 5 + [any_spec] * 4,
        out_specs=[any_spec] * 10 + [vm] * 3,
        scratch_shapes=scratch,
        compiler_params=pltpu.CompilerParams(
            vmem_limit_bytes=62 * 2**20, collective_id=0, has_side_effects=True
        ),
        cost_estimate=pl.CostEstimate(flops=2 * 10**10, bytes_accessed=10**8, transcendentals=10**7),
        name="gather",
    )(x, dy, ids, small, freqs, qkv_weight, expand_weight, dense_weight, shrink_weight)


def adam_kernel(split_rows, parts, me_ref, w_ref, m_ref, v_ref, ka_ref, kb_ref, r_ref, wo_ref, mo_ref, vo_ref):
    sub = (me_ref[0] >> SUB_BIT) & 1
    own = ka_ref[...].astype(f32) + kb_ref[...].astype(f32)
    other = r_ref[...].astype(f32)
    if split_rows:
        grad = jnp.where(pl.program_id(0) // parts == sub, own, other)
    else:
        grad = jnp.concatenate([jnp.where(sub == 0, own, other), jnp.where(sub == 0, other, own)], axis=1)
    grad = grad.reshape(w_ref.shape)
    wo_ref[...], mo_ref[...], vo_ref[...] = adam_update(
        w_ref[...], m_ref[...], v_ref[...], grad, matrix_rate, weight_decay
    )


def adam_call(me, weight, first, second, keep_a, keep_b, recv, split_rows):
    shape = weight.shape
    parts = 1
    if len(shape) == 3:
        grid = shape[0]
        full = pl.BlockSpec((1,) + shape[1:], lambda i: (i, 0, 0))
        part = pl.BlockSpec((shape[1], shape[2] // 2), lambda i: (0, i))
    elif split_rows:
        block = min(512, shape[0] // 2)
        grid = shape[0] // block
        parts = grid // 2
        full = pl.BlockSpec((block, shape[1]), lambda i: (i, 0))
        part = pl.BlockSpec((block, shape[1]), lambda i: (i % parts, 0))
    else:
        block = 64
        grid = shape[0] // block
        full = pl.BlockSpec((block, shape[1]), lambda i: (i, 0))
        part = pl.BlockSpec((block, shape[1] // 2), lambda i: (i, 0))
    return tuple(
        pl.pallas_call(
            functools.partial(adam_kernel, split_rows, parts),
            grid=(grid,),
            out_shape=[jax.ShapeDtypeStruct(shape, f32)] * 3,
            in_specs=[smem_spec()] + [full] * 3 + [part] * 3,
            out_specs=[full] * 3,
            compiler_params=vmem_params(32),
            name="adam",
        )(me, weight, first, second, keep_a, keep_b, recv)
    )


def per_device(
    inputs,
    segments,
    cotangent,
    qkv_weight,
    qkv_first,
    qkv_second,
    dense_weight,
    dense_first,
    dense_second,
    expand_weight,
    expand_first,
    expand_second,
    shrink_weight,
    shrink_first,
    shrink_second,
    small_params,
    small_first,
    small_second,
):
    dp = lax.axis_size("dp")
    tensor_count = lax.axis_size("tensor")
    dbits = dp.bit_length() - 1
    tbits = tensor_count.bit_length() - 1
    d_me = lax.axis_index("dp")
    t_me = lax.axis_index("tensor")
    sub = (d_me >> SUB_BIT) & 1
    order = place_order(dp)
    high_bits = list(range(2, dbits))
    gather_bits = high_bits + [ROW_BIT]
    rows = inputs.shape[0]
    me = jnp.stack([d_me, t_me]).astype(jnp.int32)

    small_low = jnp.pad(small_params.astype(bf16), ((0, 16 - small_params.shape[0]), (0, 0)))
    ids = jnp.broadcast_to(segments, (8, rows))
    (
        normed, back_rows, qkv_wide, expand_full, dense_full, shrink_full, hidden_act, gelu_slope, attended, proj_back,
        params, back_sum, sums,
    ) = gather_call(
        dbits, tbits, inputs, cotangent, ids, small_low, qkv_weight, expand_weight, dense_weight, shrink_weight
    )
    width, hidden = dense_full.shape[0], shrink_full.shape[0]
    tokens = normed.shape[0]
    head_start = t_me * (2 * width) + sub * width
    hidden_start = t_me * (2 * hidden) + sub * hidden
    qkv_bias_grad = sums[0].reshape(3, width)

    def scatter_tokens(partial, gate):
        half = tokens // 2
        first = partial(half, tokens, gate).astype(bf16)
        recv = exchange(first, "tensor", 0)
        part = (partial(0, half, first) + recv.astype(f32)).astype(bf16)
        done = part
        for bit in range(1, tbits):
            half = half // 2
            recv = exchange(part[half:], "tensor", bit)
            part = (part[:half].astype(f32) + recv.astype(f32)).astype(bf16)
        return part[:rows], exchange(part[rows:], "dp", SUB_BIT), done

    def scatter_weight(partial, gather_axis, gate):
        cut = functools.partial(lax.slice_in_dim, axis=gather_axis)
        first = partial(1, gate).astype(bf16)
        recv = exchange(first, "dp", ROW_BIT)
        part = (partial(0, first) + recv.astype(f32)).astype(bf16)
        done = part
        for bit in reversed(high_bits[1:]):
            half = part.shape[gather_axis] // 2
            recv = exchange(cut(part, half, 2 * half), "dp", bit)
            part = (cut(part, 0, half).astype(f32) + recv.astype(f32)).astype(bf16)
        half = part.shape[gather_axis] // 2
        recv = exchange(cut(part, half, 2 * half), "dp", high_bits[0])
        keep_a, keep_b = cut(part, 0, half // 2), cut(recv, 0, half // 2)
        send = (cut(part, half // 2, half).astype(f32) + cut(recv, half // 2, half).astype(f32)).astype(bf16)
        return (keep_a, keep_b, exchange(send, "dp", SUB_BIT)), done

    halves = [slice(0, D // 2), slice(D // 2, D)]

    def branch(start, stop, gate):
        lhs = after(attended, gate)
        return jnp.dot(lhs[start:stop], dense_full, preferred_element_type=f32) + jnp.dot(
            hidden_act[start:stop], shrink_full, preferred_element_type=f32
        )

    keep, recv, done = scatter_tokens(branch, normed)
    output = out_call(order, me, inputs, keep, recv, params[5:7])

    def weight_part(left, right, spec, on_right):
        def partial(i, gate):
            if on_right:
                return jnp.einsum(spec, after(left, gate), right[:, halves[i]], preferred_element_type=f32)
            return jnp.einsum(spec, left[:, halves[i]], after(right, gate), preferred_element_type=f32)

        return partial

    dense_parts, done = scatter_weight(weight_part(attended, back_rows, "sk,sd->kd", True), 1, done)
    shrink_parts, done = scatter_weight(weight_part(hidden_act, back_rows, "sf,sd->fd", True), 1, done)
    act_back = jnp.einsum("sd,fd->sf", after(back_rows, done), shrink_full, preferred_element_type=f32)
    pre_back = (act_back * gelu_slope.astype(f32)).astype(bf16)
    expand_bias_grad = jnp.sum(pre_back, axis=0, dtype=f32)
    expand_parts, done = scatter_weight(weight_part(normed, pre_back, "sd,sf->df", False), 0, pre_back)

    def normed_back(start, stop, gate):
        return jnp.einsum(
            "se,de->sd", after(proj_back, gate)[start:stop], qkv_wide, preferred_element_type=f32
        ) + jnp.einsum("sf,df->sd", pre_back[start:stop], expand_full, preferred_element_type=f32)

    keep, recv, done = scatter_tokens(normed_back, done)
    input_grad, gain_shift = norm_back_call(order, me, inputs, cotangent, keep, recv, params[0:1])
    qkv_parts, done = scatter_weight(weight_part(normed, proj_back, "sd,se->de", False), 0, done)

    qkv_rows = lax.dynamic_update_slice_in_dim(jnp.zeros((3, D), f32), qkv_bias_grad, head_start, 1)
    expand_rows = lax.dynamic_update_slice_in_dim(
        jnp.zeros((FF,), f32), expand_bias_grad, hidden_start, 0
    ).reshape(FF // D, D)
    params_grad = jnp.concatenate([gain_shift, qkv_rows, back_sum, back_sum, expand_rows], axis=0)
    part = params_grad
    for bit in reversed(range(dbits)):
        half = part.shape[1] // 2
        mine = (d_me >> bit) & 1
        send = lax.dynamic_slice_in_dim(part, (1 - mine) * half, half, 1)
        part = lax.dynamic_slice_in_dim(part, mine * half, half, 1) + exchange(send, "dp", bit)
    for bit in range(tbits):
        part = part + exchange(part, "tensor", bit)

    dense_new = adam_call(me, dense_weight, dense_first, dense_second, *dense_parts, True)
    shrink_new = adam_call(me, shrink_weight, shrink_first, shrink_second, *shrink_parts, True)
    expand_new = adam_call(me, expand_weight, expand_first, expand_second, *expand_parts, False)
    qkv_new = adam_call(me, qkv_weight, qkv_first, qkv_second, *qkv_parts, False)
    small_new = adam_update(small_params, small_first, small_second, part, vector_rate, 0.0)
    return (output, input_grad) + qkv_new + dense_new + expand_new + shrink_new + small_new


def solution(mesh):
    token_spec = P(("dp", "tensor"), None)
    qkv_spec = P(None, "dp", "tensor")
    row_spec = P("tensor", "dp")
    column_spec = P("dp", "tensor")
    small_spec = P(None, "dp")
    weight_specs = (qkv_spec,) * 3 + (row_spec,) * 3 + (column_spec,) * 3 + (row_spec,) * 3 + (small_spec,) * 3
    return jax.shard_map(
        per_device,
        mesh=mesh,
        in_specs=(token_spec, P("dp", "tensor"), token_spec) + weight_specs,
        out_specs=(token_spec, token_spec) + weight_specs,
        check_vma=False,
    )
```

time: 828 us -> 704 us (0.85)
  Pallas kernels: 66.3 us -> 271 us
  waiting for transfers between devices: 362 us -> 260 us
  local copies, waits for them, and re-layouts: 110 us -> 22.7 us
  other arithmetic: 60.8 us -> 8.2 us
  matrix products: 148 us -> 105 us
  starting transfers between devices: 68.7 us -> 27.7 us
    pallas_call x3 -> x5, Pallas kernels: 60.2 us -> 263 us  [the longest x1 247 us: gather_call(): pl.pallas_call(functools.partial(gather_kernel, (dbits, tbits)), out_shap...]
    ppermute x71 -> x23, waiting for transfers between devices: 362 us -> 260 us  [exchange(): return lax.ppermute(values, axis, [(i, i ^ 1 << bit) for i in range(count)])]
    unnamed x184 -> x72, local copies, waits for them, and re-layouts: 76.1 us -> 2.24 us
    dot_general x16 -> x13, matrix products: 117 us -> 73.1 us  [the longest x4 26.8 us: partial(): jnp.einsum(spec, left[:, halves[i]], after(right, gate), preferred_elemen...]
    ppermute x71 -> x23, starting transfers between devices: 68.7 us -> 27.7 us  [exchange(): return lax.ppermute(values, axis, [(i, i ^ 1 << bit) for i in range(count)])]
    convert_element_type x11 -> x5, other arithmetic: 28.7 us -> 4.3 us  [the longest x4 3.58 us: scatter_weight(): (cut(part, half // 2, half).astype(f32) + cut(recv, half // 2, half).asty...]
    sub x5 -> x1, other arithmetic: 15 us -> 0.63 us  [adam_update(): weight - rate * (first_hat / (jnp.sqrt(second_hat) + adam_eps) + decay *...]
    concatenate x11 -> x0, local copies, waits for them, and re-layouts: 10.5 us -> none  [the longest x1 4.78 us: rotary_tables(): jnp.concatenate([sine, sine], axis=-1)]
  transfers between devices with their start and end apart: 71 -> 23, of which waited for: 29 -> 11; matrix products, arithmetic and copies ran while one was open for 31% -> 8% of each run, Pallas kernels for 5% -> 3%
where the time goes in v2:
time: 704 us; the launch traced here: 696 us
  Pallas kernels  271 us (38%)
  waiting for transfers between devices  260 us (37%)
  matrix products  105 us (15%)
  starting transfers between devices  27.7 us (4%)
  local copies, waits for them, and re-layouts  22.7 us (3%)
  other arithmetic  8.2 us (1%)
    ppermute x23, waiting for transfers between devices, exchange(): return lax.ppermute(values, axis, [(i, i ^ 1 << bit) for i in range(count)])  260 us
    pallas_call x1, Pallas kernels, gather_call(): pl.pallas_call(functools.partial(gather_kernel, (dbits, tbits)), out_shap...  247 us
    ppermute x23, starting transfers between devices, exchange(): return lax.ppermute(values, axis, [(i, i ^ 1 << bit) for i in range(count)])  27.7 us
    dot_general x4, matrix products, partial(): jnp.einsum(spec, left[:, halves[i]], after(right, gate), preferred_elemen...  26.8 us
    dot_general x2, matrix products, normed_back(): jnp.einsum('sf,df->sd', pre_back[start:stop], expand_full, preferred_elem...  18.2 us
    pallas_call x4, Pallas kernels, adam_call(): pl.pallas_call(functools.partial(adam_kernel, split_rows, parts), grid=(g...  16.3 us
    dot_general x2, matrix products, normed_back(): jnp.einsum('se,de->sd', after(proj_back, gate)[start:stop], qkv_wide, pre...  14.7 us
  transfers between devices with their start and end apart: 23, of which 11 were waited for; matrix products, arithmetic and copies ran while one was open for 8% of the time, Pallas kernels for 3%

profile of v2, /device:TPU:0, one launch (start us, length us, event | category | flops | bytes accessed | tf_op | source)
XLA Modules:
  0.0 696.1 jit_solution(2419946132601103651)
XLA Ops:
  3.9 247.0 %gather.1 = (bf16[2048,2048]{1,0:T(8,128)(2,1)}, bf16[2048,2048]{1,0:T(8,128)(2,1)}, bf16[2048,768]{1,0:T(8,128)(2,1)}, bf16[2048,1024]{1,0:T(8,128)(2,1)}, bf16...) custom-call(bf16[256,2048]{1,0:T(8,128)(2,1)} %x_ref.5, ...), custom_call_target="tpu_custom_call" | custom-call | flops 20000000000 | bytes 100000000 | tf_op jit(solution)/shard_map/gather/pallas_call | solution.py:717
  251.0 7.1 %fusion.20 = f32[1024,2048]{1,0:T(8,128)S(1)} fusion(bf16[1024,2048]{1,0:T(8,128)(2,1)} %get-tuple-element.62, bf16[2048,1024]{1,0:T(8,128)(2,1)} %get-tuple-element.70), kind=kOutput, calls=%fused_computation.31 | convolution fusion | flops 4294967296 | bytes 14680064 | tf_op jit(solution)/shard_map/dot_general | solution.py:869
  261.0 7.0 %fusion.18 = f32[1024,2048]{1,0:T(8,128)S(1)} fusion(bf16[1024,2048]{1,0:T(8,128)(2,1)} %get-tuple-element.62, bf16[2048,1024]{1,0:T(8,128)(2,1)S(1)} %copy-done.26), kind=kOutput, calls=%fused_computation.29 | convolution fusion | flops 4294967296 | bytes 14680064 | tf_op jit(solution)/shard_map/dot_general | solution.py:869
  274.0 13.4 %collective-permute-done.3 = bf16[256,1024]{1,0:T(8,128)(2,1)S(1)} collective-permute-done((bf16[256,1024]{1,0:T(8,128)(2,1)S(1)}, bf16[256,1024]{1,0:T(8,128)(2,1)S(1)}, u32[]{:S(2)}, u32[]{:S(2)}) %collective-permute-start.3) | collective-permute-done | bytes 524320 | tf_op jit(solution)/shard_map/ppermute | solution.py:33
  288.7 4.8 fusion.22
  294.8 46.3 %collective-permute-done.4 = bf16[1024,1024]{1,0:T(8,128)(2,1)S(1)} collective-permute-done((bf16[1024,1024]{1,0:T(8,128)(2,1)S(1)}, bf16[1024,1024]{1,0:T(8,128)(2,1)S(1)}, u32[]{:S(2)}, u32[]{:S(2)}) %collective-permute-start.4) | collective-permute-done | bytes 2097184 | tf_op jit(solution)/shard_map/ppermute | solution.py:33
  341.1 6.1 add_convert_fusion.6
  347.3 13.6 %convert_reduce_fusion = (f32[1024]{0:T(1024)S(1)}, bf16[2048,1024]{1,0:T(8,128)(2,1)}) fusion(bf16[2048,1024]{1,0:T(8,128)(2,1)} %get-tuple-element.72, bf16[2048,2048]{1,0:T(8,128)(2,1)S(1)} %bitcast.23, bf16[1024,2048]{1,0:T(8,128)(2,1)} %get-tuple-element.62), kind=kOutput, calls=%fused_computation | convolution fusion | flops 8600419328 | bytes 20975616 | tf_op jit(solution)/shard_map/sd,fd->sf/dot_general | solution.py:886
  360.9 7.1 %fusion.25 = bf16[1024,1024]{1,0:T(8,128)(2,1)S(1)} fusion(bf16[2048,1024]{1,0:T(8,128)(2,1)} %get-tuple-element.74, bf16[2048,2048]{1,0:T(8,128)(2,1)S(1)} %bitcast.25), kind=kOutput, calls=%fused_computation.34 | convolution fusion | flops 4296015872 | bytes 10485760 | tf_op jit(solution)/shard_map/sd,sf->df/dot_general | solution.py:880
  369.4 45.4 %collective-permute-done.5 = bf16[1024,1024]{1,0:T(8,128)(2,1)S(1)} collective-permute-done((bf16[1024,1024]{1,0:T(8,128)(2,1)S(1)}, bf16[1024,1024]{1,0:T(8,128)(2,1)S(1)}, u32[]{:S(2)}, u32[]{:S(2)}) %collective-permute-start.5) | collective-permute-done | bytes 2097184 | tf_op jit(solution)/shard_map/ppermute | solution.py:33
  414.9 5.7 add_convert_fusion.5
  420.6 5.6 fusion.37
  426.3 8.4 %add_convert_fusion.1 = bf16[1024,2048]{1,0:T(8,128)(2,1)S(1)} fusion(f32[1024,2048]{1,0:T(8,128)} %fusion.37, bf16[2048,1024]{1,0:T(8,128)(2,1)} %get-tuple-element.77, bf16[2048,1024]{1,0:T(8,128)(2,1)S(1)} %copy-done.28), kind=kOutput, calls=%fused_computation.2 | convolution fusion | flops 4299161600 | bytes 18874368 | tf_op jit(solution)/shard_map/sf,df->sd/dot_general | solution.py:894
  434.8 9.1 %fusion.35 = f32[1024,2048]{1,0:T(8,128)} fusion(bf16[2048,768]{1,0:T(8,128)(2,1)} %get-tuple-element.76, bf16[2048,768]{1,0:T(8,128)(2,1)} %get-tuple-element.81), kind=kOutput, calls=%fused_computation.36 | convolution fusion | flops 3221225472 | bytes 13107200 | tf_op jit(solution)/shard_map/se,de->sd/dot_general | solution.py:892
  443.9 9.8 %add_convert_fusion = bf16[1024,2048]{1,0:T(8,128)(2,1)S(1)} fusion(bf16[1024,2048]{1,0:T(8,128)(2,1)S(1)} %collective-permute-done.6, f32[1024,2048]{1,0:T(8,128)} %fusion.35, bf16[2048,1024]{1,0:T(8,128)(2,1)} %get-tuple-element.77, bf16[2048,1024]{1,0:T(8,128)(2,1)} %get-tuple-element.74), kind=kOutput, calls=%fused_computation.1 | convolution fusion | flops 4303355904 | bytes 23068672 | tf_op jit(solution)/shard_map/sf,df->sd/dot_general | solution.py:894
  468.8 6.8 fusion.28
  477.0 29.0 %collective-permute-done.7 = bf16[512,2048]{1,0:T(8,128)(2,1)} collective-permute-done((bf16[512,2048]{1,0:T(8,128)(2,1)}, bf16[512,2048]{1,0:T(8,128)(2,1)}, u32[]{:S(2)}, u32[]{:S(2)}) %collective-permute-start.7) | collective-permute-done | bytes 2097184 | tf_op jit(solution)/shard_map/ppermute | solution.py:33
  509.4 40.9 %collective-permute-done.1 = bf16[512,2048]{1,0:T(8,128)(2,1)S(1)} collective-permute-done((bf16[512,2048]{1,0:T(8,128)(2,1)S(1)}, bf16[512,2048]{1,0:T(8,128)(2,1)S(1)}, u32[]{:S(2)}, u32[]{:S(2)}) %collective-permute-start.1) | collective-permute-done | bytes 2097184 | tf_op jit(solution)/shard_map/ppermute | solution.py:33
  567.3 7.1 %add_convert_fusion.8 = bf16[1024,768]{1,0:T(8,128)(2,1)S(1)} fusion(bf16[1024,768]{1,0:T(8,128)(2,1)} %collective-permute-done.9, bf16[2048,768]{1,0:T(8,128)(2,1)} %get-tuple-element.81, bf16[2048,2048]{1,0:T(8,128)(2,1)} %get-tuple-element.58), kind=kOutput, calls=%fused_computation.26 | convolution fusion | flops 3223584768 | bytes 10485760 | tf_op jit(solution)/shard_map/sd,se->de/dot_general | solution.py:880
  574.5 35.8 %collective-permute-done.18 = f32[11,1024]{1,0:T(8,128)S(1)} collective-permute-done((f32[11,1024]{1,0:T(8,128)S(1)}, f32[11,1024]{1,0:T(8,128)S(1)}, u32[]{:S(2)}, u32[]{:S(2)}) %collective-permute-start.18) | collective-permute-done | bytes 45088 | tf_op jit(solution)/shard_map/ppermute | solution.py:33
  615.1 15.5 %collective-permute-done.19 = f32[11,512]{1,0:T(8,128)S(1)} collective-permute-done((f32[11,512]{1,0:T(8,128)S(1)}, f32[11,512]{1,0:T(8,128)S(1)}, u32[]{:S(2)}, u32[]{:S(2)}) %collective-permute-start.19) | collective-permute-done | bytes 22560 | tf_op jit(solution)/shard_map/ppermute | solution.py:33
  633.1 14.3 %collective-permute-done.10 = bf16[512,768]{1,0:T(8,128)(2,1)S(1)} collective-permute-done((bf16[512,768]{1,0:T(8,128)(2,1)S(1)}, bf16[512,768]{1,0:T(8,128)(2,1)S(1)}, u32[]{:S(2)}, u32[]{:S(2)}) %collective-permute-start.10) | collective-permute-done | bytes 786464 | tf_op jit(solution)/shard_map/ppermute | solution.py:33
  654.4 15.3 %collective-permute-done.13.r_ref = bf16[256,256]{1,0:T(8,128)(2,1)S(1)} collective-permute-done((bf16[256,256]{1,0:T(8,128)(2,1)S(1)}, bf16[256,256]{1,0:T(8,128)(2,1)S(1)}, u32[]{:S(2)}, u32[]{:S(2)}) %collective-permute-start.13) | collective-permute-done | bytes 131104 | tf_op jit(solution)/shard_map/ppermute | solution.py:33
  679.6 6.1 adam.7
  (166 shorter events, 87.0 us)
Async XLA Ops:
  259.4 8.7 %collective-permute-start = (bf16[1024,2048]{1,0:T(8,128)(2,1)S(1)}, bf16[1024,2048]{1,0:T(8,128)(2,1)S(1)}, u32[]{:S(2)}, u32[]{:S(2)}) collective-permute-start(bf16[1024,2048]{1,0:T(8,128)(2,1)S(1)} %add_convert_fusion.3), channel_id=1, source_target_pairs={{0,1},{1,0},{2,3},{3,2},{4,5},{5,4},{6,7},{7,6},{8,9},{9,8},{10,11... | collective-permute-start | bytes 12582920 | tf_op jit(solution)/shard_map/ppermute | solution.py:33
  272.6 14.8 %collective-permute-start.3 = (bf16[256,1024]{1,0:T(8,128)(2,1)S(1)}, bf16[256,1024]{1,0:T(8,128)(2,1)S(1)}, u32[]{:S(2)}, u32[]{:S(2)}) collective-permute-start(bf16[256,1024]{1,0:T(8,128)(2,1)S(1)} %fusion.39), channel_id=1, source_target_pairs={{0,4},{4,0},{8,12},{12,8},{16,20},{20,16},{24,28},{28,24},{1,5},{5... | collective-permute-start | bytes 1572872 | tf_op jit(solution)/shard_map/ppermute | solution.py:33
  288.7 174.2 %copy-start.20 = (bf16[256,1024]{1,0:T(8,128)(2,1)}, bf16[256,1024]{1,0:T(8,128)(2,1)S(1)}, u32[]{:S(2)}) copy-start(bf16[256,1024]{1,0:T(8,128)(2,1)S(1)} %add_convert_fusion.11) | copy-start | bytes 1572868
  293.5 47.6 %collective-permute-start.4 = (bf16[1024,1024]{1,0:T(8,128)(2,1)S(1)}, bf16[1024,1024]{1,0:T(8,128)(2,1)S(1)}, u32[]{:S(2)}, u32[]{:S(2)}) collective-permute-start(bf16[1024,1024]{1,0:T(8,128)(2,1)S(1)} %fusion.22), channel_id=1, source_target_pairs={{0,4},{4,0},{8,12},{12,8},{16,20},{20,16},{24,28},{28,24},{1,5},{5... | collective-permute-start | bytes 6291464 | tf_op jit(solution)/shard_map/ppermute | solution.py:33
  368.1 46.8 %collective-permute-start.5 = (bf16[1024,1024]{1,0:T(8,128)(2,1)S(1)}, bf16[1024,1024]{1,0:T(8,128)(2,1)S(1)}, u32[]{:S(2)}, u32[]{:S(2)}) collective-permute-start(bf16[1024,1024]{1,0:T(8,128)(2,1)S(1)} %fusion.25), channel_id=1, source_target_pairs={{0,4},{4,0},{8,12},{12,8},{16,20},{20,16},{24,28},{28,24},{1,5},{5... | collective-permute-start | bytes 6291464 | tf_op jit(solution)/shard_map/ppermute | solution.py:33
  434.7 9.2 %collective-permute-start.6 = (bf16[1024,2048]{1,0:T(8,128)(2,1)S(1)}, bf16[1024,2048]{1,0:T(8,128)(2,1)S(1)}, u32[]{:S(2)}, u32[]{:S(2)}) collective-permute-start(bf16[1024,2048]{1,0:T(8,128)(2,1)S(1)} %add_convert_fusion.1), channel_id=1, source_target_pairs={{0,1},{1,0},{2,3},{3,2},{4,5},{5,4},{6,7},{7,6},{8,9},{9,8},{10,11... | collective-permute-start | bytes 12582920 | tf_op jit(solution)/shard_map/ppermute | solution.py:33
  457.2 48.7 %collective-permute-start.7 = (bf16[512,2048]{1,0:T(8,128)(2,1)}, bf16[512,2048]{1,0:T(8,128)(2,1)}, u32[]{:S(2)}, u32[]{:S(2)}) collective-permute-start(bf16[512,2048]{1,0:T(8,128)(2,1)} %slice.183), channel_id=1, source_target_pairs={{0,2},{1,3},{2,0},{3,1},{4,6},{5,7},{6,4},{7,5},{8,10},{9,11},{10,... | collective-permute-start | bytes 6291464 | tf_op jit(solution)/shard_map/ppermute | solution.py:33
  462.2 88.2 %collective-permute-start.1 = (bf16[512,2048]{1,0:T(8,128)(2,1)S(1)}, bf16[512,2048]{1,0:T(8,128)(2,1)S(1)}, u32[]{:S(2)}, u32[]{:S(2)}) collective-permute-start(bf16[512,2048]{1,0:T(8,128)(2,1)S(1)} %slice.177), channel_id=1, source_target_pairs={{0,2},{1,3},{2,0},{3,1},{4,6},{5,7},{6,4},{7,5},{8,10},{9,11},{10,... | collective-permute-start | bytes 6291464 | tf_op jit(solution)/shard_map/ppermute | solution.py:33
  463.6 187.5 %collective-permute-start.12 = (bf16[256,512]{1,0:T(8,128)(2,1)}, bf16[256,512]{1,0:T(8,128)(2,1)S(1)}, u32[]{:S(2)}, u32[]{:S(2)}) collective-permute-start(bf16[256,512]{1,0:T(8,128)(2,1)} %slice.192), channel_id=1, source_target_pairs={{0,16},{4,20},{8,24},{12,28},{16,0},{20,4},{24,8},{28,12},{1,17},{... | collective-permute-start | bytes 786440 | tf_op jit(solution)/shard_map/ppermute | solution.py:33
  465.9 87.0 %collective-permute-start.16 = (bf16[1024,512]{1,0:T(8,128)(2,1)}, bf16[1024,512]{1,0:T(8,128)(2,1)}, u32[]{:S(2)}, u32[]{:S(2)}) collective-permute-start(bf16[1024,512]{1,0:T(8,128)(2,1)} %slice.202), channel_id=1, source_target_pairs={{0,16},{4,20},{8,24},{12,28},{16,0},{20,4},{24,8},{28,12},{1,17},{... | collective-permute-start | bytes 3145736 | tf_op jit(solution)/shard_map/ppermute | solution.py:33
  475.7 88.6 %collective-permute-start.9 = (bf16[1024,768]{1,0:T(8,128)(2,1)}, bf16[1024,768]{1,0:T(8,128)(2,1)}, u32[]{:S(2)}, u32[]{:S(2)}) collective-permute-start(bf16[1024,768]{1,0:T(8,128)(2,1)} %fusion.28), channel_id=1, source_target_pairs={{0,4},{4,0},{8,12},{12,8},{16,20},{20,16},{24,28},{28,24},{1,5},{5... | collective-permute-start | bytes 4718600 | tf_op jit(solution)/shard_map/ppermute | solution.py:33
  509.4 50.0 %collective-permute-start.8 = (bf16[256,2048]{1,0:T(8,128)(2,1)}, bf16[256,2048]{1,0:T(8,128)(2,1)}, u32[]{:S(2)}, u32[]{:S(2)}) collective-permute-start(bf16[256,2048]{1,0:T(8,128)(2,1)} %get-tuple-element.100), channel_id=1, source_target_pairs={{0,8},{4,12},{8,0},{12,4},{16,24},{20,28},{24,16},{28,20},{1,9},{5... | collective-permute-start | bytes 3145736 | tf_op jit(solution)/shard_map/ppermute | solution.py:33
  552.3 123.3 %collective-permute-start.2 = (bf16[256,2048]{1,0:T(8,128)(2,1)}, bf16[256,2048]{1,0:T(8,128)(2,1)}, u32[]{:S(2)}, u32[]{:S(2)}) collective-permute-start(bf16[256,2048]{1,0:T(8,128)(2,1)} %get-tuple-element.102), channel_id=1, source_target_pairs={{0,8},{4,12},{8,0},{12,4},{16,24},{20,28},{24,16},{28,20},{1,9},{5... | collective-permute-start | bytes 3145736 | tf_op jit(solution)/shard_map/ppermute | solution.py:33
  555.1 124.4 %collective-permute-start.17 = (bf16[1024,256]{1,0:T(8,128)(2,1)}, bf16[1024,256]{1,0:T(8,128)(2,1)}, u32[]{:S(2)}, u32[]{:S(2)}) collective-permute-start(bf16[1024,256]{1,0:T(8,128)(2,1)} %add_convert_fusion.9), channel_id=1, source_target_pairs={{0,8},{4,12},{8,0},{12,4},{16,24},{20,28},{24,16},{28,20},{1,9},{5... | collective-permute-start | bytes 1572872 | tf_op jit(solution)/shard_map/ppermute | solution.py:33
  559.4 54.4 %collective-permute-start.14 = (bf16[512,1024]{1,0:T(8,128)(2,1)}, bf16[512,1024]{1,0:T(8,128)(2,1)}, u32[]{:S(2)}, u32[]{:S(2)}) collective-permute-start(bf16[512,1024]{1,0:T(8,128)(2,1)} %slice.197), channel_id=1, source_target_pairs={{0,16},{4,20},{8,24},{12,28},{16,0},{20,4},{24,8},{28,12},{1,17},{... | collective-permute-start | bytes 3145736 | tf_op jit(solution)/shard_map/ppermute | solution.py:33
  564.3 45.9 %collective-permute-start.18 = (f32[11,1024]{1,0:T(8,128)S(1)}, f32[11,1024]{1,0:T(8,128)S(1)}, u32[]{:S(2)}, u32[]{:S(2)}) collective-permute-start(f32[11,1024]{1,0:T(8,128)S(1)} %constant_dynamic-slice_fusion.2), channel_id=1, source_target_pairs={{0,16},{4,20},{8,24},{12,28},{16,0},{20,4},{24,8},{28,12},{1,17},{... | collective-permute-start | bytes 135176 | tf_op jit(solution)/shard_map/ppermute | solution.py:33
  610.2 37.1 %collective-permute-start.10 = (bf16[512,768]{1,0:T(8,128)(2,1)S(1)}, bf16[512,768]{1,0:T(8,128)(2,1)S(1)}, u32[]{:S(2)}, u32[]{:S(2)}) collective-permute-start(bf16[512,768]{1,0:T(8,128)(2,1)S(1)} %slice.187), channel_id=1, source_target_pairs={{0,16},{4,20},{8,24},{12,28},{16,0},{20,4},{24,8},{28,12},{1,17},{... | collective-permute-start | bytes 2359304 | tf_op jit(solution)/shard_map/ppermute | solution.py:33
  613.7 16.8 %collective-permute-start.19 = (f32[11,512]{1,0:T(8,128)S(1)}, f32[11,512]{1,0:T(8,128)S(1)}, u32[]{:S(2)}, u32[]{:S(2)}) collective-permute-start(f32[11,512]{1,0:T(8,128)S(1)} %constant_dynamic-slice_fusion.1), channel_id=1, source_target_pairs={{0,8},{4,12},{8,0},{12,4},{16,24},{20,28},{24,16},{28,20},{1,9},{5... | collective-permute-start | bytes 67592 | tf_op jit(solution)/shard_map/ppermute | solution.py:33
  630.6 56.3 %collective-permute-start.15 = (bf16[256,1024]{1,0:T(8,128)(2,1)S(1)}, bf16[256,1024]{1,0:T(8,128)(2,1)S(1)}, u32[]{:S(2)}, u32[]{:S(2)}) collective-permute-start(bf16[256,1024]{1,0:T(8,128)(2,1)S(1)} %add_convert_fusion.10), channel_id=1, source_target_pairs={{0,8},{4,12},{8,0},{12,4},{16,24},{20,28},{24,16},{28,20},{1,9},{5... | collective-permute-start | bytes 1572872 | tf_op jit(solution)/shard_map/ppermute | solution.py:33
  647.4 3.7 collective-permute-start.20
  651.1 40.2 %collective-permute-start.11 = (bf16[256,768]{1,0:T(8,128)(2,1)S(1)}, bf16[256,768]{1,0:T(8,128)(2,1)S(1)}, u32[]{:S(2)}, u32[]{:S(2)}) collective-permute-start(bf16[256,768]{1,0:T(8,128)(2,1)S(1)} %add_convert_fusion.12), channel_id=1, source_target_pairs={{0,8},{4,12},{8,0},{12,4},{16,24},{20,28},{24,16},{28,20},{1,9},{5... | collective-permute-start | bytes 1179656 | tf_op jit(solution)/shard_map/ppermute | solution.py:33
  651.1 1.2 collective-permute-start.21
  652.4 17.4 %collective-permute-start.13 = (bf16[256,256]{1,0:T(8,128)(2,1)S(1)}, bf16[256,256]{1,0:T(8,128)(2,1)S(1)}, u32[]{:S(2)}, u32[]{:S(2)}) collective-permute-start(bf16[256,256]{1,0:T(8,128)(2,1)S(1)} %add_convert_fusion.13), channel_id=1, source_target_pairs={{0,8},{4,12},{8,0},{12,4},{16,24},{20,28},{24,16},{28,20},{1,9},{5... | collective-permute-start | bytes 393224 | tf_op jit(solution)/shard_map/ppermute | solution.py:33
  669.7 25.4 %collective-permute-start.22 = (f32[11,256]{1,0:T(8,128)S(1)}, f32[11,256]{1,0:T(8,128)S(1)}, u32[]{:S(2)}, u32[]{:S(2)}) collective-permute-start(f32[11,256]{1,0:T(8,128)S(1)} %add.139), channel_id=1, source_target_pairs={{0,2},{1,3},{2,0},{3,1},{4,6},{5,7},{6,4},{7,5},{8,10},{9,11},{10,... | collective-permute-start | bytes 33800 | tf_op jit(solution)/shard_map/ppermute | solution.py:33
  (35 other events, 892.0 us)

commit v3 on v2

--- a/solution.py
+++ b/solution.py
@@ -100,52 +100,6 @@
 
     move_blocks(count, lambda j: place_of(j ^ me, count), lambda lanes: keep_ref[:, lanes].astype(f32), store)
     move_blocks(count, lambda j: place_of(j ^ me, count) ^ 1, lambda lanes: recv_ref[:, lanes].astype(f32), add)
-
-
-def out_kernel(order, me_ref, x_ref, keep_ref, recv_ref, b_ref, o_ref, tmp):
-    assemble(order, me_ref[0], keep_ref, recv_ref, tmp)
-    o_ref[...] = (x_ref[...].astype(f32) + tmp[...] + b_ref[0:1] + b_ref[1:2]).astype(bf16)
-
-
-def out_call(order, me, x, keep, recv, biases):
-    vm = pl.BlockSpec(memory_space=pltpu.VMEM)
-    return pl.pallas_call(
-        functools.partial(out_kernel, order),
-        out_shape=jax.ShapeDtypeStruct(x.shape, bf16),
-        in_specs=[smem_spec(), vm, vm, vm, vm],
-        out_specs=vm,
-        scratch_shapes=[pltpu.VMEM(x.shape, f32)],
-        compiler_params=vmem_params(32),
-        name="block_output",
-    )(me, x, keep, recv, biases)
-
-
-def norm_back_kernel(order, me_ref, x_ref, dy_ref, keep_ref, recv_ref, g_ref, o_ref, sums_ref, tmp):
-    assemble(order, me_ref[0], keep_ref, recv_ref, tmp)
-    rows = x_ref[...].astype(f32)
-    centered = rows - jnp.mean(rows, axis=-1, keepdims=True)
-    inv = lax.rsqrt(jnp.mean(centered * centered, axis=-1, keepdims=True) + norm_eps)
-    unit = centered * inv
-    back = tmp[...]
-    sums_ref[0:1] = jnp.sum(back * unit, axis=0, keepdims=True)
-    sums_ref[1:2] = jnp.sum(back, axis=0, keepdims=True)
-    e = back * g_ref[...]
-    o_ref[...] = dy_ref[...].astype(f32) + inv * (
-        e - jnp.mean(e, axis=-1, keepdims=True) - unit * jnp.mean(e * unit, axis=-1, keepdims=True)
-    )
-
-
-def norm_back_call(order, me, x, dy, keep, recv, gain):
-    vm = pl.BlockSpec(memory_space=pltpu.VMEM)
-    return pl.pallas_call(
-        functools.partial(norm_back_kernel, order),
-        out_shape=[jax.ShapeDtypeStruct(x.shape, f32), jax.ShapeDtypeStruct((2, D), f32)],
-        in_specs=[smem_spec()] + [vm] * 5,
-        out_specs=[vm, vm],
-        scratch_shapes=[pltpu.VMEM(x.shape, f32)],
-        compiler_params=vmem_params(40),
-        name="norm_back",
-    )(me, x, dy, keep, recv, gain)
 
 
 def swap_rotary(values):
@@ -295,6 +249,13 @@
         copy.start()
         return copy
 
+    def local_wait(self, src, dst):
+        self.local(src, dst).wait()
+
+    def sent_done(self, copy):
+        copy.wait_send()
+        self.sent = [other for other in self.sent if other is not copy]
+
     def finish(self):
         for copy in self.sent:
             copy.wait_send()
@@ -509,8 +470,7 @@
 
     load_dy = lambda lanes: dy_ref[:, lanes].astype(f32)
     move_blocks(count, lambda j: me ^ order[j], load_dy, store_to(dyb, rows))
-    n_in[1].wait_send()
-    links.sent = [copy for copy in links.sent if copy is not n_in[1]]
+    links.sent_done(n_in[1])
     move_blocks(count, lambda j: me ^ order[j ^ 1], load_dy, store_to(nsw, rows))
     for copy in loads_o:
         copy.wait()
@@ -742,48 +702,400 @@
     )(x, dy, ids, small, freqs, qkv_weight, expand_weight, dense_weight, shrink_weight)
 
 
-def adam_kernel(split_rows, parts, me_ref, w_ref, m_ref, v_ref, ka_ref, kb_ref, r_ref, wo_ref, mo_ref, vo_ref):
+class Reduced:
+    def __init__(self, links, start, rows, send, keep, ry, rz, rl, own_out, own, stage, high_bits, blk):
+        self.links, self.start, self.rows = links, start, rows
+        self.send, self.keep, self.ry, self.rz, self.rl = send, keep, ry, rz, rl
+        self.own_out, self.own, self.stage = own_out, own, stage
+        self.high_bits, self.blk = high_bits, blk
+        self.here = pl.ds(start, rows)
+        self.step, self.done = 0, False
+
+    def dot(self, dst, lhs, first, rhs, side):
+        half = dst.shape[1]
+        value = dot_tn(lhs[:, pl.ds(first, self.rows)], rhs[:, pl.ds(side * half, half)])
+        dst[self.here, :] = value.astype(bf16)
+
+    def away(self, lhs, first, rhs):
+        self.dot(self.send, lhs, first, rhs, 1)
+        self.hop = self.links.send(self.send.at[self.here, :], self.ry.at[self.here, :], "dp", ROW_BIT)
+
+    def home(self, lhs, first, rhs):
+        self.dot(self.keep, lhs, first, rhs, 0)
+
+    def load(self, src, lanes):
+        part = self.stage.at[pl.ds(0, self.rows), pl.ds(0, lanes)]
+        self.links.local_wait(src.at[self.here, :], part)
+        return self.stage[0 : self.rows, 0:lanes].astype(f32)
+
+    def fold(self):
+        self.hop.wait_recv()
+        src = self.ry if self.step == 0 else self.rz[self.step - 1]
+        lanes = src.shape[1]
+        value = self.keep[self.here, 0:lanes].astype(f32) + self.load(src, lanes)
+        if self.step < len(self.high_bits):
+            half = lanes // 2
+            self.keep[self.here, 0:lanes] = value.astype(bf16)
+            part = self.keep.at[self.here, pl.ds(half, half)]
+            bit = self.high_bits[len(self.high_bits) - 1 - self.step]
+            self.hop = self.links.send(part, self.rz[self.step].at[self.here, :], "dp", bit)
+            self.step += 1
+            return
+        blk = self.blk
+        out = self.own.at[pl.ds(0, self.rows), :]
+        self.own[0 : self.rows, :] = value[:, 0:blk]
+        copy = self.links.local(out, self.own_out.at[self.here, :])
+        self.last[self.here, :] = value[:, blk : 2 * blk].astype(bf16)
+        self.hop = self.links.send(self.last.at[self.here, :], self.rl.at[self.here, :], "dp", SUB_BIT)
+        copy.wait()
+        self.done = True
+
+    def drain(self):
+        while not self.done:
+            self.fold()
+
+
+def reduce_kernel(
+    cfg,
+    x_ref, dy_own_ref, params_ref, back_sum_ref, sums_ref,
+    n_hbm, dy_hbm, wq_hbm, w1_hbm, wo_hbm, w2_hbm, h_hbm, gp_hbm, o_hbm, dp_hbm,
+    y_out, dx_out, own_out, rl, pg_out, ry, rc1, rx1, rs1, rc2, rx2, rs2, *rest
+):
+    dbits, tbits = cfg
+    highs = dbits - 2
+    rz, rest = rest[:highs], rest[highs:]
+    (
+        big, hw1, gp, w2, wo, wq, o, dp, send, keep, last, own, sx, kx, sz, stage, tmp, pg, hsum,
+        send_sems, recv_sems, local_sems, *prb
+    ) = rest
+    order = place_order(1 << dbits)
+    count = len(order)
+    me = lax.axis_index("dp")
+    me_t = lax.axis_index("tensor")
+    sub = (me >> SUB_BIT) & 1
+    rows = x_ref.shape[0]
+    blk = D // count
+    width, hidden = wo.shape[0], w2.shape[0]
+    tokens = n_hbm.shape[0]
+    links = Links(send_sems, recv_sems, local_sems)
+    high_bits = list(range(2, dbits))
+
+    get_o = links.local(o_hbm, o)
+    get_dy = links.local(dy_hbm, big)
+    get_h = links.local(h_hbm, hw1)
+    get_w2 = links.local(w2_hbm, w2)
+    get_gp = links.local(gp_hbm, gp)
+    get_wo = links.local(wo_hbm, wo)
+    get_dp = links.local(dp_hbm, dp)
+    get_wq = links.local(wq_hbm, wq)
+    greet(dbits, tbits)
+
+    def unit(start, size):
+        made = Reduced(links, start, size, send, keep, ry, rz, rl, own_out, own, stage, high_bits, blk)
+        made.last = last
+        return made
+
+    chunk = min(512, hidden)
+    per = hidden // chunk
+    u_o = unit(0, width)
+    u_2 = [unit(width + i * chunk, chunk) for i in range(per)]
+    u_1 = [unit(width + hidden + i * chunk, chunk) for i in range(per)]
+    u_q = [unit(width + 2 * hidden + j * width, width) for j in range(3)]
+
+    get_o.wait()
+    get_dy.wait()
+    u_o.away(o, 0, big)
+    get_h.wait()
+    for i in range(per):
+        u_2[i].away(hw1, i * chunk, big)
+    u_o.home(o, 0, big)
+    for i in range(per):
+        u_2[i].home(hw1, i * chunk, big)
+
+    get_w2.wait()
+    get_gp.wait()
+    hsum[...] = jnp.zeros_like(hsum)
+    tile = 2 * rows
+
+    def back_tile(c, carry):
+        place = pl.ds(pl.multiple_of(c * tile, tile), tile)
+        for t in range(0, hidden, chunk):
+            lanes = slice(t, t + chunk)
+            value = (dot_nt(big[place, :], w2[lanes, :]) * gp[place, lanes].astype(f32)).astype(bf16)
+            gp[place, lanes] = value
+            hsum[0:1, lanes] += jnp.sum(value.astype(f32), axis=0, keepdims=True)
+        return carry
+
+    lax.fori_loop(0, tokens // tile, back_tile, 0)
+    u_o.fold()
+
+    half = tokens // 2
+    quarter = tokens // 4
+    get_n = [links.local(n_hbm.at[pl.ds(0, half), :], big.at[pl.ds(0, half), :])]
+    get_wo.wait()
+    step_lanes = 512
+
+    def branch(place, lanes):
+        return dot_nn(o[place, :], wo[:, lanes]) + dot_nn(hw1[place, :], w2[:, lanes])
+
+    def normed_back(place, lanes):
+        return dot_nt(dp[place, :], wq[lanes, :]) + dot_nt(gp[place, :], hw1[lanes, :])
+
+    def part_rows(partial, first, dst, dst_first, added):
+        place = pl.ds(first, quarter)
+        target = pl.ds(dst_first, quarter)
+
+        def body(t, carry):
+            lanes = pl.ds(pl.multiple_of(t * step_lanes, step_lanes), step_lanes)
+            value = partial(place, lanes)
+            if added is not None:
+                value = value + added[:, lanes].astype(f32)
+            dst[target, lanes] = value.astype(bf16)
+            return carry
+
+        lax.fori_loop(0, D // step_lanes, body, 0)
+
+    def far_rows(partial, rc):
+        hops = []
+        for first in (half + quarter, half):
+            part_rows(partial, first, big, first, None)
+            there = pl.ds(first - half, quarter)
+            hops.append(links.send(big.at[pl.ds(first, quarter), :], rc.at[there, :], "tensor", 0))
+        return hops
+
+    def near_rows(partial, rc, hops, sx, sx_first, kx, kx_first, rx):
+        hops[0].wait_recv()
+        links.local_wait(rc.at[pl.ds(quarter, quarter), :], stage)
+        part_rows(partial, quarter, sx, sx_first, stage)
+        hop = links.send(sx.at[pl.ds(sx_first, quarter), :], rx, "tensor", 1)
+        hops[1].wait_recv()
+        links.local_wait(rc.at[pl.ds(0, quarter), :], stage)
+        part_rows(partial, 0, kx, kx_first, stage)
+        return hop
+
+    def own_rows(hop, rx, kx, kx_first, sz, rs):
+        hop.wait_recv()
+        links.local_wait(rx, stage)
+        here, there = pl.ds(kx_first, rows), pl.ds(kx_first + rows, rows)
+        sz[0:rows, :] = (kx[there, :].astype(f32) + stage[rows : 2 * rows, :].astype(f32)).astype(bf16)
+        hop = links.send(sz.at[pl.ds(0, rows), :], rs, "dp", SUB_BIT)
+        kx[here, :] = (kx[here, :].astype(f32) + stage[0:rows, :].astype(f32)).astype(bf16)
+        return hop
+
+    def last_rows(hop, rs, kx, kx_first):
+        hop.wait_recv()
+        received = stage.at[pl.ds(0, rows), :]
+        links.local_wait(rs, received)
+        assemble(order, me, kx.at[pl.ds(kx_first, rows), :], received, tmp)
+
+    hops = far_rows(branch, rc1)
+    x_hop1 = near_rows(branch, rc1, hops, sx, 0, kx, 0, rx1)
+    get_w1 = links.local(w1_hbm, hw1)
+    u_2[0].fold()
+    for hop in hops:
+        links.sent_done(hop)
+    get_n.append(links.local(n_hbm.at[pl.ds(half, half), :], big.at[pl.ds(half, half), :]))
+    u_o.drain()
+    for copy in get_n:
+        copy.wait()
+    for i in range(per):
+        u_1[i].away(gp, i * chunk, big)
+    get_dp.wait()
+    for j in range(3):
+        u_q[j].away(dp, j * width, big)
+    for i in range(1, per):
+        u_2[i].fold()
+    for i in range(per):
+        u_1[i].home(gp, i * chunk, big)
+    for j in range(3):
+        u_q[j].home(dp, j * width, big)
+    u_2[0].drain()
+
+    get_wq.wait()
+    get_w1.wait()
+    hops = far_rows(normed_back, rc2)
+    x_hop2 = near_rows(normed_back, rc2, hops, big, quarter, big, 0, rx2)
+
+    s_hop1 = own_rows(x_hop1, rx1, kx, 0, sz, rs1)
+    u_1[0].fold()
+    for i in range(1, per):
+        u_2[i].drain()
+    last_rows(s_hop1, rs1, kx, 0)
+    links.sent_done(x_hop1)
+    sx[0:rows, :] = (x_ref[...].astype(f32) + tmp[...] + params_ref[5:6, :] + params_ref[6:7, :]).astype(bf16)
+    y_copy = links.local(sx.at[pl.ds(0, rows), :], y_out)
+    for i in range(1, per):
+        u_1[i].fold()
+    u_1[0].drain()
+    u_q[0].fold()
+    s_hop2 = own_rows(x_hop2, rx2, big, 0, w2, rs2)
+    u_q[1].fold()
+    u_q[2].fold()
+    for i in range(1, per):
+        u_1[i].drain()
+
+    last_rows(s_hop2, rs2, big, 0)
+    pg[...] = jnp.zeros_like(pg)
+    strip = 64
+
+    def norm_back(i, carry):
+        place = pl.ds(pl.multiple_of(i * strip, strip), strip)
+        x = x_ref[place, :].astype(f32)
+        x = x - jnp.mean(x, axis=-1, keepdims=True)
+        inv = lax.rsqrt(jnp.mean(x * x, axis=-1, keepdims=True) + norm_eps)
+        x = x * inv
+        back = tmp[place, :]
+        pg[0:1, :] += jnp.sum(back * x, axis=0, keepdims=True)
+        pg[1:2, :] += jnp.sum(back, axis=0, keepdims=True)
+        e = back * params_ref[0:1, :]
+        tmp[place, :] = dy_own_ref[place, :].astype(f32) + inv * (
+            e - jnp.mean(e, axis=-1, keepdims=True) - x * jnp.mean(e * x, axis=-1, keepdims=True)
+        )
+        return carry
+
+    lax.fori_loop(0, rows // strip, norm_back, 0)
+    dx_copy = links.local(tmp, dx_out)
+
+    head_start = me_t * (2 * width) + sub * width
+    hidden_start = me_t * (2 * hidden) + sub * hidden
+    lanes = pl.ds(pl.multiple_of(head_start, width), width)
+    for j in range(3):
+        pg[2 + j : 3 + j, lanes] = sums_ref[0:1, j * width : (j + 1) * width]
+    pg[5:6, :] = back_sum_ref[...]
+    pg[6:7, :] = back_sum_ref[...]
+    pg[pl.ds(7 + hidden_start // D, 1), pl.ds(pl.multiple_of(hidden_start % D, hidden), hidden)] = hsum[0:1, :]
+    base, size, slot = 0, D, 0
+    for bit in reversed(range(dbits)):
+        mine = (me >> bit) & 1
+        if size >= 256:
+            size //= 2
+            there = pl.ds(pl.multiple_of(base + (1 - mine) * size, size), size)
+            base = base + mine * size
+        else:
+            there = pl.ds(pl.multiple_of(base, size), size)
+        here = pl.ds(pl.multiple_of(base, size), size)
+        hop = links.send(pg.at[:, there], prb[slot], "dp", bit)
+        hop.wait_recv()
+        links.sent_done(hop)
+        pg[:, here] += prb[slot][...]
+        slot += 1
+    for bit in range(tbits):
+        here = pl.ds(pl.multiple_of(base, size), size)
+        hop = links.send(pg.at[:, here], prb[slot], "tensor", bit)
+        hop.wait_recv()
+        links.sent_done(hop)
+        pg[:, here] += prb[slot][...]
+        slot += 1
+    pg_out[...] = pg[:, pl.ds(pl.multiple_of(base, size), size)]
+
+    for j in range(3):
+        u_q[j].drain()
+    for made in [u_o] + u_2 + u_1 + u_q:
+        made.hop.wait_recv()
+    y_copy.wait()
+    dx_copy.wait()
+    links.finish()
+
+
+def reduce_call(dbits, tbits, x, dy, params, back_sum, sums, gathered):
+    normed, back_rows, wq, w1, wo, w2, hidden_act, slope, attended, proj_back = gathered
+    count = 1 << dbits
+    blk = D // count
+    rows = x.shape[0]
+    tokens = normed.shape[0]
+    width, hidden = wo.shape[0], w2.shape[0]
+    total = 4 * width + 2 * hidden
+    half, quarter = tokens // 2, tokens // 4
+    any_spec = pl.BlockSpec(memory_space=pl.ANY)
+    vm = pl.BlockSpec(memory_space=pltpu.VMEM)
+    shape = lambda s, t=bf16: jax.ShapeDtypeStruct(s, t)
+    vmem = lambda s, t=bf16: pltpu.VMEM(s, t)
+    prb, size = [], D
+    for _ in range(dbits):
+        size = size // 2 if size >= 256 else size
+        prb.append(vmem((16, size), f32))
+    prb += [vmem((16, size), f32)] * tbits
+    outs = [
+        shape((rows, D)),
+        shape((rows, D), f32),
+        shape((total, blk), f32),
+        shape((total, blk)),
+        shape((16, size), f32),
+        shape((total, D // 2)),
+    ]
+    outs += [shape((half, D)), shape((quarter, D)), shape((rows, D))] * 2
+    outs += [shape((total, D >> (2 + k))) for k in range(dbits - 2)]
+    scratch = [
+        vmem((tokens, D)),
+        vmem((tokens, hidden)),
+        vmem((tokens, hidden)),
+        vmem((hidden, D)),
+        vmem((width, D)),
+        vmem((D, 3 * width)),
+        vmem((tokens, width)),
+        vmem((tokens, 3 * width)),
+        vmem((total, D // 2)),
+        vmem((total, D // 2)),
+        vmem((total, blk)),
+        vmem((512, blk), f32),
+        vmem((quarter, D)),
+        vmem((quarter, D)),
+        vmem((rows, D)),
+        vmem((quarter, D)),
+        vmem((rows, D), f32),
+        vmem((16, D), f32),
+        vmem((8, hidden), f32),
+        pltpu.SemaphoreType.DMA((80,)),
+        pltpu.SemaphoreType.DMA((80,)),
+        pltpu.SemaphoreType.DMA((96,)),
+    ] + prb
+    return pl.pallas_call(
+        functools.partial(reduce_kernel, (dbits, tbits)),
+        out_shape=outs,
+        in_specs=[vm] * 5 + [any_spec] * 10,
+        out_specs=[any_spec] * 4 + [vm] + [any_spec] * (len(outs) - 5),
+        scratch_shapes=scratch,
+        compiler_params=pltpu.CompilerParams(
+            vmem_limit_bytes=62 * 2**20, collective_id=1, has_side_effects=True
+        ),
+        cost_estimate=pl.CostEstimate(flops=5 * 10**10, bytes_accessed=10**8, transcendentals=10**6),
+        name="reduce",
+    )(x, dy, params, back_sum, sums, *gathered)
+
+
+def adam_kernel(turned, split, me_ref, w_ref, m_ref, v_ref, own_ref, recv_ref, wo_ref, mo_ref, vo_ref):
     sub = (me_ref[0] >> SUB_BIT) & 1
-    own = ka_ref[...].astype(f32) + kb_ref[...].astype(f32)
-    other = r_ref[...].astype(f32)
-    if split_rows:
-        grad = jnp.where(pl.program_id(0) // parts == sub, own, other)
-    else:
-        grad = jnp.concatenate([jnp.where(sub == 0, own, other), jnp.where(sub == 0, other, own)], axis=1)
+    grad = jnp.where(pl.program_id(0) // split == sub, own_ref[...], recv_ref[...].astype(f32))
+    grad = grad.T if turned else grad
     grad = grad.reshape(w_ref.shape)
     wo_ref[...], mo_ref[...], vo_ref[...] = adam_update(
         w_ref[...], m_ref[...], v_ref[...], grad, matrix_rate, weight_decay
     )
 
 
-def adam_call(me, weight, first, second, keep_a, keep_b, recv, split_rows):
+def adam_call(me, weight, first, second, own, recv, start, rows, turned):
     shape = weight.shape
-    parts = 1
+    blk = own.shape[1]
     if len(shape) == 3:
-        grid = shape[0]
-        full = pl.BlockSpec((1,) + shape[1:], lambda i: (i, 0, 0))
-        part = pl.BlockSpec((shape[1], shape[2] // 2), lambda i: (0, i))
-    elif split_rows:
-        block = min(512, shape[0] // 2)
-        grid = shape[0] // block
-        parts = grid // 2
-        full = pl.BlockSpec((block, shape[1]), lambda i: (i, 0))
-        part = pl.BlockSpec((block, shape[1]), lambda i: (i % parts, 0))
+        split = shape[0]
+        full = pl.BlockSpec((1, blk, rows), lambda i: (i % split, 0, i // split))
+    elif turned:
+        split = shape[1] // (2 * rows)
+        full = pl.BlockSpec((blk, rows), lambda i: (0, i))
     else:
-        block = 64
-        grid = shape[0] // block
-        full = pl.BlockSpec((block, shape[1]), lambda i: (i, 0))
-        part = pl.BlockSpec((block, shape[1] // 2), lambda i: (i, 0))
+        split = shape[0] // (2 * rows)
+        full = pl.BlockSpec((rows, blk), lambda i: (i, 0))
+    part = pl.BlockSpec((rows, blk), lambda i: (start // rows + i % split, 0))
     return tuple(
         pl.pallas_call(
-            functools.partial(adam_kernel, split_rows, parts),
-            grid=(grid,),
+            functools.partial(adam_kernel, turned, split),
+            grid=(2 * split,),
             out_shape=[jax.ShapeDtypeStruct(shape, f32)] * 3,
-            in_specs=[smem_spec()] + [full] * 3 + [part] * 3,
+            in_specs=[smem_spec()] + [full] * 3 + [part] * 2,
             out_specs=[full] * 3,
             compiler_params=vmem_params(32),
             name="adam",
-        )(me, weight, first, second, keep_a, keep_b, recv)
+        )(me, weight, first, second, own, recv)
     )
 
 
@@ -829,93 +1141,21 @@
         dbits, tbits, inputs, cotangent, ids, small_low, qkv_weight, expand_weight, dense_weight, shrink_weight
     )
     width, hidden = dense_full.shape[0], shrink_full.shape[0]
-    tokens = normed.shape[0]
-    head_start = t_me * (2 * width) + sub * width
-    hidden_start = t_me * (2 * hidden) + sub * hidden
-    qkv_bias_grad = sums[0].reshape(3, width)
-
-    def scatter_tokens(partial, gate):
-        half = tokens // 2
-        first = partial(half, tokens, gate).astype(bf16)
-        recv = exchange(first, "tensor", 0)
-        part = (partial(0, half, first) + recv.astype(f32)).astype(bf16)
-        done = part
-        for bit in range(1, tbits):
-            half = half // 2
-            recv = exchange(part[half:], "tensor", bit)
-            part = (part[:half].astype(f32) + recv.astype(f32)).astype(bf16)
-        return part[:rows], exchange(part[rows:], "dp", SUB_BIT), done
-
-    def scatter_weight(partial, gather_axis, gate):
-        cut = functools.partial(lax.slice_in_dim, axis=gather_axis)
-        first = partial(1, gate).astype(bf16)
-        recv = exchange(first, "dp", ROW_BIT)
-        part = (partial(0, first) + recv.astype(f32)).astype(bf16)
-        done = part
-        for bit in reversed(high_bits[1:]):
-            half = part.shape[gather_axis] // 2
-            recv = exchange(cut(part, half, 2 * half), "dp", bit)
-            part = (cut(part, 0, half).astype(f32) + recv.astype(f32)).astype(bf16)
-        half = part.shape[gather_axis] // 2
-        recv = exchange(cut(part, half, 2 * half), "dp", high_bits[0])
-        keep_a, keep_b = cut(part, 0, half // 2), cut(recv, 0, half // 2)
-        send = (cut(part, half // 2, half).astype(f32) + cut(recv, half // 2, half).astype(f32)).astype(bf16)
-        return (keep_a, keep_b, exchange(send, "dp", SUB_BIT)), done
-
-    halves = [slice(0, D // 2), slice(D // 2, D)]
-
-    def branch(start, stop, gate):
-        lhs = after(attended, gate)
-        return jnp.dot(lhs[start:stop], dense_full, preferred_element_type=f32) + jnp.dot(
-            hidden_act[start:stop], shrink_full, preferred_element_type=f32
-        )
-
-    keep, recv, done = scatter_tokens(branch, normed)
-    output = out_call(order, me, inputs, keep, recv, params[5:7])
-
-    def weight_part(left, right, spec, on_right):
-        def partial(i, gate):
-            if on_right:
-                return jnp.einsum(spec, after(left, gate), right[:, halves[i]], preferred_element_type=f32)
-            return jnp.einsum(spec, left[:, halves[i]], after(right, gate), preferred_element_type=f32)
-
-        return partial
-
-    dense_parts, done = scatter_weight(weight_part(attended, back_rows, "sk,sd->kd", True), 1, done)
-    shrink_parts, done = scatter_weight(weight_part(hidden_act, back_rows, "sf,sd->fd", True), 1, done)
-    act_back = jnp.einsum("sd,fd->sf", after(back_rows, done), shrink_full, preferred_element_type=f32)
-    pre_back = (act_back * gelu_slope.astype(f32)).astype(bf16)
-    expand_bias_grad = jnp.sum(pre_back, axis=0, dtype=f32)
-    expand_parts, done = scatter_weight(weight_part(normed, pre_back, "sd,sf->df", False), 0, pre_back)
-
-    def normed_back(start, stop, gate):
-        return jnp.einsum(
-            "se,de->sd", after(proj_back, gate)[start:stop], qkv_wide, preferred_element_type=f32
-        ) + jnp.einsum("sf,df->sd", pre_back[start:stop], expand_full, preferred_element_type=f32)
-
-    keep, recv, done = scatter_tokens(normed_back, done)
-    input_grad, gain_shift = norm_back_call(order, me, inputs, cotangent, keep, recv, params[0:1])
-    qkv_parts, done = scatter_weight(weight_part(normed, proj_back, "sd,se->de", False), 0, done)
-
-    qkv_rows = lax.dynamic_update_slice_in_dim(jnp.zeros((3, D), f32), qkv_bias_grad, head_start, 1)
-    expand_rows = lax.dynamic_update_slice_in_dim(
-        jnp.zeros((FF,), f32), expand_bias_grad, hidden_start, 0
-    ).reshape(FF // D, D)
-    params_grad = jnp.concatenate([gain_shift, qkv_rows, back_sum, back_sum, expand_rows], axis=0)
-    part = params_grad
-    for bit in reversed(range(dbits)):
-        half = part.shape[1] // 2
-        mine = (d_me >> bit) & 1
-        send = lax.dynamic_slice_in_dim(part, (1 - mine) * half, half, 1)
-        part = lax.dynamic_slice_in_dim(part, mine * half, half, 1) + exchange(send, "dp", bit)
-    for bit in range(tbits):
-        part = part + exchange(part, "tensor", bit)
-
-    dense_new = adam_call(me, dense_weight, dense_first, dense_second, *dense_parts, True)
-    shrink_new = adam_call(me, shrink_weight, shrink_first, shrink_second, *shrink_parts, True)
-    expand_new = adam_call(me, expand_weight, expand_first, expand_second, *expand_parts, False)
-    qkv_new = adam_call(me, qkv_weight, qkv_first, qkv_second, *qkv_parts, False)
-    small_new = adam_update(small_params, small_first, small_second, part, vector_rate, 0.0)
+    gathered = (
+        normed, back_rows, qkv_wide, expand_full, dense_full, shrink_full, hidden_act, gelu_slope, attended, proj_back,
+    )
+    output, input_grad, own, recv, small_sum, *_ = reduce_call(
+        dbits, tbits, inputs, cotangent, params, back_sum, sums, gathered
+    )
+    blk = D // dp
+    if small_sum.shape[1] > blk:
+        small_sum = lax.dynamic_slice_in_dim(small_sum, (d_me % (small_sum.shape[1] // blk)) * blk, blk, 1)
+    small_sum = small_sum[: small_params.shape[0]]
+    dense_new = adam_call(me, dense_weight, dense_first, dense_second, own, recv, 0, width, False)
+    shrink_new = adam_call(me, shrink_weight, shrink_first, shrink_second, own, recv, width, width, False)
+    expand_new = adam_call(me, expand_weight, expand_first, expand_second, own, recv, width + hidden, width, True)
+    qkv_new = adam_call(me, qkv_weight, qkv_first, qkv_second, own, recv, width + 2 * hidden, width, True)
+    small_new = adam_update(small_params, small_first, small_second, small_sum, vector_rate, 0.0)
     return (output, input_grad) + qkv_new + dense_new + expand_new + shrink_new + small_new
 
 

time: 704 us -> 525 us (0.75)
  waiting for transfers between devices: 260 us -> 0 us
  Pallas kernels: 271 us -> 500 us
  matrix products: 105 us -> 0 us
  starting transfers between devices: 27.7 us -> 0 us
  local copies, waits for them, and re-layouts: 22.7 us -> 13.9 us
    ppermute x23 -> x0, waiting for transfers between devices: 260 us -> none  [exchange(): return lax.ppermute(values, axis, [(i, i ^ 1 << bit) for i in range(count)])]
    pallas_call x6 -> x5, Pallas kernels: 23.7 us -> 254 us  [the longest x1 236 us: reduce_call(): pl.pallas_call(functools.partial(reduce_kernel, (dbits, tbits)), out_shap...]
    dot_general x17 -> x0, matrix products: 105 us -> none  [the longest x4 26.8 us: partial(): jnp.einsum(spec, left[:, halves[i]], after(right, gate), preferred_elemen...]
    ppermute x23 -> x0, starting transfers between devices: 27.7 us -> none  [exchange(): return lax.ppermute(values, axis, [(i, i ^ 1 << bit) for i in range(count)])]
    slice x19 -> x0, local copies, waits for them, and re-layouts: 17.1 us -> none  [the longest x4 5.3 us: scatter_weight(): recv = exchange(cut(part, half, 2 * half), 'dp', high_bits[0])]
    unnamed x72 -> x46, local copies, waits for them, and re-layouts: 2.24 us -> 11.4 us
  transfers between devices with their start and end apart: 23 -> 0, of which waited for: 11 -> 0; matrix products, arithmetic and copies ran while one was open for 8% -> 0% of each run, Pallas kernels for 3% -> 0%
where the time goes in v3:
time: 525 us; the launch traced here: 517 us
  Pallas kernels  500 us (95%)
  local copies, waits for them, and re-layouts  13.9 us (3%)
    pallas_call x1, Pallas kernels, gather_call(): pl.pallas_call(functools.partial(gather_kernel, (dbits, tbits)), out_shap...  247 us
    pallas_call x1, Pallas kernels, reduce_call(): pl.pallas_call(functools.partial(reduce_kernel, (dbits, tbits)), out_shap...  236 us
    pallas_call x4, Pallas kernels, adam_call(): pl.pallas_call(functools.partial(adam_kernel, turned, split), grid=(2 * s...  17.6 us
    unnamed x46, local copies, waits for them, and re-layouts  11.4 us

profile of v3, /device:TPU:0, one launch (start us, length us, event | category | flops | bytes accessed | tf_op | source)
XLA Modules:
  0.0 516.8 jit_solution(1126716332860188193)
XLA Ops:
  0.7 0.7 convert_element_type.5
  1.4 0.6 pad.4.small_ref
  2.0 0.7 mul.38.freq_ref
  2.7 1.3 broadcast_in_dim.9.ids_ref
  3.9 246.9 %gather.1 = (bf16[2048,2048]{1,0:T(8,128)(2,1)}, bf16[2048,2048]{1,0:T(8,128)(2,1)}, bf16[2048,768]{1,0:T(8,128)(2,1)}, bf16[2048,1024]{1,0:T(8,128)(2,1)}, bf16...) custom-call(bf16[256,2048]{1,0:T(8,128)(2,1)} %x_ref.3, ...), custom_call_target="tpu_custom_call" | custom-call | flops 20000000000 | bytes 100000000 | tf_op jit(solution)/shard_map/gather/pallas_call | solution.py:677
  250.9 236.0 %reduce.1 = (bf16[256,2048]{1,0:T(8,128)(2,1)}, f32[256,2048]{1,0:T(8,128)}, f32[3072,256]{1,0:T(8,128)}, bf16[3072,256]{1,0:T(8,128)(2,1)}, f32[16,256]{1,0:T(8...) custom-call(bf16[256,2048]{1,0:T(8,128)(2,1)} %x_ref.3, ...), custom_call_target="tpu_custom_call" | custom-call | flops 49999998976 | bytes 100000000 | tf_op jit(solution)/shard_map/reduce/pallas_call | solution.py:1052
  486.9 0.1 pad_add_fusion.me_ref
  486.9 1.9 copy-done
  488.8 1.4 copy-done.2
  490.2 1.6 copy-done.4
  491.8 1.6 copy-done.5
  493.4 1.6 copy-done.6
  495.0 5.3 %adam.7 = (f32[2048,256]{1,0:T(8,128)}, f32[2048,256]{1,0:T(8,128)}, f32[2048,256]{1,0:T(8,128)}) custom-call(s32[2]{0:T(128)S(1)} %pad_add_fusion.me_ref, f32[2048,256]{1,0:T(8,128)S(1)} %copy-done.4, f32[2048,256]{1,0:T(8,128)S(1)} %copy-done.5, f32[2048,256]{1,0:T(8,128)S(1)} %copy-done.6, f32[3072,256]{1,0:T(8,128)S(1)} %copy-done, ...), custom_call_target="tpu_custom_call" | custom-call | tf_op jit(solution)/shard_map/adam/pallas_call | solution.py:1090
  500.3 0.0 copy-start.13
  500.3 0.0 copy-start.14
  500.4 5.7 %adam.6 = (f32[256,2048]{1,0:T(8,128)}, f32[256,2048]{1,0:T(8,128)}, f32[256,2048]{1,0:T(8,128)}) custom-call(s32[2]{0:T(128)S(1)} %pad_add_fusion.me_ref, f32[256,2048]{1,0:T(8,128)S(1)} %copy-done.7, f32[256,2048]{1,0:T(8,128)S(1)} %copy-done.8, f32[256,2048]{1,0:T(8,128)S(1)} %copy-done.9, f32[3072,256]{1,0:T(8,128)S(1)} %copy-done, ...), custom_call_target="tpu_custom_call" | custom-call | tf_op jit(solution)/shard_map/adam/pallas_call | solution.py:1090
  506.2 0.0 copy-start.12
  506.2 2.0 adam.5
  508.1 0.2 copy-done.11
  508.3 0.8 copy-done.12
  509.1 4.6 adam.4
  513.7 0.6 add_subtract_fusion
  514.4 1.0 copy.37
  515.3 1.3 copy.38
  (35 shorter events, 0.1 us)
Async XLA Ops:
  486.9 1.9 copy-start
  488.8 1.4 copy-start.2
  490.2 1.6 copy-start.4
  491.8 1.6 copy-start.5
  493.4 1.6 copy-start.6
  495.0 5.3 %copy-start.7 = (f32[256,2048]{1,0:T(8,128)S(1)}, f32[256,2048]{1,0:T(8,128)}, u32[]{:S(2)}) copy-start(f32[256,2048]{1,0:T(8,128)} %w_ref.6) | copy-start | bytes 6291460
  495.0 5.3 %copy-start.8 = (f32[256,2048]{1,0:T(8,128)S(1)}, f32[256,2048]{1,0:T(8,128)}, u32[]{:S(2)}) copy-start(f32[256,2048]{1,0:T(8,128)} %m_ref.6) | copy-start | bytes 6291460
  495.0 5.3 %copy-start.9 = (f32[256,2048]{1,0:T(8,128)S(1)}, f32[256,2048]{1,0:T(8,128)}, u32[]{:S(2)}) copy-start(f32[256,2048]{1,0:T(8,128)} %v_ref.6) | copy-start | bytes 6291460
  500.3 5.8 %copy-start.1 = (f32[3072,256]{1,0:T(8,128)S(1)}, f32[3072,256]{1,0:T(8,128)}, u32[]{:S(2)}) copy-start(f32[3072,256]{1,0:T(8,128)} %get-tuple-element.62.own_ref) | copy-start | bytes 9437188
  500.3 5.8 %copy-start.3 = (bf16[3072,256]{1,0:T(8,128)(2,1)S(1)}, bf16[3072,256]{1,0:T(8,128)(2,1)}, u32[]{:S(2)}) copy-start(bf16[3072,256]{1,0:T(8,128)(2,1)} %get-tuple-element.63.recv_ref) | copy-start | bytes 4718596
  500.3 5.8 %copy-start.13 = (f32[512,256]{1,0:T(8,128)S(1)}, f32[512,256]{1,0:T(8,128)}, u32[]{:S(2)}) copy-start(f32[512,256]{1,0:T(8,128)} %w_ref.5) | copy-start | bytes 1572868
  500.3 5.8 %copy-start.14 = (f32[512,256]{1,0:T(8,128)S(1)}, f32[512,256]{1,0:T(8,128)}, u32[]{:S(2)}) copy-start(f32[512,256]{1,0:T(8,128)} %m_ref.5) | copy-start | bytes 1572868
  500.4 5.8 %copy-start.15 = (f32[512,256]{1,0:T(8,128)S(1)}, f32[512,256]{1,0:T(8,128)}, u32[]{:S(2)}) copy-start(f32[512,256]{1,0:T(8,128)} %v_ref.5) | copy-start | bytes 1572868
  506.1 2.0 copy-start.10
  506.2 2.1 copy-start.11
  506.2 2.9 copy-start.12
  509.1 4.6 copy-start.18
  509.1 4.6 copy-start.19
  509.1 4.6 copy-start.20
  509.1 4.6 copy-start.21
  509.1 5.3 %copy-start.17 = (bf16[256,2048]{1,0:T(8,128)(2,1)S(1)}, bf16[256,2048]{1,0:T(8,128)(2,1)}, u32[]{:S(2)}) copy-start(bf16[256,2048]{1,0:T(8,128)(2,1)} %get-tuple-element.97) | copy-start | bytes 3145732
  513.7 1.6 copy-start.16

commit v4 on v3

v4 whole, which is shorter than its diff:
```python
import functools
import jax
import numpy as np
import jax.numpy as jnp
from jax import lax
from jax.experimental import pallas as pl
from jax.experimental.pallas import tpu as pltpu
from jax.sharding import PartitionSpec as P

D = 2048
HD = 64
ROT = 32
FF = 8192
STEP = 10

norm_eps = 1e-05
beta_first = 0.9
beta_second = 0.95
adam_eps = 1e-08
weight_decay = 0.1
matrix_rate = 0.05
vector_rate = 1.0
masked_score = -1e30

SUB_BIT = 1
ROW_BIT = 0

bf16 = jnp.bfloat16
f32 = jnp.float32


def exchange(values, axis, bit):
    count = lax.axis_size(axis)
    return lax.ppermute(values, axis, [(i, i ^ (1 << bit)) for i in range(count)])


def place_order(count):
    bits = count.bit_length() - 1
    order = []
    for p in range(count):
        high = (p >> 1) & ((1 << (bits - 2)) - 1)
        order.append(((p & 1) << SUB_BIT) | (high << 2) | ((p >> (bits - 1)) << ROW_BIT))
    return order


def adam_update(weight, first, second, grad, rate, decay):
    first_new = beta_first * first + (1.0 - beta_first) * grad
    second_new = beta_second * second + (1.0 - beta_second) * grad * grad
    first_hat = first_new / (1.0 - beta_first**STEP)
    second_hat = second_new / (1.0 - beta_second**STEP)
    weight_new = weight - rate * (first_hat / (jnp.sqrt(second_hat) + adam_eps) + decay * weight)
    return (weight_new, first_new, second_new)


def after(values, *others):
    return lax.optimization_barrier((values,) + others)[0]


def gelu_value(pre_values):
    return jax.nn.gelu(pre_values, approximate=True)


def vmem_params(mib):
    return pltpu.CompilerParams(vmem_limit_bytes=mib * 2**20)


def place_of(block, count):
    bits = count.bit_length() - 1
    return ((block >> SUB_BIT) & 1) | ((block >> 2) << 1) | (((block >> ROW_BIT) & 1) << (bits - 1))


def move_blocks(count, source, load, store):
    width = D // count
    if width % 128 == 0:
        for j in range(count):
            start = pl.multiple_of(source(j) * width, width)
            store(pl.ds(j * width, width), load(pl.ds(start, width)))
        return
    for unit in range(count // 2):
        parts = []
        for half in range(2):
            block = source(2 * unit + half)
            value = load(pl.ds(pl.multiple_of((block >> 1) * 128, 128), 128))
            parts.append(pltpu.roll(value, ((block & 1) ^ half) * 64, 1))
        lane = lax.broadcasted_iota(jnp.int32, parts[0].shape, 1)
        store(pl.ds(unit * 128, 128), jnp.where(lane < 64, parts[0], parts[1]))


def smem_spec():
    return pl.BlockSpec(memory_space=pltpu.SMEM)


def assemble(order, me, keep_ref, recv_ref, tmp):
    count = len(order)

    def store(lanes, value):
        tmp[:, lanes] = value

    def add(lanes, value):
        tmp[:, lanes] += value

    move_blocks(count, lambda j: place_of(j ^ me, count), lambda lanes: keep_ref[:, lanes].astype(f32), store)
    move_blocks(count, lambda j: place_of(j ^ me, count) ^ 1, lambda lanes: recv_ref[:, lanes].astype(f32), add)


def swap_rotary(values):
    lane = lax.broadcasted_iota(jnp.int32, values.shape, 1)
    half = ROT // 2
    return jnp.where(
        lane % ROT < half, pltpu.roll(values, 128 - half, 1), pltpu.roll(values, half, 1)
    )


def dot_nn(a, b):
    return lax.dot_general(a, b, (((1,), (0,)), ((), ())), preferred_element_type=f32)


def dot_nt(a, b):
    return lax.dot_general(a, b, (((1,), (1,)), ((), ())), preferred_element_type=f32)


def dot_tn(a, b):
    return lax.dot_general(a, b, (((0,), (0,)), ((), ())), preferred_element_type=f32)


def rel_index(rel, seq, tbits):
    index = seq
    for b in range(tbits):
        index = index | (((rel >> b) & 1) << (tbits - b))
    return index


def mask_bias(bias, start_row, qb, rows):
    kend = (qb + 1) * rows
    key = lax.broadcasted_iota(jnp.int32, (kend, rows), 0)
    query = lax.broadcasted_iota(jnp.int32, (kend, rows), 1) + qb * rows
    bias[:kend, :] = jnp.where((key >= start_row) & (key <= query), 0.0, masked_score)


def attend_rows(qkv, lse, bias, o, seq, qb, width, out_rows):
    rows = bias.shape[1]
    kend = (qb + 1) * rows
    place = slice(qb * rows, kend)
    lane = lax.broadcasted_iota(jnp.int32, (rows, 128), 1)
    zero = jnp.zeros((rows, 128), bf16)

    def pair_body(pair, carry):
        base = pl.multiple_of(pair * 128, 128)
        q = qkv[seq, place, pl.ds(base, 128)] * jnp.asarray(HD ** (-0.5), bf16)
        k = qkv[seq, :kend, pl.ds(base + width, 128)]
        v = qkv[seq, :kend, pl.ds(base + 2 * width, 128)]
        vt = v.T
        outs = []
        for h in range(2):
            mine = (lane < HD) if h == 0 else (lane >= HD)
            s = dot_nt(k, jnp.where(mine, q, zero)) + bias[:kend, :]
            peak = jnp.max(s, axis=0, keepdims=True)
            expo = jnp.exp(s - peak)
            total = jnp.sum(expo, axis=0, keepdims=True)
            weights = (expo * (1.0 / total)).astype(bf16)
            outs.append(dot_nn(vt[h * HD : (h + 1) * HD, :], weights))
            lse[seq, pl.ds(pair * 2 + h, 1), place] = peak + jnp.log(total)
        o[out_rows, pl.ds(base, 128)] = jnp.concatenate(outs, axis=0).T.astype(bf16)
        return carry

    lax.fori_loop(0, width // 128, pair_body, 0)


def attend_back_rows(qkv, lse, bias, do, cosb, sinb, dk, dv, dp, sums, seq, qb, width, out_rows):
    rows = bias.shape[1]
    kend = (qb + 1) * rows
    place = slice(qb * rows, kend)
    scale = HD ** (-0.5)
    lane = lax.broadcasted_iota(jnp.int32, (rows, 128), 1)
    zero = jnp.zeros((rows, 128), bf16)

    def pair_body(pair, carry):
        base = pl.multiple_of(pair * 128, 128)
        lanes = pl.ds(base, 128)
        q = qkv[seq, place, lanes]
        k = qkv[seq, :kend, pl.ds(base + width, 128)]
        v = qkv[seq, :kend, pl.ds(base + 2 * width, 128)]
        kt = k.T
        dout = do[out_rows, lanes]
        outs = []
        for h in range(2):
            mine = (lane < HD) if h == 0 else (lane >= HD)
            qm = jnp.where(mine, q, zero) * jnp.asarray(scale, bf16)
            dom = jnp.where(mine, dout, zero)
            s = dot_nt(k, qm) + bias[:kend, :]
            probs = jnp.exp(s - lse[seq, pl.ds(pair * 2 + h, 1), place])
            dprobs = dot_nt(v, dom)
            inner = jnp.sum(probs * dprobs, axis=0, keepdims=True)
            ds = (probs * (dprobs - inner)).astype(bf16)
            dv[:kend, lanes] += dot_nn(probs.astype(bf16), dom)
            dk[:kend, lanes] += dot_nn(ds, qm)
            outs.append(dot_nn(kt[h * HD : (h + 1) * HD, :], ds))
        dq = jnp.concatenate(outs, axis=0).T * scale
        dq = dq * cosb[seq, place, :] - swap_rotary(dq) * sinb[seq, place, :]
        dq = dq.astype(bf16)
        dp[out_rows, lanes] = dq
        sums[0:1, lanes] += jnp.sum(dq.astype(f32), axis=0, keepdims=True)
        return carry

    lax.fori_loop(0, width // 128, pair_body, 0)


def attend_back_keys(cosb, sinb, dk, dv, dp, sums, seq, b, width, out_rows):
    rows = out_rows.size
    place = slice(b * rows, (b + 1) * rows)
    cosine = cosb[seq, place, :]
    sine = sinb[seq, place, :]
    for j in range(width // 128):
        lanes = slice(j * 128, (j + 1) * 128)
        part = dk[place, lanes]
        part = (part * cosine - swap_rotary(part) * sine).astype(bf16)
        kl = slice(width + j * 128, width + (j + 1) * 128)
        dp[out_rows, kl] = part
        sums[0:1, kl] += jnp.sum(part.astype(f32), axis=0, keepdims=True)
        part = dv[place, lanes].astype(bf16)
        vl = slice(2 * width + j * 128, 2 * width + (j + 1) * 128)
        dp[out_rows, vl] = part
        sums[0:1, vl] += jnp.sum(part.astype(f32), axis=0, keepdims=True)


class Links:
    def __init__(self, send_sems, recv_sems, local_sems):
        self.send_sems, self.recv_sems, self.local_sems = send_sems, recv_sems, local_sems
        self.sent, self.count, self.locals = [], 0, 0

    def send(self, src, dst, axis, bit):
        partner = lax.axis_index(axis) ^ (1 << bit)
        i = self.count
        self.count += 1
        copy = pltpu.make_async_remote_copy(
            src_ref=src,
            dst_ref=dst,
            send_sem=self.send_sems.at[i],
            recv_sem=self.recv_sems.at[i],
            device_id={axis: partner},
            device_id_type=pl.DeviceIdType.MESH,
        )
        copy.start()
        self.sent.append(copy)
        return copy

    def local(self, src, dst):
        copy = pltpu.make_async_copy(src, dst, self.local_sems.at[self.locals])
        self.locals += 1
        copy.start()
        return copy

    def local_wait(self, src, dst):
        self.local(src, dst).wait()

    def sent_done(self, copy):
        copy.wait_send()
        self.sent = [other for other in self.sent if other is not copy]

    def finish(self):
        for copy in self.sent:
            copy.wait_send()


def greet(dbits, tbits):
    barrier = pltpu.get_barrier_semaphore()
    partners = [("dp", b) for b in range(dbits)] + [("tensor", b) for b in range(tbits)]
    for axis, bit in partners:
        pl.semaphore_signal(
            barrier,
            inc=1,
            device_id={axis: lax.axis_index(axis) ^ (1 << bit)},
            device_id_type=pl.DeviceIdType.MESH,
        )
    pl.semaphore_wait(barrier, len(partners))


class Gathered:
    def __init__(self, links, slot, count, bits, outgoing):
        self.links, self.slot, self.bits, self.outgoing = links, slot, bits, outgoing
        self.left = count - 1
        self.coming = {}

    def source(self, p):
        size = 1 << (p.bit_length() - 1)
        return p - size, self.bits[p.bit_length() - 1]

    def send(self, p):
        src, bit = self.source(p)
        ref = self.outgoing if p == 1 else self.slot(src)
        self.coming[p] = self.links.send(ref, self.slot(p), "dp", bit)

    def wait(self, p):
        self.coming[p].wait_recv()
        self.left -= 1


class GatheredPairs(Gathered):
    def __init__(self, links, slot, count, bits, outgoing, own, received):
        super().__init__(links, slot, count, bits, outgoing)
        self.own, self.received = own, received

    def send(self, p):
        src, bit = self.source(p)
        if p == 1:
            self.coming[p] = self.links.send(self.outgoing, self.received, "dp", bit)
        elif p % 2 == 0 and src > 0:
            self.coming[p] = self.links.send(self.slot(src // 2), self.slot(p // 2), "dp", bit)

    def wait(self, p):
        if p == 1:
            self.coming[p].wait_recv()
            both = [self.own[...].astype(f32), self.received[...].astype(f32)]
            self.slot(0)[...] = jnp.concatenate(both, axis=1).astype(bf16)
            for later in range(1, len(self.bits)):
                bit = self.bits[later]
                self.coming[1 << later] = self.links.send(self.slot(0), self.slot(1 << (later - 1)), "dp", bit)
        elif p % 2 == 0:
            self.coming[p].wait_recv()
        self.left -= 1


def cast_store(dst, src):
    dst[...] = src[...].astype(bf16)


def gather_kernel(
    cfg,
    x_ref, dy_ref, ids_ref, small_ref, freq_ref, qkv_ref, w1_ref, wo_ref, w2_ref,
    n_out, dy_out, wq_out, w1_out, wo_out, w2_out, h_out, gp_out, o_out, dp_out, params_out, dysum_out, sums_out,
    n, dyb, wq, w1, wo, w2, sq, s1, so, s2, sta, stb, stc, std, tmp, nsw, pbuf, idb, cosb, sinb, startb,
    qkvb, lse, bias, o, do, dk, dv, dp, hst, gst, send_sems, recv_sems, local_sems, *pieces
):
    dbits, tbits = cfg
    order = place_order(1 << dbits)
    count = len(order)
    me = lax.axis_index("dp")
    me_t = lax.axis_index("tensor")
    sub = (me >> SUB_BIT) & 1
    rows = x_ref.shape[0]
    width = wo.shape[0]
    hidden = w2.shape[0]
    blk = D // count
    seqs = 2
    blocks = 1 << tbits
    length = rows * blocks
    links = Links(send_sems, recv_sems, local_sems)
    bits = [SUB_BIT] + list(range(2, dbits)) + [ROW_BIT]

    own_q = pl.ds(pl.multiple_of(sub * width, width), width)
    other_q = pl.ds(pl.multiple_of((1 - sub) * width, width), width)
    own_h = pl.ds(pl.multiple_of(sub * hidden, hidden), hidden)
    other_h = pl.ds(pl.multiple_of((1 - sub) * hidden, hidden), hidden)
    loads = {"q": [], "1": [], "2": [], "o": []}
    for j in range(3):
        lanes = pl.ds(j * width, width)
        loads["q"].append(links.local(qkv_ref.at[j, :, other_q], std.at[:, lanes]))
        loads["q"].append(links.local(qkv_ref.at[j, :, own_q], stc.at[:, lanes]))
    loads["2"].append(links.local(w2_ref.at[other_h, :], stb))
    loads["2"].append(links.local(w2_ref.at[own_h, :], sta))

    def row_gather(ref, outgoing):
        return Gathered(links, lambda p: ref.at[pl.ds(p * blk, blk), :], count, bits, outgoing)

    def column_gather(ref, outgoing, own, received):
        unit = max(blk, 128)
        slot = lambda p: ref.at[:, pl.ds(p * unit, unit)]
        if unit == blk:
            return Gathered(links, slot, count, bits, outgoing), slot(0)
        return GatheredPairs(links, slot, count, bits, outgoing, own, received), own

    gathers = {"q": row_gather(wq, sq), "1": row_gather(w1, s1)}
    gathers["o"], wo_own = column_gather(wo, so, *pieces[0:2])
    gathers["2"], w2_own = column_gather(w2, s2, *pieces[2:4])
    outs = {"q": (wq, wq_out), "1": (w1, w1_out), "o": (wo, wo_out), "2": (w2, w2_out), "n": (n, n_out), "d": (dyb, dy_out)}
    token_bufs = {"n": n, "d": dyb}
    token_left = {"n": 2 * blocks - 1, "d": 2 * blocks - 1}
    coming, stores, kept, attended, begun = {}, [], {}, set(), set()

    def tok(ref, i):
        return ref.at[pl.ds(i * rows, rows), :]

    def send(kind, i):
        if kind in gathers:
            gathers[kind].send(i)
        elif kind in token_bufs:
            ref = token_bufs[kind]
            if i == 1:
                coming[kind, i] = links.send(nsw, tok(ref, 1), "dp", SUB_BIT)
            else:
                step = i.bit_length() - 1
                coming[kind, i] = links.send(tok(ref, i - (1 << step)), tok(ref, i), "tensor", tbits - step)
        else:
            buf = pbuf if kind == "P" else idb
            axis, bit = ("dp", bits[i - 1]) if kind == "P" or i == 1 else ("tensor", tbits + 1 - i)
            size = 1 << (i - 1)
            coming[kind, i] = links.send(buf.at[pl.ds(0, size)], buf.at[pl.ds(size, size)], axis, bit)

    def wait(kind, i):
        if kind in gathers:
            gathers[kind].wait(i)
            complete = gathers[kind].left == 0
        else:
            coming[kind, i].wait_recv()
            complete = False
            if kind in token_bufs:
                token_left[kind] -= 1
                complete = token_left[kind] == 0
        if complete:
            stores.append(links.local(*outs[kind]))

    def arrived(name):
        for copy in loads[name]:
            copy.wait()

    def cast_q():
        arrived("q")
        sq[...] = std[:, 0 : 3 * width].astype(bf16)
        wq[0:blk, :] = stc[:, 0 : 3 * width].astype(bf16)
        loads["1"].append(links.local(w1_ref.at[:, other_h], std))
        loads["1"].append(links.local(w1_ref.at[:, own_h], stc))

    def cast_1():
        arrived("1")
        s1[...] = std[...].astype(bf16)
        w1[0:blk, :] = stc[...].astype(bf16)

    def cast_2():
        arrived("2")
        s2[...] = stb[...].astype(bf16)
        w2_own[...] = sta[...].astype(bf16)
        loads["o"].append(links.local(wo_ref.at[other_q, :], stb.at[pl.ds(0, width), :]))
        loads["o"].append(links.local(wo_ref.at[own_q, :], sta.at[pl.ds(0, width), :]))

    def cast_o():
        arrived("o")
        so[...] = stb[0:width, :].astype(bf16)
        wo_own[...] = sta[0:width, :].astype(bf16)

    def statistics():
        x = x_ref[...].astype(f32)
        x = x - jnp.mean(x, axis=-1, keepdims=True)
        inv = lax.rsqrt(jnp.mean(x * x, axis=-1, keepdims=True) + norm_eps)
        tmp[...] = x * inv

    def store_to(ref):
        def store(lanes, value):
            ref[0:rows, lanes] = value.astype(bf16)

        return store

    load_tmp = lambda lanes: tmp[:, lanes]
    load_dy = lambda lanes: dy_ref[:, lanes].astype(f32)

    def norm():
        per = max(1, 128 // blk)
        for a in range(0, count, per):
            part = [pbuf[place_of((a + k) ^ me, count)].astype(f32) for k in range(per)]
            lanes = pl.ds(a * blk, per * blk)
            params_out[:, lanes] = part[0] if per == 1 else jnp.concatenate(part, axis=1)
        tmp[...] = tmp[...] * params_out[0:1, :] + params_out[1:2, :]
        move_blocks(count, lambda j: me ^ order[j ^ 1], load_tmp, store_to(nsw))
        move_blocks(count, lambda j: me ^ order[j], load_tmp, store_to(n))

    def back_own():
        move_blocks(count, lambda j: me ^ order[j], load_dy, store_to(dyb))
        dysum_out[...] = jnp.sum(dy_ref[...].astype(f32), axis=0, keepdims=True)

    def back_swapped():
        links.sent_done(coming["n", 1])
        move_blocks(count, lambda j: me ^ order[j ^ 1], load_dy, store_to(nsw))

    def tables():
        for seq in range(seqs):
            row = jnp.concatenate(
                [idb[rel_index(me_t ^ b, seq, tbits)][0:1, :] for b in range(blocks)], axis=1
            ).astype(f32)
            first = jnp.sum(jnp.where(row < 1.0, 1.0, 0.0), axis=1, keepdims=True)
            second = jnp.sum(jnp.where(row < 2.0, 1.0, 0.0), axis=1, keepdims=True)
            begin = jnp.where(row < 1.0, 0.0, jnp.where(row < 2.0, first, second))
            place = lax.broadcasted_iota(jnp.int32, (1, length), 1).astype(f32)
            startb[seq, 0:1, :] = begin.astype(jnp.int32)
            angle = freq_ref[:, 0:1] * (place - begin)
            cosine, sine = jnp.cos(angle), jnp.sin(angle)
            rest = (HD - ROT, length)
            cosine = jnp.concatenate([cosine, cosine, jnp.ones(rest, f32)], axis=0)
            sine = jnp.concatenate([-sine, sine, jnp.zeros(rest, f32)], axis=0)
            cosb[seq] = jnp.concatenate([cosine, cosine], axis=0).T
            sinb[seq] = jnp.concatenate([sine, sine], axis=0).T

    head_start = me_t * (2 * width) + sub * width
    hidden_start = me_t * (2 * hidden) + sub * hidden
    pairs = width // 128

    def two_blocks(c):
        return pl.ds(2 * c * rows, 2 * rows)

    def project(c):
        lanes = pl.ds(pl.multiple_of(head_start, width), width)
        qkv_bias = [params_out[2 + j : 3 + j, lanes] for j in range(3)]
        rel = sum(((c >> (tbits - 1 - b)) & 1) << b for b in range(tbits))
        block = me_t ^ rel
        place = pl.ds(pl.multiple_of(block * rows, rows), rows)
        part = dot_nn(n[two_blocks(c), :], wq[...])
        for seq in range(seqs):
            seq_rows = slice(seq * rows, (seq + 1) * rows)
            cosine, sine = cosb[seq, place, :], sinb[seq, place, :]
            for j in range(3 * pairs):
                kind, pair = j // pairs, j % pairs
                value = part[seq_rows, j * 128 : (j + 1) * 128] + qkv_bias[kind][:, pair * 128 : (pair + 1) * 128]
                if kind < 2:
                    value = value * cosine + swap_rotary(value) * sine
                qkvb[seq, place, j * 128 : (j + 1) * 128] = value.astype(bf16)

    def seq_rows_of(seq, b):
        return pl.ds(pl.multiple_of(rel_index(me_t ^ b, seq, tbits) * rows, rows), rows)

    def attend(seq, qb):
        mask_bias(bias, startb[seq, 0:1, qb * rows : (qb + 1) * rows], qb, rows)
        attend_rows(qkvb, lse, bias, o, seq, qb, width, seq_rows_of(seq, qb))
        attended.add((seq, qb))
        if len(attended) == seqs * blocks:
            stores.append(links.local(o, o_out))

    def attend_back(seq, qb):
        if seq not in begun:
            begun.add(seq)
            dk[...] = jnp.zeros_like(dk)
            dv[...] = jnp.zeros_like(dv)
        mask_bias(bias, startb[seq, 0:1, qb * rows : (qb + 1) * rows], qb, rows)
        attend_back_rows(
            qkvb, lse, bias, do, cosb, sinb, dk, dv, dp, sums_out, seq, qb, width, seq_rows_of(seq, qb)
        )

    def attend_keys(seq):
        for b in range(blocks):
            attend_back_keys(cosb, sinb, dk, dv, dp, sums_out, seq, b, width, seq_rows_of(seq, b))

    tile = hst.shape[2]

    def hide(c):
        row = 7 + hidden_start // D
        hidden_bias = params_out[pl.ds(row, 1), pl.ds(pl.multiple_of(hidden_start % D, hidden), hidden)]
        for t in range(hidden // tile):
            lanes = pl.ds(t * tile, tile)
            slot = t % 2
            for copy in kept.pop(slot, ()):
                copy.wait()
            v = dot_nn(n[two_blocks(c), :], w1[:, lanes]) + hidden_bias[:, t * tile : (t + 1) * tile]
            root = 0.7978845608028654
            square = v * v
            th = jnp.tanh(root * (v + 0.044715 * v * square))
            hst[slot] = (0.5 * v * (1.0 + th)).astype(bf16)
            gst[slot] = (
                0.5 * (1.0 + th) + 0.5 * v * (1.0 - th * th) * (root * (1.0 + (3 * 0.044715) * square))
            ).astype(bf16)
            kept[slot] = (
                links.local(hst.at[slot], h_out.at[two_blocks(c), lanes]),
                links.local(gst.at[slot], gp_out.at[two_blocks(c), lanes]),
            )

    def output_back(c):
        do[two_blocks(c), :] = dot_nt(dyb[two_blocks(c), :], wo[...]).astype(bf16)

    def end():
        stores.append(links.local(dp, dp_out))
        for copies in kept.values():
            stores.extend(copies)
        for copy in stores:
            copy.wait()
        links.finish()

    pbuf[0] = small_ref[...]
    idb[0] = ids_ref[...]
    sums_out[...] = jnp.zeros_like(sums_out)
    greet(dbits, tbits)
    steps = {
        "castq": cast_q, "cast1": cast_1, "cast2": cast_2, "casto": cast_o, "stat": statistics, "ln": norm,
        "dyr": back_own, "dys": back_swapped, "table": tables, "end": end,
    }
    indexed = {"Q": project, "A": attend, "B": attend_back, "K": attend_keys, "H": hide, "D": output_back}
    for name in gather_schedule(count, blocks):
        if name in steps:
            steps[name]()
        elif name[0] == "S":
            send(name[1], int(name[2:]))
        elif name[0] == "W":
            wait(name[1], int(name[2:]))
        else:
            indexed[name[0]](*[int(i) for i in name[1:]])


GATHER_ORDER = [
    6, 0, 14, 29, 1, 2, 30, 7, 75, 90, 91, 93, 8, 12, 44, 3, 4, 5, 9, 31, 13, 78, 32, 34, 15, 47, 94, 33, 45,
    16, 49, 63, 35, 36, 21, 40, 48, 10, 18, 11, 22, 101, 37, 38, 86, 19, 20, 17, 46, 61, 42, 25, 27, 41, 62,
    43, 50, 23, 51, 39, 57, 53, 52, 54, 26, 105, 92, 24, 76, 107, 28, 108, 96, 106, 112, 95, 116, 55, 56,
    111, 113, 77, 110, 67, 64, 58, 97, 65, 59, 98, 114, 115, 66, 60, 119, 99, 100, 68, 117, 103, 120, 102,
    73, 79, 80, 81, 109, 104, 72, 69, 82, 121, 70, 118, 71, 123, 74, 122, 83, 124, 126, 128, 127, 125, 129,
    84, 88, 85, 131, 130, 132, 133, 134, 87, 89, 135,
]


def gather_schedule(count, blocks):
    names = []

    def take(kind, places, first):
        def push(p):
            size = first
            while size < places:
                if p < size:
                    names.append("S%s%d" % (kind, p + size))
                size *= 2

        names.append("S%s1" % kind)
        push(0)
        for p in range(1, places):
            names.append("W%s%d" % (kind, p))
            push(p)

    for i in range(1, count.bit_length()):
        names.extend(["SP%d" % i, "WP%d" % i])
    for i in range(1, blocks.bit_length() + 1):
        names.extend(["SI%d" % i, "WI%d" % i])
    names.extend(["stat", "ln", "castq"])
    take("n", 2 * blocks, 2)
    take("q", count, 2)
    names.extend(["table", "cast1", "dyr", "dys"])
    take("1", count, 2)
    take("d", 2 * blocks, 2)
    names.append("cast2")
    take("2", count, 2)
    names.append("casto")
    take("o", count, 2)
    names.extend("Q%d" % c for c in range(blocks))
    names.extend("A%d%d" % (s, b) for s in range(2) for b in range(blocks))
    names.extend("H%d" % c for c in range(blocks))
    names.extend("D%d" % c for c in range(blocks))
    for s in range(2):
        names.extend("B%d%d" % (s, b) for b in range(blocks))
        names.append("K%d" % s)
    names.append("end")
    if (count, blocks) == (8, 4):
        return [names[i] for i in GATHER_ORDER]
    return names


def gather_call(dbits, tbits, x, dy, ids, small, qkv_weight, expand_weight, dense_weight, shrink_weight):
    count = 1 << dbits
    blk = D // count
    rows = x.shape[0]
    width = qkv_weight.shape[2] // 2
    hidden = expand_weight.shape[1] // 2
    tokens = rows * (2 << tbits)
    length = rows << tbits
    heads = width // HD
    half = ROT // 2
    powers = (10000.0 ** (-np.arange(half) / half)).astype(np.float32)
    freqs = jnp.asarray(np.repeat(powers[:, None], 128, axis=1))
    any_spec = pl.BlockSpec(memory_space=pl.ANY)
    vm = pl.BlockSpec(memory_space=pltpu.VMEM)
    shape = lambda s, t=bf16: jax.ShapeDtypeStruct(s, t)
    vmem = lambda s, t=bf16: pltpu.VMEM(s, t)
    weights = 4 * (2 * count - 1) + 2 * 32 + 16
    scratch = [
        vmem((tokens, D)),
        vmem((tokens, D)),
        vmem((D, 3 * width)),
        vmem((D, hidden)),
        vmem((width, D)),
        vmem((hidden, D)),
        vmem((blk, 3 * width)),
        vmem((blk, hidden)),
        vmem((width, blk)),
        vmem((hidden, blk)),
        vmem((hidden, blk), f32),
        vmem((hidden, blk), f32),
        vmem((blk, hidden), f32),
        vmem((blk, hidden), f32),
        vmem((rows, D), f32),
        vmem((rows, D)),
        vmem((count, small.shape[0], blk)),
        vmem((2 << tbits, 8, rows), jnp.int32),
        vmem((2, length, 128), f32),
        vmem((2, length, 128), f32),
        vmem((2, 8, length), jnp.int32),
        vmem((2, length, 3 * width)),
        vmem((2, heads, length), f32),
        vmem((length, rows), f32),
        vmem((tokens, width)),
        vmem((tokens, width)),
        vmem((length, width), f32),
        vmem((length, width), f32),
        vmem((tokens, 3 * width)),
        vmem((2, 2 * rows, min(hidden, 512))),
        vmem((2, 2 * rows, min(hidden, 512))),
        pltpu.SemaphoreType.DMA((weights,)),
        pltpu.SemaphoreType.DMA((weights,)),
        pltpu.SemaphoreType.DMA((48,)),
    ]
    pieces = (vmem((width, blk)), vmem((hidden, blk)))
    scratch += [pieces[0]] * 2 + [pieces[1]] * 2 if blk % 128 else [vmem((16, 128))] * 4
    return pl.pallas_call(
        functools.partial(gather_kernel, (dbits, tbits)),
        out_shape=[
            shape((tokens, D)),
            shape((tokens, D)),
            shape((D, 3 * width)),
            shape((D, hidden)),
            shape((width, D)),
            shape((hidden, D)),
            shape((tokens, hidden)),
            shape((tokens, hidden)),
            shape((tokens, width)),
            shape((tokens, 3 * width)),
            shape((small.shape[0], D), f32),
            shape((1, D), f32),
            shape((8, 3 * width), f32),
        ],
        in_specs=[vm] * 5 + [any_spec] * 4,
        out_specs=[any_spec] * 10 + [vm] * 3,
        scratch_shapes=scratch,
        compiler_params=pltpu.CompilerParams(
            vmem_limit_bytes=62 * 2**20, collective_id=0, has_side_effects=True
        ),
        cost_estimate=pl.CostEstimate(flops=2 * 10**10, bytes_accessed=10**8, transcendentals=10**7),
        name="gather",
    )(x, dy, ids, small, freqs, qkv_weight, expand_weight, dense_weight, shrink_weight)


class Unit:
    def __init__(self, start, rows, lhs, first, rhs, send_start, frees):
        self.here, self.rows = pl.ds(start, rows), rows
        self.lhs, self.first, self.rhs = lhs, first, rhs
        self.out = pl.ds(send_start, rows)
        self.frees, self.hop, self.load, self.slot = frees, None, None, None


class TokenSum:
    def __init__(self, partial, far, near, keep, rc, rx, rs):
        self.partial, self.far, self.near, self.keep = partial, far, near, keep
        self.rc, self.rx, self.rs = rc, rx, rs
        self.hops = {}


def reduce_kernel(
    cfg,
    x_ref, dy_own_ref, params_ref, back_sum_ref, sums_ref,
    n_hbm, dy_hbm, wq_hbm, w1_hbm, wo_hbm, w2_hbm, h_hbm, gp_hbm, o_hbm, dp_hbm,
    y_out, dx_out, own_out, rl, pg_out, ry, rc1, rx1, rs1, rc2, rx2, rs2, *rest
):
    dbits, tbits = cfg
    highs = dbits - 2
    rz, rest = rest[:highs], rest[highs:]
    (
        big, hw1, gp, w2, wo, wq, o, dp, outgoing, keep, own, came, sx, kx, sz, sc, stage, tmp, pg, hsum,
        send_sems, recv_sems, local_sems, *rest
    ) = rest
    prb, last = rest[: dbits + tbits], rest[dbits + tbits :]
    order = place_order(1 << dbits)
    count = len(order)
    me = lax.axis_index("dp")
    me_t = lax.axis_index("tensor")
    sub = (me >> SUB_BIT) & 1
    rows = x_ref.shape[0]
    blk = D // count
    width, hidden = wo.shape[0], w2.shape[0]
    tokens = n_hbm.shape[0]
    links = Links(send_sems, recv_sems, local_sems)
    high_bits = list(range(2, dbits))
    side = D // 2
    half, quarter = tokens // 2, tokens // 4
    step_lanes = 512

    pending = {}

    def fetch(name, src, dst):
        pending.setdefault(name, []).append(links.local(src, dst))

    def need(*names):
        for name in names:
            for copy in pending.pop(name, ()):
                copy.wait()

    fetch("o", o_hbm, o)
    fetch("dy", dy_hbm, big)
    fetch("h", h_hbm, hw1)

    def load_more():
        fetch("w2", w2_hbm, w2)
        fetch("gp", gp_hbm, gp)
        fetch("dp", dp_hbm, dp)
        fetch("wq", wq_hbm, wq)
        fetch("wo", wo_hbm, wo)

    def load_n():
        for i in range(2):
            links.sent_done(sums["dn"].hops["c", i])
        for i in range(2):
            part = pl.ds(i * half, half)
            fetch("n", n_hbm.at[part, :], big.at[part, :])

    units = {"o": Unit(2 * hidden + 3 * width, width, o, 0, "dy", hidden + 3 * width, None)}
    per = hidden // width
    for i in range(per):
        at = i * width
        units["a%d" % i] = Unit(at, width, hw1, at, "dy", at, None)
        units["c%d" % i] = Unit(at + hidden, width, gp, at, "n", at, "a%d" % i)
    for j in range(3):
        at = hidden + j * width
        units["q%d" % j] = Unit(at + hidden, width, dp, j * width, "n", at, None)

    def product(unit, part):
        need(unit.rhs, *(["dp"] if unit.lhs is dp else ["h"] if unit.lhs is hw1 else ["o"]))
        lhs = unit.lhs[:, pl.ds(unit.first, unit.rows)]
        return dot_tn(lhs, big[:, pl.ds(part * side, side)]).astype(bf16)

    def away(unit):
        if unit.frees:
            links.sent_done(units[unit.frees].first_hop)
        outgoing[unit.out, :] = product(unit, 1)

    def home(unit):
        keep[unit.here, :] = product(unit, 0)

    def send_y(unit):
        unit.hop = links.send(outgoing.at[unit.out, :], ry.at[unit.here, :], "dp", ROW_BIT)
        unit.first_hop = unit.hop

    free = list(range(came.shape[0]))

    def load_received(unit, src):
        if free:
            unit.slot = free.pop()
            part = came.at[unit.slot, :, pl.ds(0, src.shape[1])]
            unit.load = links.local(src.at[unit.here, :], part)

    def add_received(unit, src):
        lanes = src.shape[1]
        value = keep[unit.here, 0:lanes].astype(f32)
        if unit.load is None:
            part = stage.at[pl.ds(0, unit.rows), pl.ds(0, lanes)]
            links.local_wait(src.at[unit.here, :], part)
            return value + part[...].astype(f32)
        unit.load.wait()
        unit.load = None
        free.append(unit.slot)
        return value + came[unit.slot, :, 0:lanes].astype(f32)

    def fold_first(unit):
        keep[unit.here, :] = add_received(unit, ry).astype(bf16)

    def send_high(unit, k=0):
        lanes = side >> (k + 1)
        part = keep.at[unit.here, pl.ds(lanes, lanes)]
        unit.hop = links.send(part, rz[k].at[unit.here, :], "dp", high_bits[highs - 1 - k])

    slots = []

    def fold_last(unit):
        for k in range(highs - 1):
            keep[unit.here, 0 : side >> (k + 1)] = add_received(unit, rz[k]).astype(bf16)
            send_high(unit, k + 1)
            unit.hop.wait_recv()
        value = add_received(unit, rz[highs - 1])
        slot = len(slots) % own.shape[0]
        if len(slots) >= own.shape[0]:
            slots[-own.shape[0]].wait()
        own[slot] = value[:, 0:blk]
        slots.append(links.local(own.at[slot], own_out.at[unit.here, :]))
        if last:
            last[0][unit.here, :] = value[:, blk : 2 * blk].astype(bf16)
        else:
            keep[unit.here, blk : 2 * blk] = value[:, blk : 2 * blk].astype(bf16)

    def send_sub(unit):
        part = last[0].at[unit.here, :] if last else keep.at[unit.here, pl.ds(blk, blk)]
        unit.hop = links.send(part, rl.at[unit.here, :], "dp", SUB_BIT)

    hsum[...] = jnp.zeros_like(hsum)

    def hidden_back(c):
        need("dy", "w2", "gp")
        place = pl.ds(c * quarter, quarter)
        for t in range(0, hidden, 512):
            lanes = slice(t, t + 512)
            value = (dot_nt(big[place, :], w2[lanes, :]) * gp[place, lanes].astype(f32)).astype(bf16)
            gp[place, lanes] = value
            hsum[0:1, lanes] += jnp.sum(value.astype(f32), axis=0, keepdims=True)

    def branch(place, lanes):
        return dot_nn(o[place, :], wo[:, lanes]) + dot_nn(hw1[place, :], w2[:, lanes])

    def normed_back(place, lanes):
        return dot_nt(dp[place, :], wq[lanes, :]) + dot_nt(gp[place, :], hw1[lanes, :])

    def part_rows(partial, first, dst, added):
        place = pl.ds(first, quarter)

        def body(t, carry):
            lanes = pl.ds(pl.multiple_of(t * step_lanes, step_lanes), step_lanes)
            value = partial(place, lanes)
            if added is not None:
                value = value + added[:, lanes].astype(f32)
            dst[:, lanes] = value.astype(bf16)
            return carry

        lax.fori_loop(0, D // step_lanes, body, 0)

    big_rows = lambda first: big.at[pl.ds(first, quarter), :]
    sums = {
        "dn": TokenSum(normed_back, (big_rows(half), big_rows(half + quarter)), sx, kx, rc1, rx1, rs1),
        "br": TokenSum(branch, (sc, sc), sc, sx, rc2, rx2, rs2),
    }

    def far_rows(t, i):
        need("wo", "w2", "o", "h") if t is sums["br"] else need("dp", "wq", "w1")
        if t is sums["br"] and i == 0:
            links.sent_done(t.hops["c", 1])
        part_rows(t.partial, half + i * quarter, t.far[i], None)

    def send_core(t, i):
        there = pl.ds(i * quarter, quarter)
        t.hops["c", i] = links.send(t.far[i], t.rc.at[there, :], "tensor", 0)

    def near_rows(t):
        if t is sums["br"]:
            links.sent_done(t.hops["c", 0])
        links.local_wait(t.rc.at[pl.ds(quarter, quarter), :], stage)
        part_rows(t.partial, quarter, t.near, stage)

    def send_x(t, i):
        part = pl.ds(i * rows, rows)
        t.hops["x", i] = links.send(t.near.at[part, :], t.rx.at[part, :], "tensor", 1)

    def keep_rows(t):
        if t is sums["br"]:
            for i in range(2):
                links.sent_done(sums["dn"].hops["x", i])
        links.local_wait(t.rc.at[pl.ds(0, quarter), :], stage)
        part_rows(t.partial, 0, t.keep, stage)

    def partner_rows(t):
        if t is sums["br"]:
            links.sent_done(sums["dn"].hops["s"])
        links.local_wait(t.rx.at[pl.ds(rows, rows), :], stage.at[pl.ds(0, rows), :])
        sz[...] = (t.keep[rows : 2 * rows, :].astype(f32) + stage[0:rows, :].astype(f32)).astype(bf16)

    def send_last(t):
        t.hops["s"] = links.send(sz, t.rs, "dp", SUB_BIT)

    def own_rows(t):
        links.local_wait(t.rx.at[pl.ds(0, rows), :], stage.at[pl.ds(0, rows), :])
        t.keep[0:rows, :] = (t.keep[0:rows, :].astype(f32) + stage[0:rows, :].astype(f32)).astype(bf16)
        received = stage.at[pl.ds(rows, rows), :]
        links.local_wait(t.rs, received)
        assemble(order, me, t.keep.at[pl.ds(0, rows), :], received, tmp)

    def norm_back():
        own_rows(sums["dn"])
        pg[...] = jnp.zeros_like(pg)
        strip = 64

        def body(i, carry):
            place = pl.ds(pl.multiple_of(i * strip, strip), strip)
            x = x_ref[place, :].astype(f32)
            x = x - jnp.mean(x, axis=-1, keepdims=True)
            inv = lax.rsqrt(jnp.mean(x * x, axis=-1, keepdims=True) + norm_eps)
            x = x * inv
            back = tmp[place, :]
            pg[0:1, :] += jnp.sum(back * x, axis=0, keepdims=True)
            pg[1:2, :] += jnp.sum(back, axis=0, keepdims=True)
            e = back * params_ref[0:1, :]
            tmp[place, :] = dy_own_ref[place, :].astype(f32) + inv * (
                e - jnp.mean(e, axis=-1, keepdims=True) - x * jnp.mean(e * x, axis=-1, keepdims=True)
            )
            return carry

        lax.fori_loop(0, rows // strip, body, 0)
        fetch("dx", tmp, dx_out)
        head_start = me_t * (2 * width) + sub * width
        hidden_start = me_t * (2 * hidden) + sub * hidden
        lanes = pl.ds(pl.multiple_of(head_start, width), width)
        for j in range(3):
            pg[2 + j : 3 + j, lanes] = sums_ref[0:1, j * width : (j + 1) * width]
        pg[5:6, :] = back_sum_ref[...]
        pg[6:7, :] = back_sum_ref[...]
        pg[pl.ds(7 + hidden_start // D, 1), pl.ds(pl.multiple_of(hidden_start % D, hidden), hidden)] = hsum[0:1, :]

    hops, base, size = [], 0, D
    for bit in reversed(range(dbits)):
        mine = (me >> bit) & 1
        if size >= 256:
            size //= 2
            there = (base + (1 - mine) * size, size)
            base = base + mine * size
        else:
            there = (base, size)
        hops.append(("dp", bit, there, (base, size)))
    for bit in range(tbits):
        hops.append(("tensor", bit, (base, size), (base, size)))
    lanes_of = lambda at: pl.ds(pl.multiple_of(at[0], at[1]), at[1])
    small_hops = {}

    def send_small(i):
        axis, bit, there, _ = hops[i]
        small_hops[i] = links.send(pg.at[:, lanes_of(there)], prb[i], axis, bit)

    def add_small(i):
        links.sent_done(small_hops[i])
        pg[:, lanes_of(hops[i][3])] += prb[i][...]

    def block_output():
        need("dx")
        own_rows(sums["br"])
        kx[0:rows, :] = (x_ref[...].astype(f32) + tmp[...] + params_ref[5:6, :] + params_ref[6:7, :]).astype(bf16)
        fetch("y", kx.at[pl.ds(0, rows), :], y_out)

    def end():
        pg_out[...] = pg[:, lanes_of((base, size))]
        need("y")
        for copy in slots[-own.shape[0] :]:
            copy.wait()
        links.finish()

    greet(dbits, tbits)
    plain = {
        "load0": lambda: need("o", "dy", "h"),
        "load1": load_more,
        "w1load": lambda: fetch("w1", w1_hbm, hw1),
        "hload": lambda: fetch("h", h_hbm, hw1),
        "nload": load_n,
        "dnout": norm_back,
        "brout": block_output,
        "end": end,
    }
    of_unit = {"away": away, "home": home, "f1": fold_first, "f2": fold_last}
    send_unit = {"y": send_y, "h": send_high, "z": send_sub}
    of_sum = {
        "31": lambda t: far_rows(t, 1), "30": lambda t: far_rows(t, 0), "01": near_rows, "00": keep_rows,
        "own": partner_rows,
    }
    send_sum = {
        "c1": lambda t: send_core(t, 1), "c0": lambda t: send_core(t, 0), "b": lambda t: send_x(t, 1),
        "a": lambda t: send_x(t, 0), "s": send_last,
    }
    wait_sum = {"c1": ("c", 1), "c0": ("c", 0), "b": ("x", 1), "a": ("x", 0), "s": "s"}
    for name in reduce_schedule(count, units, len(hops)):
        kind, _, rest = name.partition("_")
        if name in plain:
            plain[name]()
        elif kind in of_unit:
            of_unit[kind](units[rest])
        elif name[:2] == "dh":
            hidden_back(int(name[2:]))
        elif name[0] == "g":
            add_small(int(name[1:]))
        elif name[:2] == "SG":
            send_small(int(name[2:]))
        elif name[:2] == "WG":
            small_hops[int(name[2:])].wait_recv()
        elif name[0] == "S" and name[1:3] in sums:
            send_sum[name[3:]](sums[name[1:3]])
        elif name[0] == "W" and name[1:3] in sums:
            sums[name[1:3]].hops[wait_sum[name[3:]]].wait_recv()
        elif name[0] == "S":
            send_unit[name[1]](units[name[2:]])
        elif name[0] == "W":
            unit = units[name[2:]]
            unit.hop.wait_recv()
            if name[1] in "yh":
                load_received(unit, ry if name[1] == "y" else rz[0])
        else:
            of_sum[name[2:]](sums[name[:2]])


REDUCE_ORDER = [
    0, 11, 12, 8, 9, 5, 7, 14, 4, 1, 20, 18, 2, 49, 13, 50, 51, 15, 19, 6, 17, 10, 3, 46, 16, 47, 48, 21, 22,
    23, 64, 24, 52, 65, 66, 53, 54, 25, 26, 28, 29, 27, 61, 43, 39, 44, 70, 45, 85, 86, 31, 40, 67, 71, 38,
    62, 30, 63, 41, 42, 68, 69, 91, 92, 82, 87, 32, 33, 34, 167, 122, 88, 123, 83, 124, 58, 95, 93, 94, 59,
    60, 78, 79, 76, 80, 84, 96, 97, 98, 119, 89, 120, 107, 121, 72, 143, 75, 90, 55, 56, 81, 144, 145, 108,
    57, 109, 99, 36, 77, 100, 169, 125, 126, 127, 73, 35, 140, 74, 116, 101, 102, 103, 37, 171, 149, 113,
    110, 128, 117, 118, 150, 174, 165, 151, 146, 152, 129, 114, 111, 112, 137, 130, 115, 131, 147, 132, 133,
    153, 138, 148, 154, 139, 155, 164, 166, 156, 105, 157, 158, 159, 160, 141, 142, 134, 161, 104, 135, 136,
    106, 172, 162, 163, 175, 170, 173, 168, 176,
]


def reduce_schedule(count, units, hops):
    names = ["load0", "load1"]
    early = [u for u in units if u[0] in "oa"]
    late = [u for u in units if u[0] in "cq"]

    def start(group):
        for u in group:
            names.extend(["away_" + u, "Sy" + u, "home_" + u])

    def fold(group):
        for u in group:
            names.extend(["Wy" + u, "f1_" + u, "Sh" + u])
        for u in group:
            names.extend(["Wh" + u, "f2_" + u, "Sz" + u])

    def total(k):
        for part in ("31", "Sc1", "30", "Sc0", "Wc1", "Wc0", "01", "Sb", "Sa", "00", "Wb", "own", "Ss", "Ws", "Wa", "out"):
            names.append(part[0] + k + part[1:] if part[0] in "SW" else k + part)

    start(early)
    names.extend("dh%d" % c for c in range(4))
    names.append("w1load")
    total("dn")
    names.extend(["hload", "nload"])
    fold(early)
    start(late)
    total("br")
    fold(late)
    for i in range(hops):
        names.extend(["SG%d" % i, "WG%d" % i, "g%d" % i])
    names.extend("Wz" + u for u in units)
    names.append("end")
    if count == 8 and len(units) == 12 and hops == 5:
        return [names[i] for i in REDUCE_ORDER]
    return names


def reduce_call(dbits, tbits, x, dy, params, back_sum, sums, gathered):
    normed, back_rows, wq, w1, wo, w2, hidden_act, slope, attended, proj_back = gathered
    count = 1 << dbits
    blk = D // count
    rows = x.shape[0]
    tokens = normed.shape[0]
    width, hidden = wo.shape[0], w2.shape[0]
    total = 4 * width + 2 * hidden
    half, quarter = tokens // 2, tokens // 4
    any_spec = pl.BlockSpec(memory_space=pl.ANY)
    vm = pl.BlockSpec(memory_space=pltpu.VMEM)
    shape = lambda s, t=bf16: jax.ShapeDtypeStruct(s, t)
    vmem = lambda s, t=bf16: pltpu.VMEM(s, t)
    prb, size = [], D
    for _ in range(dbits):
        size = size // 2 if size >= 256 else size
        prb.append(vmem((16, size), f32))
    prb += [vmem((16, size), f32)] * tbits
    outs = [
        shape((rows, D)),
        shape((rows, D), f32),
        shape((total, blk), f32),
        shape((total, blk)),
        shape((16, size), f32),
        shape((total, D // 2)),
    ]
    outs += [shape((half, D)), shape((quarter, D)), shape((rows, D))] * 2
    outs += [shape((total, D >> (2 + k))) for k in range(dbits - 2)]
    scratch = [
        vmem((tokens, D)),
        vmem((tokens, hidden)),
        vmem((tokens, hidden)),
        vmem((hidden, D)),
        vmem((width, D)),
        vmem((D, 3 * width)),
        vmem((tokens, width)),
        vmem((tokens, 3 * width)),
        vmem((total - hidden, D // 2)),
        vmem((total, D // 2)),
        vmem((2, width, blk), f32),
        vmem((3, width, D // 2)),
        vmem((quarter, D)),
        vmem((quarter, D)),
        vmem((rows, D)),
        vmem((quarter, D)),
        vmem((quarter, D)),
        vmem((rows, D), f32),
        vmem((16, D), f32),
        vmem((8, hidden), f32),
        pltpu.SemaphoreType.DMA((80,)),
        pltpu.SemaphoreType.DMA((80,)),
        pltpu.SemaphoreType.DMA((160,)),
    ] + prb
    if blk % 128:
        scratch.append(vmem((total, blk)))
    return pl.pallas_call(
        functools.partial(reduce_kernel, (dbits, tbits)),
        out_shape=outs,
        in_specs=[vm] * 5 + [any_spec] * 10,
        out_specs=[any_spec] * 4 + [vm] + [any_spec] * (len(outs) - 5),
        scratch_shapes=scratch,
        compiler_params=pltpu.CompilerParams(
            vmem_limit_bytes=62 * 2**20, collective_id=1, has_side_effects=True
        ),
        cost_estimate=pl.CostEstimate(flops=5 * 10**10, bytes_accessed=10**8, transcendentals=10**6),
        name="reduce",
    )(x, dy, params, back_sum, sums, *gathered)


def adam_kernel(plans, me_ref, *refs):
    sub = (me_ref[0] >> SUB_BIT) & 1
    step = pl.program_id(0)
    count = len(plans)
    ins, outs = refs[: 5 * count], refs[5 * count :]
    for k, (begin, half, turned) in enumerate(plans):
        w_ref, m_ref, v_ref, own_ref, recv_ref = ins[5 * k : 5 * k + 5]
        wo_ref, mo_ref, vo_ref = outs[3 * k : 3 * k + 3]

        @pl.when((step >= begin) & (step < begin + 2 * half))
        def _():
            mine = ((step - begin) // half) == sub
            grad = jnp.where(mine, own_ref[...], recv_ref[...].astype(f32))
            grad = (grad.T if turned else grad).reshape(w_ref.shape)
            wo_ref[...], mo_ref[...], vo_ref[...] = adam_update(
                w_ref[...], m_ref[...], v_ref[...], grad, matrix_rate, weight_decay
            )


def adam_call(me, matrices, own, recv):
    blk = own.shape[1]
    plans, operands, in_specs, out_specs, out_shape = [], [], [], [], []
    begin = 0
    for weight, first, second, start, rows, turned in matrices:
        shape = weight.shape
        half = shape[0] if len(shape) == 3 else shape[1 if turned else 0] // (2 * rows)

        def at(i, begin=begin, half=half):
            return jnp.clip(i - begin, 0, 2 * half - 1)

        if len(shape) == 3:
            full = pl.BlockSpec((1, blk, rows), lambda i, at=at, half=half: (at(i) % half, 0, at(i) // half))
        elif turned:
            full = pl.BlockSpec((blk, rows), lambda i, at=at: (0, at(i)))
        else:
            full = pl.BlockSpec((rows, blk), lambda i, at=at: (at(i), 0))
        base = start // rows
        part = pl.BlockSpec((rows, blk), lambda i, at=at, half=half, base=base: (base + at(i) % half, 0))
        plans.append((begin, half, turned))
        operands += [weight, first, second, own, recv]
        in_specs += [full] * 3 + [part] * 2
        out_specs += [full] * 3
        out_shape += [jax.ShapeDtypeStruct(shape, f32)] * 3
        begin += 2 * half
    return tuple(
        pl.pallas_call(
            functools.partial(adam_kernel, plans),
            grid=(begin,),
            out_shape=out_shape,
            in_specs=[smem_spec()] + in_specs,
            out_specs=out_specs,
            compiler_params=vmem_params(60),
            name="adam",
        )(me, *operands)
    )


def per_device(
    inputs,
    segments,
    cotangent,
    qkv_weight,
    qkv_first,
    qkv_second,
    dense_weight,
    dense_first,
    dense_second,
    expand_weight,
    expand_first,
    expand_second,
    shrink_weight,
    shrink_first,
    shrink_second,
    small_params,
    small_first,
    small_second,
):
    dp = lax.axis_size("dp")
    tensor_count = lax.axis_size("tensor")
    dbits = dp.bit_length() - 1
    tbits = tensor_count.bit_length() - 1
    d_me = lax.axis_index("dp")
    t_me = lax.axis_index("tensor")
    sub = (d_me >> SUB_BIT) & 1
    order = place_order(dp)
    high_bits = list(range(2, dbits))
    gather_bits = high_bits + [ROW_BIT]
    rows = inputs.shape[0]
    me = jnp.stack([d_me, t_me]).astype(jnp.int32)

    small_low = jnp.pad(small_params.astype(bf16), ((0, 16 - small_params.shape[0]), (0, 0)))
    ids = jnp.broadcast_to(segments, (8, rows))
    (
        normed, back_rows, qkv_wide, expand_full, dense_full, shrink_full, hidden_act, gelu_slope, attended, proj_back,
        params, back_sum, sums,
    ) = gather_call(
        dbits, tbits, inputs, cotangent, ids, small_low, qkv_weight, expand_weight, dense_weight, shrink_weight
    )
    width, hidden = dense_full.shape[0], shrink_full.shape[0]
    gathered = (
        normed, back_rows, qkv_wide, expand_full, dense_full, shrink_full, hidden_act, gelu_slope, attended, proj_back,
    )
    output, input_grad, own, recv, small_sum, *_ = reduce_call(
        dbits, tbits, inputs, cotangent, params, back_sum, sums, gathered
    )
    blk = D // dp
    if small_sum.shape[1] > blk:
        small_sum = lax.dynamic_slice_in_dim(small_sum, (d_me % (small_sum.shape[1] // blk)) * blk, blk, 1)
    small_sum = small_sum[: small_params.shape[0]]
    block = min(512, hidden)
    new = adam_call(
        me,
        [
            (shrink_weight, shrink_first, shrink_second, 0, block, False),
            (expand_weight, expand_first, expand_second, hidden, block, True),
            (qkv_weight, qkv_first, qkv_second, 2 * hidden, width, True),
            (dense_weight, dense_first, dense_second, 2 * hidden + 3 * width, width, False),
        ],
        own,
        recv,
    )
    shrink_new, expand_new, qkv_new, dense_new = new[0:3], new[3:6], new[6:9], new[9:12]
    small_new = adam_update(small_params, small_first, small_second, small_sum, vector_rate, 0.0)
    return (output, input_grad) + qkv_new + dense_new + expand_new + shrink_new + small_new


def solution(mesh):
    token_spec = P(("dp", "tensor"), None)
    qkv_spec = P(None, "dp", "tensor")
    row_spec = P("tensor", "dp")
    column_spec = P("dp", "tensor")
    small_spec = P(None, "dp")
    weight_specs = (qkv_spec,) * 3 + (row_spec,) * 3 + (column_spec,) * 3 + (row_spec,) * 3 + (small_spec,) * 3
    return jax.shard_map(
        per_device,
        mesh=mesh,
        in_specs=(token_spec, P("dp", "tensor"), token_spec) + weight_specs,
        out_specs=(token_spec, token_spec) + weight_specs,
        check_vma=False,
    )
```

time: 525 us -> 441 us (0.84)
  Pallas kernels: 500 us -> 426 us
  local copies, waits for them, and re-layouts: 13.9 us -> 4.2 us
    pallas_call x1, Pallas kernels: 247 us -> 206 us  [gather_call(): pl.pallas_call(functools.partial(gather_kernel, (dbits, tbits)), out_shap...]
    pallas_call x1, Pallas kernels: 236 us -> 196 us  [reduce_call(): pl.pallas_call(functools.partial(reduce_kernel, (dbits, tbits)), out_shap...]
    unnamed x46 -> x14, local copies, waits for them, and re-layouts: 11.4 us -> 2.31 us
    pallas_call x4 -> x1, Pallas kernels: 17.6 us -> 23.4 us  [adam_call(): pl.pallas_call(functools.partial(adam_kernel, plans), grid=(begin,), out_...]
where the time goes in v4:
time: 441 us; the launch traced here: 433 us
  Pallas kernels  426 us (97%)
    pallas_call x1, Pallas kernels, gather_call(): pl.pallas_call(functools.partial(gather_kernel, (dbits, tbits)), out_shap...  206 us
    pallas_call x1, Pallas kernels, reduce_call(): pl.pallas_call(functools.partial(reduce_kernel, (dbits, tbits)), out_shap...  196 us
    pallas_call x1, Pallas kernels, adam_call(): pl.pallas_call(functools.partial(adam_kernel, plans), grid=(begin,), out_...  23.4 us

profile of v4, /device:TPU:0, one launch (start us, length us, event | category | flops | bytes accessed | tf_op | source)
XLA Modules:
  0.0 432.9 jit_solution(1175581355782934625)
XLA Ops:
  0.7 0.7 convert_element_type.5
  1.4 0.6 pad.4.small_ref
  2.0 1.3 broadcast_in_dim.8.ids_ref
  3.3 206.0 %gather.1 = (bf16[2048,2048]{1,0:T(8,128)(2,1)}, bf16[2048,2048]{1,0:T(8,128)(2,1)}, bf16[2048,768]{1,0:T(8,128)(2,1)}, bf16[2048,1024]{1,0:T(8,128)(2,1)}, bf16...) custom-call(bf16[256,2048]{1,0:T(8,128)(2,1)} %x_ref.3, ...), custom_call_target="tpu_custom_call" | custom-call | flops 20000000000 | bytes 100000000 | tf_op jit(solution)/shard_map/gather/pallas_call | solution.py:702
  209.3 196.2 %reduce.1 = (bf16[256,2048]{1,0:T(8,128)(2,1)}, f32[256,2048]{1,0:T(8,128)}, f32[3072,256]{1,0:T(8,128)}, bf16[3072,256]{1,0:T(8,128)(2,1)}, f32[16,256]{1,0:T(8...) custom-call(bf16[256,2048]{1,0:T(8,128)(2,1)} %x_ref.3, ...), custom_call_target="tpu_custom_call" | custom-call | flops 49999998976 | bytes 100000000 | tf_op jit(solution)/shard_map/reduce/pallas_call | solution.py:1180
  405.5 0.6 pad_add_fusion.me_ref
  406.1 0.0 copy-start.2
  406.1 0.0 copy-start.3
  406.1 0.0 copy-start.4
  406.1 0.0 copy-start.5
  406.1 0.0 copy-start.1
  406.1 23.4 %adam.1 = (f32[2048,256]{1,0:T(8,128)}, f32[2048,256]{1,0:T(8,128)}, f32[2048,256]{1,0:T(8,128)}, f32[256,2048]{1,0:T(8,128)}, f32[256,2048]{1,0:T(8,128)}, /*in...) custom-call(s32[2]{0:T(128)} %pad_add_fusion.me_ref, ...), custom_call_target="tpu_custom_call" | custom-call | tf_op jit(solution)/shard_map/adam/pallas_call | solution.py:1239
  429.5 0.0 copy-start
  429.5 0.0 copy-done.2
  429.5 0.0 copy-done.3
  429.5 0.0 copy-done.4
  429.5 0.0 copy-done.5
  429.6 0.6 add_subtract_fusion
  430.2 0.0 copy-done.1
  430.2 1.0 copy.38
  431.2 0.0 copy-done
  431.2 1.3 copy.39
Async XLA Ops:
  406.1 23.4 %copy-start.2 = (f32[11,256]{1,0:T(8,128)S(1)}, f32[11,256]{1,0:T(8,128)}, u32[]{:S(2)}) copy-start(f32[11,256]{1,0:T(8,128)} %param.34) | copy-start | bytes 33796
  406.1 23.4 %copy-start.3 = (f32[11,256]{1,0:T(8,128)S(1)}, f32[11,256]{1,0:T(8,128)}, u32[]{:S(2)}) copy-start(f32[11,256]{1,0:T(8,128)} %param.35) | copy-start | bytes 33796
  406.1 23.4 %copy-start.4 = (f32[11,256]{1,0:T(8,128)S(1)}, f32[11,256]{1,0:T(8,128)}, u32[]{:S(2)}) copy-start(f32[11,256]{1,0:T(8,128)} %param.36) | copy-start | bytes 33796
  406.1 23.4 %copy-start.5 = (f32[16,256]{1,0:T(8,128)S(1)}, f32[16,256]{1,0:T(8,128)}, u32[]{:S(2)}) copy-start(f32[16,256]{1,0:T(8,128)} %get-tuple-element.76) | copy-start | bytes 49156
  406.1 24.1 %copy-start.1 = (bf16[256,2048]{1,0:T(8,128)(2,1)S(1)}, bf16[256,2048]{1,0:T(8,128)(2,1)}, u32[]{:S(2)}) copy-start(bf16[256,2048]{1,0:T(8,128)(2,1)} %get-tuple-element.97) | copy-start | bytes 3145732
  429.5 1.7 copy-start
